TPU v7x, 32 devices: a whole 2x2x4 slice. The times are simulated.
32 devices in a mesh: tok: 16 (over z, y, x), mem: 2 (over core).
Axes of the slice: x: 2, y: 2, z: 4, core: 2. Of those that a mesh axis runs over, the one named last changes fastest.
Arguments:
- inputs: bfloat16 [16384, 1472], P('tok'), may hold values from -6 to 6
- memory: bfloat16 [16, 1024, 1472], P('tok', 'mem'), may hold values from -6 to 6
- kept_mask: int32 [16, 1024], P('tok', 'mem'), may hold values from 0 to 1, as said below
- segment_ids: int32 [16384], P('tok'), may hold values from 0 to 63, never falling along the last dimension, each value on 1 to 512 neighbouring positions
- bucket_ids: int32 [1024], replicated, may hold values from 0 to 31
- out_grad: bfloat16 [16384, 1472], P('tok'), may hold values from -6 to 6
- self_weights: float32 [4, 384, 1472], P(None, 'mem', 'tok')
- self_first: float32 [4, 384, 1472], P(None, 'mem', 'tok'), may hold values from -0.00015258789 to 0.00015258789
- self_second: float32 [4, 384, 1472], P(None, 'mem', 'tok'), may hold values from 2.5843174e-09 to 1.0317618e-08
- cross_weights: float32 [4, 384, 1472], P(None, ('tok', 'mem'))
- cross_first: float32 [4, 384, 1472], P(None, ('tok', 'mem')), may hold values from -0.00015258789 to 0.00015258789
- cross_second: float32 [4, 384, 1472], P(None, ('tok', 'mem')), may hold values from 2.5843174e-09 to 1.0317618e-08
- ffn_weights: float32 [3, 3584, 1472], P(None, 'mem', 'tok')
- ffn_first: float32 [3, 3584, 1472], P(None, 'mem', 'tok'), may hold values from -3.8146973e-05 to 3.8146973e-05
- ffn_second: float32 [3, 3584, 1472], P(None, 'mem', 'tok'), may hold values from 6.3870964e-11 to 2.60397e-10
- norm_gains: float32 [3, 1472], P(None, 'tok'), may hold values from 0.5 to 1.5
- gains_first: float32 [3, 1472], P(None, 'tok'), may hold values from -0.00015258789 to 0.00015258789
- gains_second: float32 [3, 1472], P(None, 'tok'), may hold values from 1.4739454e-09 to 5.8957816e-09
- rel_bias: float32 [6, 32], P('mem'), may hold values from -3 to 3
- rel_first: float32 [6, 32], P('mem'), may hold values from -0.00015258789 to 0.00015258789
- rel_second: float32 [6, 32], P('mem'), may hold values from 1.4739454e-09 to 5.8957816e-09
Outputs:
- layer_out: bfloat16 [16384, 1472], P('tok')
- input_grad: float32 [16384, 1472], P('tok')
- memory_grad: float32 [16, 1024, 1472], P('tok', 'mem')
- grad_norm: float32 [], replicated
- self_new: float32 [4, 384, 1472], P(None, 'mem', 'tok')
- self_first_new: float32 [4, 384, 1472], P(None, 'mem', 'tok')
- self_second_new: float32 [4, 384, 1472], P(None, 'mem', 'tok')
- cross_new: float32 [4, 384, 1472], P(None, ('tok', 'mem'))
- cross_first_new: float32 [4, 384, 1472], P(None, ('tok', 'mem'))
- cross_second_new: float32 [4, 384, 1472], P(None, ('tok', 'mem'))
- ffn_new: float32 [3, 3584, 1472], P(None, 'mem', 'tok')
- ffn_first_new: float32 [3, 3584, 1472], P(None, 'mem', 'tok')
- ffn_second_new: float32 [3, 3584, 1472], P(None, 'mem', 'tok')
- gains_new: float32 [3, 1472], P(None, 'tok')
- gains_first_new: float32 [3, 1472], P(None, 'tok')
- gains_second_new: float32 [3, 1472], P(None, 'tok')
- rel_new: float32 [6, 32], P('mem')
- rel_first_new: float32 [6, 32], P('mem')
- rel_second_new: float32 [6, 32], P('mem')
Inputs may be any that keep to these rules, and one draw needn't show every extreme that they name: `kept_mask`: 1 where the deletion gate kept the row's encoder position; position 0 of every row is kept. `segment_ids`: segment numbers never fall along the tokens; a segment holds half of 1024 tokens or fewer. `bucket_ids`: entry d is the bucket of a key d positions before its query.
All inputs are finite; a program needn't handle non-finite values.
Results may differ from a plain program's by a relative error of at most 0.03.
The roundings to bfloat16 on the way count: a program that leaves them out, or rounds other values in their place, can miss the bound.
Values may be sent and summed in bfloat16 or wider, within the bound.
No kernel may reach another device: no remote copies, remote signals or barrier semaphores. Data moves between devices by JAX's collectives and lax.ppermute only.
A program may use at most 384 MiB of HBM per device.

v0:
```python
import jax
import jax.numpy as jnp
from jax import lax
from jax.sharding import PartitionSpec as P

H = 6
DK = 64
NB = 32
LEN = 1024
STEP = 10
INNER = 384


EPS_NORM = 1e-06
NEG_FILL = -1e30
BETA_FIRST = 0.9
BETA_SECOND = 0.95
ADAM_EPS = 1e-08
RATE_MATRIX = 0.05
RATE_SMALL = 1.0
DECAY_MATRIX = 0.1
CLIP_NORM = 1.0


def combined_all(part, axis, combine):
    gathered = jax.tree.map(lambda a: lax.all_gather(a, axis), part)

    def take(source):
        return jax.tree.map(lambda a: lax.dynamic_index_in_dim(a, source, 0, False), gathered)

    return lax.fori_loop(
        1, lax.axis_size(axis), lambda source, state: combine(state, take(source)), take(0)
    )


def rms_parts(values, gain_vec):
    inv_root = lax.rsqrt(jnp.mean(values * values, axis=-1, keepdims=True) + EPS_NORM)
    return values * inv_root * gain_vec


def norm_back(values, gain_vec, upstream):
    unused, pull_back = jax.vjp(rms_parts, values, gain_vec)
    return pull_back(upstream)


def gated_unit(gate_val, upward):
    return jax.nn.gelu(gate_val, approximate=True) * upward


def toeplitz_grid(bias_vec, length):
    head_count = bias_vec.shape[0]
    extended = jnp.concatenate(
        [bias_vec[:, ::-1], jnp.broadcast_to(bias_vec[:, :1], (head_count, length))], axis=1
    )
    tiled = jnp.tile(extended, (1, length + 1))
    window = tiled[:, length - 1 : length - 1 + length * (2 * length - 1)]
    return window.reshape(head_count, length, 2 * length - 1)[:, :, :length]


def diagonal_sums(grid_vals):
    head_count, length, unused = grid_vals.shape
    padded = jnp.concatenate(
        [jnp.zeros((head_count, length, length), jnp.float32), grid_vals], axis=2
    )
    flat_vals = padded.reshape(head_count, 2 * length * length)
    flat_vals = jnp.concatenate([flat_vals, jnp.zeros((head_count, length), jnp.float32)], axis=1)
    skewed = flat_vals.reshape(head_count, length, 2 * length + 1)
    totals = jnp.sum(skewed, axis=1)
    return totals[:, length:0:-1]


def join_stats(first_pair, second_pair):
    score_top = jnp.maximum(first_pair[0], second_pair[0])
    joined = first_pair[1] * jnp.exp(first_pair[0] - score_top) + second_pair[1] * jnp.exp(
        second_pair[0] - score_top
    )
    return (score_top, joined)


def reduce_rows(pieces):
    return (
        lax.psum_scatter(pieces[0], "tok", scatter_dimension=2, tiled=True),
        lax.psum_scatter(pieces[1], "tok", scatter_dimension=2, tiled=True),
        lax.psum_scatter(pieces[2], "tok", scatter_dimension=2, tiled=True),
    )


def adam_step(weight, first_mom, second_mom, gradient, clip_scale, step_rate, decay_rate):
    clipped = gradient * clip_scale
    first_new = BETA_FIRST * first_mom + (1.0 - BETA_FIRST) * clipped
    second_new = BETA_SECOND * second_mom + (1.0 - BETA_SECOND) * clipped * clipped
    first_hat = first_new / (1.0 - BETA_FIRST**STEP)
    second_hat = second_new / (1.0 - BETA_SECOND**STEP)
    weight_new = weight - step_rate * (
        first_hat / (jnp.sqrt(second_hat) + ADAM_EPS) + decay_rate * weight
    )
    return (weight_new, first_new, second_new)


def shards(
    inputs,
    memory,
    kept_mask,
    segment_ids,
    bucket_ids,
    out_grad,
    self_weights,
    self_first,
    self_second,
    cross_weights,
    cross_first,
    cross_second,
    ffn_weights,
    ffn_first,
    ffn_second,
    norm_gains,
    gains_first,
    gains_second,
    rel_bias,
    rel_first,
    rel_second,
):
    self_full, ffn_full, gain_full = (
        lax.all_gather(self_weights.astype(jnp.bfloat16), "tok", axis=2, tiled=True),
        lax.all_gather(ffn_weights.astype(jnp.bfloat16), "tok", axis=2, tiled=True),
        lax.all_gather(norm_gains.astype(jnp.bfloat16), "tok", axis=1, tiled=True),
    )
    cross_full = lax.all_gather(
        cross_weights.astype(jnp.bfloat16), ("tok", "mem"), axis=1, tiled=True
    )
    gain_vals = gain_full.astype(jnp.float32)
    head_local = rel_bias.shape[0]
    row_count = memory.shape[0]
    enc_local = memory.shape[1]
    tokens_dev = inputs.shape[0]
    mem_index = lax.axis_index("mem")
    share_tok = tokens_dev // lax.axis_size("mem")
    first_tok = mem_index * share_tok
    resid_zero = inputs.astype(jnp.float32)
    normed_one = rms_parts(resid_zero, gain_vals[0]).astype(jnp.bfloat16)
    qkv_self = jnp.einsum(
        "td,cid->cti", normed_one, self_full[:3], preferred_element_type=jnp.float32
    ).astype(jnp.bfloat16)
    query_h = qkv_self[0].reshape(row_count, LEN, head_local, DK)
    key_h = qkv_self[1].reshape(row_count, LEN, head_local, DK)
    value_h = qkv_self[2].reshape(row_count, LEN, head_local, DK)
    positions = jnp.arange(LEN, dtype=jnp.int32)
    causal = positions[:, None] >= positions[None, :]
    bucket_hot = (bucket_ids[None, :] == jnp.arange(NB, dtype=jnp.int32)[:, None]).astype(
        jnp.float32
    )
    bias_vec = jnp.dot(rel_bias, bucket_hot, precision=lax.Precision.HIGHEST)
    bias_grid = toeplitz_grid(bias_vec, LEN)
    seg_rows = segment_ids.reshape(row_count, LEN)
    allowed = causal[None] & (seg_rows[:, :, None] == seg_rows[:, None, :])

    def self_scores():
        raw_scores = (
            jnp.einsum("rqhd,rkhd->rhqk", query_h, key_h, preferred_element_type=jnp.float32)
            + bias_grid[None]
        )
        return jnp.where(allowed[:, None], raw_scores, NEG_FILL)

    scores_self = self_scores()
    score_top = jnp.max(scores_self, axis=-1, keepdims=True)
    exp_self = jnp.exp(scores_self - score_top)
    total_self = jnp.sum(exp_self, axis=-1, keepdims=True)
    self_lse = score_top + jnp.log(total_self)
    probs_low = (exp_self / total_self).astype(jnp.bfloat16)
    self_attn = (
        jnp.einsum("rhqk,rkhd->rqhd", probs_low, value_h, preferred_element_type=jnp.float32)
        .reshape(tokens_dev, head_local * DK)
        .astype(jnp.bfloat16)
    )
    self_part = jnp.dot(self_attn, self_full[3], preferred_element_type=jnp.float32)
    self_sum = lax.psum(self_part, "mem")
    resid_one = resid_zero + self_sum
    normed_two = rms_parts(resid_one, gain_vals[1]).astype(jnp.bfloat16)
    query_flat = jnp.einsum(
        "td,id->ti", normed_two, cross_full[0], preferred_element_type=jnp.float32
    ).astype(jnp.bfloat16)
    query_c = query_flat.reshape(row_count, LEN, H, DK)
    kv_cross = jnp.einsum(
        "rkd,cid->crki", memory, cross_full[1:3], preferred_element_type=jnp.float32
    ).astype(jnp.bfloat16)
    key_c = kv_cross[0].reshape(row_count, enc_local, H, DK)
    value_c = kv_cross[1].reshape(row_count, enc_local, H, DK)
    kept_cols = (kept_mask > 0)[:, None, None, :]

    def cross_scores():
        raw_scores = jnp.einsum(
            "rqhd,rkhd->rhqk", query_c, key_c, preferred_element_type=jnp.float32
        )
        return jnp.where(kept_cols, raw_scores, NEG_FILL)

    scores_cross = cross_scores()
    local_top = jnp.max(scores_cross, axis=-1)
    local_total = jnp.sum(
        jnp.where(kept_cols, jnp.exp(scores_cross - local_top[..., None]), 0.0), axis=-1
    )
    cross_top, cross_total = combined_all((local_top, local_total), "mem", join_stats)
    cross_probs = (
        jnp.where(kept_cols, jnp.exp(scores_cross - cross_top[..., None]), 0.0)
        / cross_total[..., None]
    )
    cross_part = jnp.einsum(
        "rhqk,rkhd->rqhd",
        cross_probs.astype(jnp.bfloat16),
        value_c,
        preferred_element_type=jnp.float32,
    ).reshape(tokens_dev, INNER)
    cross_attn = lax.psum(cross_part, "mem")
    cross_attn_low = cross_attn.astype(jnp.bfloat16)
    cross_lse = cross_top + jnp.log(cross_total)
    resid_two = resid_one + jnp.dot(
        cross_attn_low, cross_full[3], preferred_element_type=jnp.float32
    )
    normed_three = rms_parts(resid_two, gain_vals[2]).astype(jnp.bfloat16)
    gate_up = jnp.einsum(
        "td,cfd->ctf", normed_three, ffn_full[:2], preferred_element_type=jnp.float32
    )
    hidden = gated_unit(gate_up[0], gate_up[1]).astype(jnp.bfloat16)
    ffn_part = jnp.dot(hidden, ffn_full[2], preferred_element_type=jnp.float32)
    ffn_sum = lax.psum(ffn_part, "mem")
    layer_out = (resid_two + ffn_sum).astype(jnp.bfloat16)
    grad_out = out_grad.astype(jnp.float32)
    grad_hidden = jnp.einsum("td,fd->tf", out_grad, ffn_full[2], preferred_element_type=jnp.float32)
    unused, unit_pull = jax.vjp(gated_unit, gate_up[0], gate_up[1])
    grad_gate, grad_upward = unit_pull(grad_hidden)
    grad_gu = jnp.stack([grad_gate, grad_upward]).astype(jnp.bfloat16)
    ffn_grad = jnp.concatenate(
        [
            jnp.einsum("ctf,td->cfd", grad_gu, normed_three, preferred_element_type=jnp.float32),
            jnp.einsum("tf,td->fd", hidden, out_grad, preferred_element_type=jnp.float32)[None],
        ],
        axis=0,
    )
    back_three = jnp.einsum(
        "ctf,cfd->td", grad_gu, ffn_full[:2], preferred_element_type=jnp.float32
    )
    back_three = lax.psum(back_three, "mem")
    grad_resid_three, gain_three = norm_back(resid_two, gain_vals[2], back_three)
    grad_two = grad_out + grad_resid_three
    grad_two_low = grad_two.astype(jnp.bfloat16)
    grad_cattn = jnp.einsum(
        "td,id->ti", grad_two_low, cross_full[3], preferred_element_type=jnp.float32
    ).astype(jnp.bfloat16)
    own_attn = lax.dynamic_slice_in_dim(cross_attn_low, first_tok, share_tok, 0)
    own_grad = lax.dynamic_slice_in_dim(grad_two_low, first_tok, share_tok, 0)
    grad_cross_out = jnp.einsum("ti,td->id", own_attn, own_grad, preferred_element_type=jnp.float32)
    grad_heads = grad_cattn.reshape(row_count, LEN, H, DK)
    delta_cross = jnp.swapaxes(
        jnp.sum(
            (grad_cattn.astype(jnp.float32) * cross_attn).reshape(row_count, LEN, H, DK), axis=-1
        ),
        1,
        2,
    )
    probs_again = jnp.where(kept_cols, jnp.exp(cross_scores() - cross_lse[..., None]), 0.0)
    grad_pcross = jnp.einsum(
        "rqhd,rkhd->rhqk", grad_heads, value_c, preferred_element_type=jnp.float32
    )
    grad_cscores = (probs_again * (grad_pcross - delta_cross[..., None])).astype(jnp.bfloat16)
    grad_query_c = jnp.einsum(
        "rhqk,rkhd->rqhd", grad_cscores, key_c, preferred_element_type=jnp.float32
    ).reshape(tokens_dev, INNER)
    grad_query_c = lax.psum(grad_query_c, "mem").astype(jnp.bfloat16)
    grad_key_c = jnp.einsum(
        "rhqk,rqhd->rkhd", grad_cscores, query_c, preferred_element_type=jnp.float32
    )
    grad_value_c = jnp.einsum(
        "rhqk,rqhd->rkhd",
        probs_again.astype(jnp.bfloat16),
        grad_heads,
        preferred_element_type=jnp.float32,
    )
    grad_kv = (
        jnp.stack([grad_key_c, grad_value_c])
        .reshape(2, row_count, enc_local, INNER)
        .astype(jnp.bfloat16)
    )
    memory_grad = jnp.einsum(
        "crki,cid->rkd", grad_kv, cross_full[1:3], preferred_element_type=jnp.float32
    )
    grad_kv_w = jnp.einsum("crki,rkd->cid", grad_kv, memory, preferred_element_type=jnp.float32)
    own_normed = lax.dynamic_slice_in_dim(normed_two, first_tok, share_tok, 0)
    own_query = lax.dynamic_slice_in_dim(grad_query_c, first_tok, share_tok, 0)
    grad_query_w = jnp.einsum(
        "ti,td->id", own_query, own_normed, preferred_element_type=jnp.float32
    )
    cross_grad = jnp.concatenate([grad_query_w[None], grad_kv_w, grad_cross_out[None]], axis=0)
    back_two = jnp.dot(grad_query_c, cross_full[0], preferred_element_type=jnp.float32)
    grad_resid_two, gain_two = norm_back(resid_one, gain_vals[1], back_two)
    grad_one = grad_two + grad_resid_two
    grad_one_low = grad_one.astype(jnp.bfloat16)
    grad_sattn = jnp.einsum(
        "td,id->ti", grad_one_low, self_full[3], preferred_element_type=jnp.float32
    ).astype(jnp.bfloat16)
    grad_self_out = jnp.einsum(
        "ti,td->id", self_attn, grad_one_low, preferred_element_type=jnp.float32
    )
    grad_sheads = grad_sattn.reshape(row_count, LEN, head_local, DK)
    probs_self = jnp.exp(self_scores() - self_lse)
    grad_pself = jnp.einsum(
        "rqhd,rkhd->rhqk", grad_sheads, value_h, preferred_element_type=jnp.float32
    )
    delta_self = jnp.sum(probs_self * grad_pself, axis=-1, keepdims=True)
    grad_sscores = (probs_self * (grad_pself - delta_self)).astype(jnp.bfloat16)
    grad_query = jnp.einsum(
        "rhqk,rkhd->rqhd", grad_sscores, key_h, preferred_element_type=jnp.float32
    )
    grad_key = jnp.einsum(
        "rhqk,rqhd->rkhd", grad_sscores, query_h, preferred_element_type=jnp.float32
    )
    grad_value = jnp.einsum(
        "rhqk,rqhd->rkhd",
        probs_self.astype(jnp.bfloat16),
        grad_sheads,
        preferred_element_type=jnp.float32,
    )
    grad_qkv = (
        jnp.stack([grad_query, grad_key, grad_value])
        .reshape(3, tokens_dev, head_local * DK)
        .astype(jnp.bfloat16)
    )
    score_sums = jnp.sum(grad_sscores.astype(jnp.float32), axis=0)
    rel_grad = jnp.dot(diagonal_sums(score_sums), bucket_hot.T, precision=lax.Precision.HIGHEST)
    self_grad = jnp.concatenate(
        [
            jnp.einsum("cti,td->cid", grad_qkv, normed_one, preferred_element_type=jnp.float32),
            grad_self_out[None],
        ],
        axis=0,
    )
    back_one = jnp.einsum(
        "cti,cid->td", grad_qkv, self_full[:3], preferred_element_type=jnp.float32
    )
    back_one = lax.psum(back_one, "mem")
    grad_resid_one, gain_one = norm_back(resid_zero, gain_vals[0], back_one)
    input_grad = grad_one + grad_resid_one
    gains_grad = jnp.stack([gain_one, gain_two, gain_three])[:, None, :]
    self_reduced, ffn_reduced, gains_reduced = reduce_rows((self_grad, ffn_grad, gains_grad))
    cross_reduced = lax.psum_scatter(cross_grad, ("tok", "mem"), scatter_dimension=1, tiled=True)
    gains_reduced = gains_reduced[:, 0, :]
    gain_squares = jnp.where(mem_index == 0, jnp.sum(gains_reduced * gains_reduced), 0.0)
    local_squares = (
        jnp.sum(self_reduced * self_reduced)
        + jnp.sum(ffn_reduced * ffn_reduced)
        + jnp.sum(cross_reduced * cross_reduced)
        + gain_squares
    )
    rel_padded = lax.dynamic_update_slice_in_dim(
        jnp.zeros((H, NB), jnp.float32), rel_grad, mem_index * head_local, 0
    )
    total_squares, rel_total = lax.psum((local_squares, rel_padded), ("tok", "mem"))
    grad_norm = jnp.sqrt(total_squares + jnp.sum(rel_total * rel_total))
    rel_reduced = lax.dynamic_slice_in_dim(rel_total, mem_index * head_local, head_local, 0)
    clip_scale = CLIP_NORM / jnp.maximum(grad_norm, CLIP_NORM)
    self_new = adam_step(
        self_weights, self_first, self_second, self_reduced, clip_scale, RATE_MATRIX, DECAY_MATRIX
    )
    cross_new = adam_step(
        cross_weights,
        cross_first,
        cross_second,
        cross_reduced,
        clip_scale,
        RATE_MATRIX,
        DECAY_MATRIX,
    )
    ffn_new = adam_step(
        ffn_weights, ffn_first, ffn_second, ffn_reduced, clip_scale, RATE_MATRIX, DECAY_MATRIX
    )
    gains_new = adam_step(
        norm_gains, gains_first, gains_second, gains_reduced, clip_scale, RATE_SMALL, 0.0
    )
    rel_new = adam_step(rel_bias, rel_first, rel_second, rel_reduced, clip_scale, RATE_SMALL, 0.0)
    return (
        layer_out,
        input_grad,
        memory_grad,
        grad_norm,
        self_new[0],
        self_new[1],
        self_new[2],
        cross_new[0],
        cross_new[1],
        cross_new[2],
        ffn_new[0],
        ffn_new[1],
        ffn_new[2],
        gains_new[0],
        gains_new[1],
        gains_new[2],
        rel_new[0],
        rel_new[1],
        rel_new[2],
    )


def solution(mesh):
    placed = (
        P("tok", None),
        P("tok", "mem", None),
        P("tok", "mem"),
        P("tok"),
        P(),
        P("tok", None),
        P(None, "mem", "tok"),
        P(None, "mem", "tok"),
        P(None, "mem", "tok"),
        P(None, ("tok", "mem"), None),
        P(None, ("tok", "mem"), None),
        P(None, ("tok", "mem"), None),
        P(None, "mem", "tok"),
        P(None, "mem", "tok"),
        P(None, "mem", "tok"),
        P(None, "tok"),
        P(None, "tok"),
        P(None, "tok"),
        P("mem", None),
        P("mem", None),
        P("mem", None),
    )
    return jax.shard_map(
        shards,
        mesh=mesh,
        in_specs=placed,
        out_specs=(
            P("tok", None),
            P("tok", None),
            P("tok", "mem", None),
            P(),
            P(None, "mem", "tok"),
            P(None, "mem", "tok"),
            P(None, "mem", "tok"),
            P(None, ("tok", "mem"), None),
            P(None, ("tok", "mem"), None),
            P(None, ("tok", "mem"), None),
            P(None, "mem", "tok"),
            P(None, "mem", "tok"),
            P(None, "mem", "tok"),
            P(None, "tok"),
            P(None, "tok"),
            P(None, "tok"),
            P("mem", None),
            P("mem", None),
            P("mem", None),
        ),
        check_vma=False,
    )
```

profile of v0, /device:TPU:0, one launch (start us, length us, event | category | flops | bytes accessed | tf_op | source)
XLA Modules:
  0.0 2519.0 jit_solution(14019241076331628613)
XLA Ops:
  12.7 11.8 broadcast_bitcast_fusion
  24.5 48.9 %copy.193 = f32[1,3,1025,2048]{3,1,2,0:T(4,128)} copy(f32[1,3,1025,2048]{3,2,1,0:T(8,128)} %broadcast_bitcast_fusion) | data formatting | bytes 50380800
  73.4 23.4 slice_bitcast_fusion.4
  96.8 42.9 %all-gather.2 = bf16[16,92,3]{1,2,0:T(4,128)(2,1)S(1)} all-gather(bf16[1,92,3]{1,2,0:T(4,128)(2,1)S(1)} %convert_bitcast_fusion), channel_id=1, replica_groups=mesh['tok'=16,'mem'=2] {'tok'}, dimensions={0}, use_global_device_ids=true | all-gather | bytes 9384 | tf_op jit(solution)/shard_map/all_gather | solution.py:126
  139.8 466.8 %while.2 = (u32[]{:T(128)}, f32[1,3,2096128]{2,1,0:T(4,128)}, f32[6288384]{0:T(1024)}, u32[]{}, f32[]{:T(128)}, /*index=5*/u32[]{}, u32[]{}, u32[]{}) while((u32[]{:T(128)}, f32[1,3,2096128]{2,1,0:T(4,128)}, f32[6288384]{0:T(1024)}, u32[]{}, f32[]{:T(128)}, /*index=5*/u32[]{}, u32[]{}, u32[]{}) %tuple.63), condition=%wide.cond, body=%wide.body.sunk | while | flops 9 | bytes 33538248
  140.3 83.8 %dynamic-slice_reduce_fusion.4 = f32[2096128]{0:T(1024)} fusion(f32[]{:T(128)} %broadcast.328, f32[1,3,2096128]{2,1,0:T(4,128)} %get-tuple-element.209, u32[]{:T(128)S(6)} %multiply.72, u32[]{:T(128)S(6)} %multiply.73), kind=kLoop, calls=%fused_computation.230.clone.1 | loop fusion | bytes 16769036
  224.2 71.3 %dynamic-update-slice.4 = f32[6288384]{0:T(1024)} dynamic-update-slice(f32[6288384]{0:T(1024)} %get-tuple-element.202, f32[2096128]{0:T(1024)} %dynamic-slice_reduce_fusion.4, u32[]{:T(128)S(6)} %add.436) | dynamic-update-slice | bytes 16769028
  295.9 83.8 %dynamic-slice_reduce_fusion.4 = f32[2096128]{0:T(1024)} fusion(f32[]{:T(128)} %broadcast.328, f32[1,3,2096128]{2,1,0:T(4,128)} %get-tuple-element.209, u32[]{:T(128)S(6)} %multiply.72, u32[]{:T(128)S(6)} %multiply.73), kind=kLoop, calls=%fused_computation.230.clone.1 | loop fusion | bytes 16769036
  379.7 71.3 %dynamic-update-slice.4 = f32[6288384]{0:T(1024)} dynamic-update-slice(f32[6288384]{0:T(1024)} %get-tuple-element.202, f32[2096128]{0:T(1024)} %dynamic-slice_reduce_fusion.4, u32[]{:T(128)S(6)} %add.436) | dynamic-update-slice | bytes 16769028
  451.5 83.8 %dynamic-slice_reduce_fusion.4 = f32[2096128]{0:T(1024)} fusion(f32[]{:T(128)} %broadcast.328, f32[1,3,2096128]{2,1,0:T(4,128)} %get-tuple-element.209, u32[]{:T(128)S(6)} %multiply.72, u32[]{:T(128)S(6)} %multiply.73), kind=kLoop, calls=%fused_computation.230.clone.1 | loop fusion | bytes 16769036
  535.3 71.3 %dynamic-update-slice.4 = f32[6288384]{0:T(1024)} dynamic-update-slice(f32[6288384]{0:T(1024)} %get-tuple-element.202, f32[2096128]{0:T(1024)} %dynamic-slice_reduce_fusion.4, u32[]{:T(128)S(6)} %add.436) | dynamic-update-slice | bytes 16769028
  606.6 37.0 %reshape.491 = f32[3,1024,2047]{2,1,0:T(8,128)} reshape(f32[6288384]{0:T(1024)} %get-tuple-element.79) | data formatting | bytes 50307072 | tf_op jit(solution)/shard_map/reshape | solution.py:57
  643.7 11.9 slice.115
  655.6 12.8 copy.185
  688.1 6.7 fusion.158
  706.4 7.0 slice.118
  713.5 6.9 copy.188
  720.4 10.6 fusion.155
  730.9 6.7 copy.189
  741.2 4.7 multiply_reduce_fusion.6
  765.9 6.2 copy.187
  772.2 6.4 all-reduce.19.cloned.1.call-done
  780.1 7.3 multiply_reduce_fusion.5
  787.4 228.1 %all-gather.13.cloned.1.call-done = bf16[3,1792,1472]{1,0,2:T(4,128)(2,1)} async-done(((bf16[3,1792,92]{1,0,2:T(4,128)(2,1)}), bf16[3,1792,1472]{1,0,2:T(4,128)(2,1)}) %all-gather.13.cloned.1.call-update) | async-done | bytes 15826960 | tf_op jit(solution)/shard_map/all_gather | solution.py:125
  1015.6 11.5 slice.128
  1028.1 18.1 fusion.28
  1046.2 14.6 slice.131
  1060.8 17.3 fusion.59
  1081.1 15.7 fusion.47
  1097.0 16.2 fusion.53
  1113.1 13.7 all-reduce.21.cloned.1.call-done
  1126.8 6.2 multiply_reduce_fusion.1
  1142.4 8.4 fusion.89
  1150.8 7.4 multiply_convert_fusion.1
  1165.3 8.1 all-reduce.28
  1177.3 8.7 multiply_reduce_fusion.2
  1192.7 12.3 copy.169
  1205.8 12.2 fusion.42
  1222.2 6.0 multiply_reduce_fusion
  1228.2 7.0 multiply_convert_fusion
  1241.2 5.1 convolution_bitcast_fusion.1
  1248.2 16.5 convolution_bitcast_fusion
  1264.8 17.1 fusion.46
  1281.9 22.0 pad_maximum_fusion
  1304.0 8.7 copy.192
  1321.4 7.1 copy.168
  1328.5 5.0 pad_bitcast_fusion
  1333.5 40.1 %copy.194 = bf16[1,3,1024,2048]{3,1,2,0:T(4,128)(2,1)} copy(bf16[1,3,1024,2048]{3,2,1,0:T(8,128)(2,1)S(1)} %pad_bitcast_fusion) | data formatting | bytes 25165824
  1373.6 16.2 fusion.159
  1389.9 469.4 %while.3 = (u32[]{:T(128)}, f32[1,3,2098176]{2,1,0:T(4,128)}, f32[6294528]{0:T(1024)}, u32[]{}, f32[]{:T(128)}, /*index=5*/u32[]{}, u32[]{}, u32[]{}) while((u32[]{:T(128)}, f32[1,3,2098176]{2,1,0:T(4,128)}, f32[6294528]{0:T(1024)}, u32[]{}, f32[]{:T(128)}, /*index=5*/u32[]{}, u32[]{}, u32[]{}) %tuple.66), condition=%wide.cond.1, body=%wide.body.1.sunk | while | flops 9 | bytes 33571016
  1390.8 83.9 %dynamic-slice_reduce_fusion.5 = f32[2098176]{0:T(1024)} fusion(f32[]{:T(128)} %broadcast.329, f32[1,3,2098176]{2,1,0:T(4,128)} %get-tuple-element.233, u32[]{:T(128)S(6)} %multiply.76, u32[]{:T(128)S(6)} %multiply.77), kind=kLoop, calls=%fused_computation.231.clone.1 | loop fusion | bytes 16785420
  1474.7 72.1 %dynamic-update-slice.5 = f32[6294528]{0:T(1024)} dynamic-update-slice(f32[6294528]{0:T(1024)} %get-tuple-element.226, f32[2098176]{0:T(1024)} %dynamic-slice_reduce_fusion.5, u32[]{:T(128)S(6)} %add.438) | dynamic-update-slice | bytes 16785412
  1547.3 83.9 %dynamic-slice_reduce_fusion.5 = f32[2098176]{0:T(1024)} fusion(f32[]{:T(128)} %broadcast.329, f32[1,3,2098176]{2,1,0:T(4,128)} %get-tuple-element.233, u32[]{:T(128)S(6)} %multiply.76, u32[]{:T(128)S(6)} %multiply.77), kind=kLoop, calls=%fused_computation.231.clone.1 | loop fusion | bytes 16785420
  1631.2 72.0 %dynamic-update-slice.5 = f32[6294528]{0:T(1024)} dynamic-update-slice(f32[6294528]{0:T(1024)} %get-tuple-element.226, f32[2098176]{0:T(1024)} %dynamic-slice_reduce_fusion.5, u32[]{:T(128)S(6)} %add.438) | dynamic-update-slice | bytes 16785412
  1703.7 83.9 %dynamic-slice_reduce_fusion.5 = f32[2098176]{0:T(1024)} fusion(f32[]{:T(128)} %broadcast.329, f32[1,3,2098176]{2,1,0:T(4,128)} %get-tuple-element.233, u32[]{:T(128)S(6)} %multiply.76, u32[]{:T(128)S(6)} %multiply.77), kind=kLoop, calls=%fused_computation.231.clone.1 | loop fusion | bytes 16785420
  1787.6 71.7 %dynamic-update-slice.5 = f32[6294528]{0:T(1024)} dynamic-update-slice(f32[6294528]{0:T(1024)} %get-tuple-element.226, f32[2098176]{0:T(1024)} %dynamic-slice_reduce_fusion.5, u32[]{:T(128)S(6)} %add.438) | dynamic-update-slice | bytes 16785412
  1859.3 39.6 %reshape.508 = f32[3,1024,2049]{2,1,0:T(8,128)} reshape(f32[6294528]{0:T(1024)} %get-tuple-element.84) | data formatting | bytes 50356224 | tf_op jit(solution)/shard_map/reshape | solution.py:67
  1898.9 9.7 reduce_sum.202
  1916.3 4.9 fusion.40
  1921.2 78.5 %all-reduce.5 = f32[3,1,1472]{2,0,1:T(4,128)S(1)} all-reduce(f32[3,1,1472]{2,0,1:T(4,128)S(1)} %maximum_bitcast_fusion), channel_id=7, replica_groups=mesh['tok'=16,'mem'=2] {'tok'}, use_global_device_ids=true, to_apply=%region_27.28.clone | all-reduce | flops 4416 | bytes 35328
  2001.1 433.7 %all-reduce.25.cloned.1.call-done = (f32[4,192,1472]{1,0,2:T(4,128)}, f32[3,1792,1472]{1,2,0:T(8,128)}) async-done(((f32[4,192,1472]{1,0,2:T(4,128)}, f32[3,1792,1472]{1,2,0:T(8,128)}), (f32[4,192,1472]{1,0,2:T(4,128)}, f32[3,1792,1472]{1,2,0:T(8,128)})) %all-reduce.25.cloned.1.call-update) | async-done | bytes 36175888
  2441.3 14.6 fusion.43
  2455.9 39.5 %all-reduce.6 = (f32[]{:T(128)}, f32[6,32]{1,0:T(8,128)S(1)}) all-reduce(f32[]{:T(128)S(6)} %add.257, f32[6,32]{1,0:T(8,128)S(1)} %dynamic_update_slice.3), channel_id=1, replica_groups=mesh['tok'=16,'mem'=2] {'tok','mem'}, use_global_device_ids=true, to_apply=%region_29.30 | all-reduce | flops 193 | bytes 1544 | tf_op jit(solution)/shard_map/psum | solution.py:355
  2497.6 7.4 multiply_subtract_fusion
  (289 shorter events, 136.2 us)
Async XLA Ops:
  7.2 730.5 %copy-start = (bf16[1,512,1472]{1,2,0:T(8,128)(2,1)S(1)}, bf16[1,512,1472]{1,2,0:T(8,128)(2,1)}, u32[]{:S(2)}) copy-start(bf16[1,512,1472]{1,2,0:T(8,128)(2,1)} %param.22) | copy-start | bytes 4521988
  7.2 665.4 %all-gather.9.cloned.1.call-start = ((), (), s32[]{:S(2)}) async-start(), calls=%async_computation | async-start | bytes 3203072 | tf_op jit(solution)/shard_map/all_gather | solution.py:124
  9.1 697.3 %all-gather.11.cloned.1.call-start = ((), (), s32[]{:S(2)}) async-start(), calls=%async_computation.2 | async-start | bytes 4866048 | tf_op jit(solution)/shard_map/all_gather | solution.py:128
  10.9 730.4 %all-reduce.17.cloned.1.call-start = ((), (), s32[]{:S(2)}) async-start(), calls=%async_computation.1 | async-start | bytes 12058624 | tf_op jit(solution)/shard_map/psum | solution.py:176
  73.4 23.4 copy-start.69
  655.6 15.4 copy-start.68
  668.4 14.9 copy-start.56
  668.4 77.6 %copy-start.54 = (f32[1472]{0:T(1024)}, f32[1472]{0:T(1024)S(1)}, u32[]{:S(2)}) copy-start(f32[1472]{0:T(1024)S(1)} %get-tuple-element.92) | copy-start | bytes 17668
  671.0 16.9 copy-start.62
  671.0 16.9 copy-start.60
  688.0 6.7 copy-start.23
  688.0 6.7 copy-start.25
  688.1 8.5 copy-start.31
  706.1 72.4 %all-reduce.19.cloned.1.call-start = ((), (), s32[]{:S(2)}) async-start(), calls=%async_computation.3 | async-start | bytes 3145728 | tf_op jit(solution)/shard_map/psum | solution.py:212
  737.7 8.9 copy-start.21
  750.8 6.7 copy-start.8
  762.0 253.5 %all-gather.13.cloned.1.call-start = ((), (), s32[]{:S(2)}) async-start(), calls=%async_computation.4 | async-start | bytes 22421504 | tf_op jit(solution)/shard_map/all_gather | solution.py:125
  765.7 361.1 %all-reduce.21.cloned.1.call-start = ((), (), s32[]{:S(2)}) async-start(), calls=%async_computation.5 | async-start | bytes 12058624 | tf_op jit(solution)/shard_map/psum | solution.py:241
  780.1 7.4 copy-start.19
  1015.6 12.5 copy-start.3
  1046.2 14.6 copy-start.10
  1096.9 817.6 %all-reduce.23.cloned.1.call-start = ((), (), s32[]{:S(2)}) async-start(), calls=%async_computation.6 | async-start | bytes 18874368
  1126.8 6.2 copy-start.7
  1126.8 7.1 copy-start.11
  1142.4 8.4 copy-start.78
  1150.8 7.4 copy-start.28
  1163.0 14.3 copy-start.55
  1163.0 14.3 copy-start.59
  1177.3 8.7 copy-start.35
  1177.3 8.9 copy-start.49
  1186.2 6.5 copy-start.37
  1186.4 6.3 copy-start.39
  1205.1 711.2 %all-reduce.27.cloned.1.call-start = ((), (), s32[]{:S(2)}) async-start(), calls=%async_computation.8 | async-start | bytes 24117248 | tf_op jit(solution)/shard_map/psum | solution.py:224
  1205.8 13.1 slice-start
  1205.8 12.2 copy-start.18
  1205.8 13.1 slice-start.1
  1205.8 16.2 slice-start.2
  1218.0 10.2 copy-start.6
  1228.2 7.0 copy-start.26
  1241.2 5.2 copy-start.43
  1246.3 18.4 slice-start.3
  1246.4 1188.5 %all-reduce.25.cloned.1.call-start = ((), (), s32[]{:S(2)}) async-start(), calls=%async_computation.7 | async-start | bytes 75366400
  1248.2 16.5 slice-start.4
  1248.2 16.5 copy-start.81
  1304.0 8.7 copy-start.30
  1373.6 16.2 copy-start.66
  1373.6 16.3 copy-start.67
  1898.9 10.5 copy-start.77
  1898.9 10.9 copy-start.38
  1898.9 10.9 copy-start.40
  1914.5 86.6 %copy-start.63 = (f32[1024]{0:T(1024)S(1)}, f32[1024]{0:T(1024)}, u32[]{:S(2)}) copy-start(f32[1024]{0:T(1024)} %copy-done.62) | copy-start | bytes 12292
  2497.4 13.8 copy-start.1
  2497.4 7.5 copy-start.41
  2497.4 7.5 copy-start.50
  2497.4 7.5 copy-start.51
  2497.4 10.0 copy-start.70
  2497.5 10.0 copy-start.71
  2497.5 10.0 copy-start.72
  2497.5 10.7 copy-start.73
  2497.5 10.7 copy-start.74
  2497.5 10.7 copy-start.75
  2497.5 11.3 copy-start.42
  2497.5 11.3 copy-start.52
  2497.5 11.3 copy-start.53
  (33 other events, 98.6 us)
Sparse Core Ops, SparseCore 0:
  11.3 69.5 all-gather.8
  84.3 62.7 all-gather.10
  706.2 27.4 all-reduce.16
  762.2 16.3 all-reduce.18
  781.7 233.8 all-gather.12
  1097.0 29.7 all-reduce.20
  1205.2 192.1 all-reduce.22
  1399.9 48.6 all-reduce.26
  1455.0 979.7 all-reduce.24
where the time goes:
time: 2560 us; the launch traced here: 2520 us
  local copies, waits for them, and re-layouts  1290 us (50%)
  waiting for transfers between devices  682 us (27%)
  matrix products  205 us (8%)
  blocking collectives  173 us (7%)
  other arithmetic  147 us (6%)
    unnamed x207, local copies, waits for them, and re-layouts  1130 us
    unnamed x11, waiting for transfers between devices  434 us
    all_gather x1, waiting for transfers between devices, shards(): lax.all_gather(ffn_weights.astype(jnp.bfloat16), 'tok', axis=2, tiled=True)  228 us
    unnamed x1, blocking collectives  78.5 us
  transfers between devices with their start and end apart: 9, of which 4 were waited for; matrix products, arithmetic and copies ran while one was open for 57% of the time, Pallas kernels for 0%

commit v1 on v0

v1 whole, which is shorter than its diff:
```python
import functools

import jax
import jax.numpy as jnp
from jax import lax
from jax.experimental import pallas as pl
from jax.experimental.pallas import tpu as pltpu
from jax.sharding import PartitionSpec as P

H = 6
DK = 64
NB = 32
LEN = 1024
STEP = 10
INNER = 384
D = 1472

EPS_NORM = 1e-06
NEG_FILL = -1e30
BETA_FIRST = 0.9
BETA_SECOND = 0.95
ADAM_EPS = 1e-08
RATE_MATRIX = 0.05
RATE_SMALL = 1.0
DECAY_MATRIX = 0.1
CLIP_NORM = 1.0

QB = 256
FC = 256
VMEM = 60 * 1024 * 1024
BF = jnp.bfloat16
F32 = jnp.float32


def dot_nn(a, b):
    return lax.dot_general(a, b, (((1,), (0,)), ((), ())), preferred_element_type=F32)


def dot_tn(a, b):
    return lax.dot_general(a, b, (((0,), (0,)), ((), ())), preferred_element_type=F32)


def dot_nt(a, b):
    return lax.dot_general(a, b, (((1,), (1,)), ((), ())), preferred_element_type=F32)


def bias_tile(vec, delta):
    row = vec[:, delta * QB : delta * QB + 2 * QB]
    wide = pltpu.roll(jnp.broadcast_to(row, (QB, 2 * QB)), 0, 1, stride=1, stride_axis=0)
    return wide[:, QB:]


def band(block):
    return max(0, block - LEN // 2 // QB)


def self_scores(q_ref, k_ref, segr_ref, segc_ref, tiles, block):
    low, high = band(block) * QB, (block + 1) * QB
    cols = slice(block * QB, high)
    scores = dot_tn(k_ref[:, low:high], q_ref[:, cols])
    scores = scores + jnp.concatenate([tiles[block - b] for b in range(band(block), block + 1)], axis=0)
    keys = lax.broadcasted_iota(jnp.int32, scores.shape, 0) + low
    queries = lax.broadcasted_iota(jnp.int32, scores.shape, 1) + block * QB
    allowed = (segc_ref[low:high, :] == segr_ref[:, cols]) & (keys <= queries)
    return jnp.where(allowed, scores, NEG_FILL)


def softmax_store(scores, v_block, o_ref, lse_ref, cols):
    top = jnp.max(scores, axis=0, keepdims=True)
    exps = jnp.exp(scores - top)
    total = jnp.sum(exps, axis=0, keepdims=True)
    probs = (exps * (1.0 / total)).astype(BF)
    o_ref[:, cols] = dot_nn(v_block, probs).astype(BF)
    lse_ref[0, :, cols] = top + jnp.log(total)


def self_fwd_kernel(q_ref, k_ref, v_ref, segr_ref, segc_ref, vec_ref, o_ref, lse_ref):
    tiles = [bias_tile(vec_ref[0], d) for d in range(LEN // 2 // QB + 1)]
    for block in range(LEN // QB):
        scores = self_scores(q_ref, k_ref, segr_ref, segc_ref, tiles, block)
        low, high = band(block) * QB, (block + 1) * QB
        softmax_store(scores, v_ref[:, low:high], o_ref, lse_ref, slice(block * QB, high))


def cross_fwd_kernel(q_ref, k_ref, v_ref, keep_ref, o_ref, lse_ref):
    for block in range(LEN // QB):
        cols = slice(block * QB, (block + 1) * QB)
        scores = dot_tn(k_ref[...], q_ref[:, cols]) + keep_ref[...]
        softmax_store(scores, v_ref[...], o_ref, lse_ref, cols)


def score_grads(scores, lse, k_block, v_block, q_block, do_block):
    probs = jnp.exp(scores - lse)
    grad_probs = dot_tn(v_block, do_block)
    delta = jnp.sum(probs * grad_probs, axis=0, keepdims=True)
    grads = (probs * (grad_probs - delta)).astype(BF)
    grad_q = dot_nn(k_block, grads)
    grad_k = dot_nt(q_block, grads)
    grad_v = dot_nt(do_block, probs.astype(BF))
    return grads, grad_q, grad_k, grad_v


def self_bwd_kernel(
    q_ref, k_ref, v_ref, do_ref, lse_ref, segr_ref, segc_ref, vec_ref,
    grad_ref, diag_ref, dk_acc, dv_acc, tile_acc,
):
    count = LEN // 2 // QB + 1
    tiles = [bias_tile(vec_ref[0], d) for d in range(count)]
    dk_acc[...] = jnp.zeros_like(dk_acc)
    dv_acc[...] = jnp.zeros_like(dv_acc)
    tile_acc[...] = jnp.zeros_like(tile_acc)
    for block in range(LEN // QB):
        low, high = band(block) * QB, (block + 1) * QB
        cols = slice(block * QB, high)
        scores = self_scores(q_ref, k_ref, segr_ref, segc_ref, tiles, block)
        grads, grad_q, grad_k, grad_v = score_grads(
            scores, lse_ref[0, :, cols], k_ref[:, low:high], v_ref[:, low:high], q_ref[:, cols], do_ref[:, cols]
        )
        grad_ref[0, :, cols] = grad_q.astype(BF)
        dk_acc[:, low:high] += grad_k
        dv_acc[:, low:high] += grad_v
        for b in range(band(block), block + 1):
            start = b * QB - low
            tile_acc[block - b] += grads[start : start + QB].astype(F32)
    grad_ref[1] = dk_acc[...].astype(BF)
    grad_ref[2] = dv_acc[...].astype(BF)
    spots = lax.broadcasted_iota(jnp.int32, (QB, QB), 0) + lax.broadcasted_iota(jnp.int32, (QB, QB), 1)
    mirror = (spots == QB - 1).astype(F32)
    for d in range(count):
        mirrored = lax.dot_general(
            tile_acc[d], mirror, (((1,), (0,)), ((), ())),
            precision=lax.Precision.HIGHEST, preferred_element_type=F32,
        )
        padded = jnp.concatenate([mirrored, jnp.zeros((QB, QB), F32)], axis=1)
        skewed = pltpu.roll(padded, 0, 1, stride=1, stride_axis=0)
        diag_ref[0, d : d + 1, :] = jnp.sum(skewed, axis=0, keepdims=True)


def cross_bwd_kernel(q_ref, k_ref, v_ref, do_ref, lse_ref, keep_ref, grad_ref, dk_acc, dv_acc):
    dk_acc[...] = jnp.zeros_like(dk_acc)
    dv_acc[...] = jnp.zeros_like(dv_acc)
    for block in range(LEN // QB):
        cols = slice(block * QB, (block + 1) * QB)
        scores = dot_tn(k_ref[...], q_ref[:, cols]) + keep_ref[...]
        grads, grad_q, grad_k, grad_v = score_grads(
            scores, lse_ref[0, :, cols], k_ref[...], v_ref[...], q_ref[:, cols], do_ref[:, cols]
        )
        grad_ref[0, :, cols] = grad_q.astype(BF)
        dk_acc[...] += grad_k
        dv_acc[...] += grad_v
    grad_ref[1] = dk_acc[...].astype(BF)
    grad_ref[2] = dv_acc[...].astype(BF)


def head_spec(first):
    return pl.BlockSpec((DK, LEN), lambda h: (first + h, 0))


def whole_spec(shape):
    return pl.BlockSpec(shape, lambda h: (0,) * len(shape))


def attn_call(kernel, heads, in_specs, out_specs, out_shape, operands, scratch, flops):
    return pl.pallas_call(
        kernel,
        grid=(heads,),
        in_specs=in_specs,
        out_specs=out_specs,
        out_shape=out_shape,
        scratch_shapes=scratch,
        compiler_params=pltpu.CompilerParams(vmem_limit_bytes=VMEM),
        cost_estimate=pl.CostEstimate(flops=flops, bytes_accessed=4 << 20, transcendentals=heads << 20),
    )(*operands)


def shape_of(*dims, dtype=BF):
    return jax.ShapeDtypeStruct(dims, dtype)


GRAD_SPEC = pl.BlockSpec((3, DK, LEN), lambda h: (0, h, 0))
LSE_SPEC = pl.BlockSpec((1, 1, LEN), lambda h: (h, 0, 0))


def self_forward(qkv, seg_row, seg_col, vec, heads):
    vec_spec = pl.BlockSpec((1, 1, vec.shape[2]), lambda h: (h, 0, 0))
    return attn_call(
        self_fwd_kernel, heads,
        [head_spec(0), head_spec(heads), head_spec(2 * heads), whole_spec((1, LEN)), whole_spec((LEN, 1)), vec_spec],
        [head_spec(0), LSE_SPEC],
        [shape_of(heads * DK, LEN), shape_of(heads, 1, LEN, dtype=F32)],
        (qkv, qkv, qkv, seg_row, seg_col, vec), [], heads * 2 * 2 * DK * LEN * LEN,
    )


def cross_forward(query, keyval, keep, heads):
    return attn_call(
        cross_fwd_kernel, heads,
        [head_spec(0), head_spec(0), head_spec(heads), whole_spec((LEN, 1))],
        [head_spec(0), LSE_SPEC],
        [shape_of(heads * DK, LEN), shape_of(heads, 1, LEN, dtype=F32)],
        (query, keyval, keyval, keep), [], heads * 2 * 2 * DK * LEN * LEN,
    )


def self_backward(qkv, grad_attn, lse, seg_row, seg_col, vec, heads):
    count = LEN // 2 // QB + 1
    vec_spec = pl.BlockSpec((1, 1, vec.shape[2]), lambda h: (h, 0, 0))
    out = shape_of(3, heads * DK, LEN)
    return attn_call(
        self_bwd_kernel, heads,
        [
            head_spec(0), head_spec(heads), head_spec(2 * heads), head_spec(0), LSE_SPEC,
            whole_spec((1, LEN)), whole_spec((LEN, 1)), vec_spec,
        ],
        [GRAD_SPEC, pl.BlockSpec((1, count, 2 * QB), lambda h: (h, 0, 0))],
        [out, shape_of(heads, count, 2 * QB, dtype=F32)],
        (qkv, qkv, qkv, grad_attn, lse, seg_row, seg_col, vec),
        [pltpu.VMEM((DK, LEN), F32), pltpu.VMEM((DK, LEN), F32), pltpu.VMEM((count, QB, QB), F32)],
        heads * 2 * 5 * DK * LEN * LEN,
    )


def cross_backward(query, keyval, grad_attn, lse, keep, heads):
    out = shape_of(3, heads * DK, LEN)
    return attn_call(
        cross_bwd_kernel, heads,
        [head_spec(0), head_spec(0), head_spec(heads), head_spec(0), LSE_SPEC, whole_spec((LEN, 1))],
        [GRAD_SPEC],
        [out],
        (query, keyval, keyval, grad_attn, lse, keep),
        [pltpu.VMEM((DK, LEN), F32), pltpu.VMEM((DK, LEN), F32)],
        heads * 2 * 5 * DK * LEN * LEN,
    )


def owner_copies(refs, owners_ref, target, sems, inward):
    copies = []
    slot = 0
    for ref in refs:
        for j in range(ref.shape[0]):
            owner = owners_ref[slot]
            here = target.at[:, owner]
            pair = (ref.at[j], here) if inward else (here, ref.at[j])
            copies.append(pltpu.make_async_copy(*pair, sems.at[slot]))
            slot += 1
    return copies


def ffn_kernel(by_owner, first, last, *refs):
    owners_ref, x_hbm, og_hbm, weight_hbm = refs[:4]
    refs = refs[4:]
    acc_refs, refs = ((), refs) if first else (refs[:2], refs[2:])
    out_refs, refs = refs[:2], refs[2:]
    grad_refs, refs = refs[:by_owner], refs[by_owner:]
    x_ref, og_ref, out_acc, back_acc, weights, grads, x_sems, in_sems, out_sems, acc_sems = refs[:10]
    unused, count, block, width = weights.shape
    rows = count * block
    inputs = [
        pltpu.make_async_copy(src, dst, x_sems.at[i])
        for i, (src, dst) in enumerate(((x_hbm, x_ref), (og_hbm, og_ref)))
    ]
    loads = [pltpu.make_async_copy(weight_hbm.at[:, c], weights.at[c], in_sems.at[c]) for c in range(3)]
    accs = [
        pltpu.make_async_copy(src, dst, acc_sems.at[i])
        for i, (src, dst) in enumerate(zip(acc_refs, (out_acc, back_acc)))
    ]
    for copy in (inputs[0], *loads, inputs[1], *accs):
        copy.start()
    inputs[0].wait()
    loads[0].wait()
    normed = x_ref[...]
    slope = 0.7978845608028654
    stores = []
    for step in range(width // FC):
        cols = slice(step * FC, (step + 1) * FC)
        w_gate = weights[0, :, :, cols].reshape(rows, FC)
        gate = dot_tn(w_gate, normed)
        square = gate * gate
        tanh = jnp.tanh(slope * gate * (1.0 + 0.044715 * square))
        half = 0.5 * (1.0 + tanh)
        act = gate * half
        act_grad = half + 0.5 * gate * (1.0 - tanh * tanh) * (slope * (1.0 + 0.134145 * square))
        if step == 0:
            loads[1].wait()
        w_up = weights[1, :, :, cols].reshape(rows, FC)
        upward = dot_tn(w_up, normed)
        hidden = (act * upward).astype(BF)
        if step == 0:
            loads[2].wait()
            inputs[1].wait()
        w_down = weights[2, :, :, cols].reshape(rows, FC)
        out_grad = og_ref[...]
        grad_hidden = dot_tn(w_down, out_grad)
        grad_gate = (grad_hidden * upward * act_grad).astype(BF)
        grad_up = (grad_hidden * act).astype(BF)
        if step == 0:
            for copy in accs:
                copy.wait()
        back = dot_nn(w_gate, grad_gate) + dot_nn(w_up, grad_up)
        out = dot_nn(w_down, hidden)
        if step > 0 or not first:
            back = back_acc[...] + back
            out = out_acc[...] + out
        final = step == width // FC - 1
        if final and last:
            out_low, back_low = refs[10:]
            back_low[...] = back.astype(BF)
            out_low[...] = out.astype(BF)
            sources = (out_low, back_low)
        else:
            back_acc[...] = back
            out_acc[...] = out
            sources = (out_acc, back_acc)
        if final:
            stores = [pltpu.make_async_copy(src, dst, acc_sems.at[i]) for i, (src, dst) in enumerate(zip(sources, out_refs))]
            for copy in stores:
                copy.start()
        shape = (count, block, FC)
        grads[0, :, :, cols] = dot_nt(normed, grad_gate).astype(BF).reshape(shape)
        grads[1, :, :, cols] = dot_nt(normed, grad_up).astype(BF).reshape(shape)
        grads[2, :, :, cols] = dot_nt(out_grad, hidden).astype(BF).reshape(shape)
    if by_owner == 1:
        sends = [pltpu.make_async_copy(grads.at[c], grad_refs[0].at[:, c], out_sems.at[c]) for c in range(3)]
    else:
        sends = owner_copies(grad_refs, owners_ref, grads, out_sems, False)
    for copy in sends:
        copy.start()
    for copy in stores + sends:
        copy.wait()


SMEM_SPEC = pl.BlockSpec(memory_space=pltpu.SMEM)
VMEM_SPEC = pl.BlockSpec(memory_space=pltpu.VMEM)
ANY_SPEC = pl.BlockSpec(memory_space=pl.ANY)


def feed_forward(owners, normed, out_grad, weights, sums, by_owner, last):
    count, unused, block, width = weights.shape
    rows, tokens = normed.shape
    first = sums is None
    kind = BF if last else F32
    total = shape_of(rows, tokens, dtype=kind)
    sizes = block_sizes(count) if by_owner else [count]
    results = pl.pallas_call(
        functools.partial(ffn_kernel, len(sizes), first, last),
        in_specs=[SMEM_SPEC] + [ANY_SPEC] * (3 if first else 5),
        out_specs=[ANY_SPEC] * (2 + len(sizes)),
        out_shape=[total, total] + [shape_of(size, 3, block, width) for size in sizes],
        input_output_aliases={} if first or last else {4: 0, 5: 1},
        scratch_shapes=[
            pltpu.VMEM((rows, tokens), BF),
            pltpu.VMEM((rows, tokens), BF),
            pltpu.VMEM((rows, tokens), F32),
            pltpu.VMEM((rows, tokens), F32),
            pltpu.VMEM((3, count, block, width), BF),
            pltpu.VMEM((3, count, block, width), BF),
            pltpu.SemaphoreType.DMA((2,)),
            pltpu.SemaphoreType.DMA((3,)),
            pltpu.SemaphoreType.DMA((count,)),
            pltpu.SemaphoreType.DMA((2,)),
        ]
        + [pltpu.VMEM((rows, tokens), BF)] * (2 if last else 0),
        compiler_params=pltpu.CompilerParams(vmem_limit_bytes=VMEM),
        cost_estimate=pl.CostEstimate(
            flops=9 * 2 * rows * width * tokens, bytes_accessed=32 << 20, transcendentals=width * tokens
        ),
    )(owners, normed, out_grad, weights, *(() if first else sums))
    return results[:2], list(results[2:])


def block_sizes(count):
    return [2] * 8 if count == 16 else [count]


def place_kernel(parts, inward, owners_ref, *refs):
    sems = refs[-1]
    if inward:
        copies = owner_copies(refs[:parts], owners_ref, refs[parts], sems, True)
    else:
        copies = owner_copies(refs[1 : 1 + parts], owners_ref, refs[0], sems, False)
    for copy in copies:
        copy.start()
    for copy in copies:
        copy.wait()


def place_blocks(owners, blocks):
    count = owners.shape[0]
    return pl.pallas_call(
        functools.partial(place_kernel, len(blocks), True),
        in_specs=[SMEM_SPEC] + [ANY_SPEC] * len(blocks),
        out_specs=VMEM_SPEC,
        out_shape=shape_of(1, count, *blocks[0].shape[2:]),
        scratch_shapes=[pltpu.SemaphoreType.DMA((count,))],
        compiler_params=pltpu.CompilerParams(vmem_limit_bytes=VMEM),
    )(owners, *blocks)[0]


def split_blocks(owners, value):
    count = owners.shape[0]
    sizes = block_sizes(count)
    return list(
        pl.pallas_call(
            functools.partial(place_kernel, len(sizes), False),
            in_specs=[SMEM_SPEC, VMEM_SPEC],
            out_specs=[ANY_SPEC] * len(sizes),
            out_shape=[shape_of(size, 1, *value.shape[1:]) for size in sizes],
            scratch_shapes=[pltpu.SemaphoreType.DMA((count,))],
            compiler_params=pltpu.CompilerParams(vmem_limit_bytes=VMEM),
        )(owners, value[None])
    )


def merge_kernel(own_map, other_map, own_ref, other_ref, out_ref):
    rows = own_ref.shape[-1]
    here = dot_nn(own_map[...], own_ref[...].reshape(-1, rows))
    there = dot_nn(other_map[...], other_ref[...].reshape(-1, rows))
    out_ref[0] = (here + there).astype(BF)


def merge_cores(own_map, other_map, own, other):
    count, maps, share, rows = own.shape
    height = own_map.shape[0]
    whole = pl.BlockSpec(own_map.shape, lambda c: (0, 0))
    part = pl.BlockSpec((count, 1, share, rows), lambda c: (0, c, 0, 0))
    return pl.pallas_call(
        merge_kernel,
        grid=(maps,),
        in_specs=[whole, whole, part, part],
        out_specs=pl.BlockSpec((1, height, rows), lambda c: (c, 0, 0)),
        out_shape=shape_of(maps, height, rows),
        compiler_params=pltpu.CompilerParams(vmem_limit_bytes=VMEM),
        cost_estimate=pl.CostEstimate(flops=4 * maps * height * count * share * rows, bytes_accessed=12 << 20, transcendentals=0),
    )(own_map, other_map, own, other)


def cross_grad_kernel(parts, owners_ref, own_map, other_map, own_ref, other_ref, attn_own, attn_other, x_ref, mem_ref, g_ref, *refs):
    grads, sems = refs[parts:]
    unused, count, maps, share, rows = grads.shape
    pairs = [(own_ref[c], other_ref[c]) for c in range(3)] + [(attn_own[...], attn_other[...])]
    for c, (own, other) in enumerate(pairs):
        picked = (dot_tn(own_map[...], own) + dot_tn(other_map[...], other)).astype(BF)
        wide = (x_ref, mem_ref, mem_ref, g_ref)[c][...]
        grads[0, :, c] = dot_nt(picked, wide).astype(BF).reshape(count, share, rows)
    copies = owner_copies(refs[:parts], owners_ref, grads, sems, False)
    for copy in copies:
        copy.start()
    for copy in copies:
        copy.wait()


def cross_weight_grads(owners, own_map, other_map, own, other, attn_own, attn_other, normed, memory, grad, share):
    count = owners.shape[0]
    sizes = block_sizes(count)
    rows, tokens = normed.shape
    return list(
        pl.pallas_call(
            functools.partial(cross_grad_kernel, len(sizes)),
            in_specs=[SMEM_SPEC] + [VMEM_SPEC] * 9,
            out_specs=[ANY_SPEC] * len(sizes),
            out_shape=[shape_of(size, 1, 4, share, rows) for size in sizes],
            scratch_shapes=[pltpu.VMEM((1, count, 4, share, rows), BF), pltpu.SemaphoreType.DMA((count,))],
            compiler_params=pltpu.CompilerParams(vmem_limit_bytes=VMEM),
            cost_estimate=pl.CostEstimate(flops=8 * count * share * rows * tokens, bytes_accessed=16 << 20, transcendentals=0),
        )(owners, own_map, other_map, own, other, attn_own, attn_other, normed, memory, grad)
    )


def self_grad_kernel(parts, owners_ref, x_ref, qkv_ref, g_ref, attn_ref, *refs):
    grads, sems = refs[parts:]
    unused, count, block, width = grads.shape
    first = dot_nt(x_ref[...], qkv_ref[...].reshape(-1, x_ref.shape[1]))
    second = dot_nt(g_ref[...], attn_ref[...])
    grads[0] = jnp.concatenate([first, second], axis=1).astype(BF).reshape(count, block, width)
    copies = owner_copies(refs[:parts], owners_ref, grads, sems, False)
    for copy in copies:
        copy.start()
    for copy in copies:
        copy.wait()


def self_weight_grads(owners, normed, grad_qkv, grad, attn):
    count = owners.shape[0]
    sizes = block_sizes(count)
    rows, tokens = normed.shape
    width = 4 * attn.shape[0]
    return list(
        pl.pallas_call(
            functools.partial(self_grad_kernel, len(sizes)),
            in_specs=[SMEM_SPEC] + [VMEM_SPEC] * 4,
            out_specs=[ANY_SPEC] * len(sizes),
            out_shape=[shape_of(size, 1, rows // count, width) for size in sizes],
            scratch_shapes=[pltpu.VMEM((1, count, rows // count, width), BF), pltpu.SemaphoreType.DMA((count,))],
            compiler_params=pltpu.CompilerParams(vmem_limit_bytes=VMEM),
            cost_estimate=pl.CostEstimate(flops=2 * rows * width * tokens, bytes_accessed=12 << 20, transcendentals=0),
        )(owners, normed, grad_qkv, grad, attn)
    )


def squeeze_rows(value, block, pad):
    return jnp.concatenate([value[i : i + block] for i in range(0, value.shape[0], pad)], axis=0)


def spread_kernel(block, pad, in_ref, out_ref):
    value = in_ref[...].astype(F32)
    gap = jnp.zeros((pad - block, value.shape[1]), F32)
    parts = []
    for i in range(0, value.shape[0], block):
        parts += [value[i : i + block], gap]
    out_ref[...] = jnp.concatenate(parts, axis=0).astype(BF)


def spread_rows(value, block, pad):
    height, tokens = value.shape
    rows = height // block * pad
    return pl.pallas_call(
        functools.partial(spread_kernel, block, pad),
        grid=(tokens // QB,),
        in_specs=[pl.BlockSpec((height, QB), lambda j: (0, j))],
        out_specs=pl.BlockSpec((rows, QB), lambda j: (0, j)),
        out_shape=shape_of(rows, tokens),
        compiler_params=pltpu.CompilerParams(vmem_limit_bytes=VMEM),
        cost_estimate=pl.CostEstimate(flops=rows * tokens, bytes_accessed=4 * rows * tokens, transcendentals=0),
    )(value)


def out_kernel(block, pad, resid_ref, own_ref, other_ref, out_ref):
    total = resid_ref[...] + (own_ref[...].astype(F32) + other_ref[...].astype(F32))
    out_ref[...] = squeeze_rows(total, block, pad).astype(BF)


def layer_output(resid, own, other, block, pad):
    rows, tokens = resid.shape
    part = pl.BlockSpec((rows, QB), lambda j: (0, j))
    return pl.pallas_call(
        functools.partial(out_kernel, block, pad),
        grid=(tokens // QB,),
        in_specs=[part, part, part],
        out_specs=pl.BlockSpec((rows // pad * block, QB), lambda j: (0, j)),
        out_shape=shape_of(rows // pad * block, tokens),
        compiler_params=pltpu.CompilerParams(vmem_limit_bytes=VMEM),
        cost_estimate=pl.CostEstimate(flops=4 * rows * tokens, bytes_accessed=10 * rows * tokens, transcendentals=0),
    )(resid, own, other)


def norm_back_kernel(upstream, squeeze, n_ups, *refs):
    values_ref, inv_ref, gain_ref, base_ref = refs[:4]
    outs = refs[4 + n_ups :]
    up = upstream(*refs[4 : 4 + n_ups])
    values = values_ref[...].astype(F32)
    inv_root = inv_ref[...]
    scaled = up * gain_ref[...]
    along = jnp.sum(values * scaled, axis=0, keepdims=True) * (inv_root * inv_root * (1.0 / D))
    total = base_ref[...].astype(F32) + inv_root * (scaled - values * along)
    if squeeze:
        outs[0][...] = squeeze_rows(total, *squeeze)
    else:
        outs[0][...] = total
        outs[2][...] = total.astype(BF)
    gain_part = jnp.sum(up * (values * inv_root), axis=1, keepdims=True)

    @pl.when(pl.program_id(0) == 0)
    def start():
        outs[1][...] = gain_part

    @pl.when(pl.program_id(0) > 0)
    def add():
        outs[1][...] += gain_part


def norm_back(values, inv_root, gain, base, upstream, ups, fixed, squeeze=None, flops=0):
    rows, tokens = values.shape
    part = pl.BlockSpec((rows, QB), lambda j: (0, j))

    def spec(array, whole):
        if whole:
            return pl.BlockSpec(array.shape, lambda j: (0,) * array.ndim)
        return pl.BlockSpec(array.shape[:-1] + (QB,), lambda j: (0,) * (array.ndim - 1) + (j,))

    column = pl.BlockSpec((rows, 1), lambda j: (0, 0))
    height = rows // squeeze[1] * squeeze[0] if squeeze else rows
    return pl.pallas_call(
        functools.partial(norm_back_kernel, upstream, squeeze, len(ups)),
        grid=(tokens // QB,),
        in_specs=[part, pl.BlockSpec((1, QB), lambda j: (0, j)), column, part]
        + [spec(a, w) for a, w in zip(ups, fixed)],
        out_specs=[pl.BlockSpec((height, QB), lambda j: (0, j)), column] + ([] if squeeze else [part]),
        out_shape=[shape_of(height, tokens, dtype=F32), shape_of(rows, 1, dtype=F32)]
        + ([] if squeeze else [shape_of(rows, tokens)]),
        compiler_params=pltpu.CompilerParams(vmem_limit_bytes=VMEM),
        cost_estimate=pl.CostEstimate(flops=flops + 12 * rows * tokens, bytes_accessed=20 * rows * tokens, transcendentals=0),
    )(values, inv_root, gain, base, *ups)


def rotated(value, step):
    return lax.ppermute(value, "tok", [(t, (t // 4 + step) % 4 * 4 + t % 4) for t in range(16)])


def flipped(value, bits):
    return lax.ppermute(value, "tok", [(t, t ^ bits) for t in range(16)])


def block_owners():
    count = lax.axis_size("tok")
    index = lax.axis_index("tok")
    if count != 16:
        return jnp.arange(count, dtype=jnp.int32)
    owners = [(index // 4 + 4 - k) % 4 * 4 + (index % 4 ^ bits) for bits in range(4) for k in range(4)]
    return jnp.stack(owners).astype(jnp.int32)


class Transfer:
    def __init__(self, steps):
        self.steps = steps
        self.value = None
        self.flying = None

    @property
    def done(self):
        return self.value is not None

    def resume(self, arrived):
        try:
            return next(self.steps) if self.flying is None else self.steps.send(arrived)
        except StopIteration as stop:
            self.value = stop.value
            return []

    def launch(self, sends):
        self.flying = [move(operand, *way) for operand, move, way in sends]

    def finish(self):
        while not self.done:
            self.launch(self.resume(self.flying))
        return self.value


def tick(state, *transfers):
    moving = [t for t in transfers if not t.done]
    state, arrived = lax.optimization_barrier((state, [t.flying or [] for t in moving]))
    sends = [t.resume(a) for t, a in zip(moving, arrived)]
    operands = [[send[0] for send in group] for group in sends]
    state, operands = lax.optimization_barrier((state, operands))
    for t, group, ready in zip(moving, sends, operands):
        t.launch([(value, *send[1:]) for value, send in zip(ready, group)])
    return state


def gather_steps(value):
    if lax.axis_size("tok") != 16:
        return [lax.all_gather(value, "tok", axis=0, tiled=False)]
    far = yield [(value, rotated, (k,)) for k in (1, 2, 3)]
    low, high = jnp.stack([value, far[0]]), jnp.stack(far[1:])
    x_low, x_high, y_low, y_high = yield [
        (low, flipped, (1,)), (high, flipped, (1,)), (low, flipped, (2,)), (high, flipped, (2,))
    ]
    d_low, d_high = yield [(y_low, flipped, (1,)), (x_high, flipped, (2,))]
    return [low, high, x_low, x_high, y_low, y_high, d_low, d_high]


def low_sum(*terms):
    return sum(term.astype(F32) for term in terms).astype(BF)


def scatter_steps(blocks):
    if len(blocks) == 1:
        return lax.psum_scatter(blocks[0], "tok", scatter_dimension=0, tiled=False).astype(F32)
    m_low, m_high, x_low, x_high, y_low, y_high, d_low, d_high = blocks
    to_y, to_x, x_first, y_second = yield [
        (d_low, flipped, (1,)), (d_high, flipped, (2,)), (x_low, flipped, (1,)), (y_high, flipped, (2,))
    ]
    x_second, y_first = yield [
        (low_sum(x_high, to_x), flipped, (1,)), (low_sum(y_low, to_y), flipped, (2,))
    ]
    held = [
        low_sum(mine[k], gx[k], gy[k])
        for mine, gx, gy in ((m_low, x_first, y_first), (m_high, x_second, y_second))
        for k in range(2)
    ]
    far = yield [(held[k], rotated, (4 - k,)) for k in (1, 2, 3)]
    return sum(term.astype(F32) for term in (held[0], *far))


def sum_all(value):
    if lax.axis_size("tok") != 16:
        return lax.psum(value, ("tok", "mem"))
    value = value + other_core(value)
    value = (value + flipped(value, 1)) + (flipped(value, 2) + flipped(value, 3))
    return (value + rotated(value, 2)) + (rotated(value, 1) + rotated(value, 3))


def norm_stats(values):
    return lax.rsqrt(jnp.sum(values * values, axis=0, keepdims=True) * (1.0 / D) + EPS_NORM)


def adam_step(weight, first_mom, second_mom, gradient, clip_scale, step_rate, decay_rate):
    clipped = gradient * clip_scale
    first_new = BETA_FIRST * first_mom + (1.0 - BETA_FIRST) * clipped
    second_new = BETA_SECOND * second_mom + (1.0 - BETA_SECOND) * clipped * clipped
    first_hat = first_new / (1.0 - BETA_FIRST**STEP)
    second_hat = second_new / (1.0 - BETA_SECOND**STEP)
    weight_new = weight - step_rate * (
        first_hat / (jnp.sqrt(second_hat) + ADAM_EPS) + decay_rate * weight
    )
    return (weight_new, first_new, second_new)


def other_core(value):
    return lax.ppermute(value, "mem", [(0, 1), (1, 0)])


def core_pair(value, mem_index):
    other = other_core(value)
    return jnp.where(mem_index == 0, value, other), jnp.where(mem_index == 0, other, value)


def chunk_sizes(width):
    if lax.axis_size("tok") != 16:
        return [FC] * (width // FC)
    return [4 * FC, width - 4 * FC]


def shards(
    inputs,
    memory,
    kept_mask,
    segment_ids,
    bucket_ids,
    out_grad,
    self_weights,
    self_first,
    self_second,
    cross_weights,
    cross_first,
    cross_second,
    ffn_weights,
    ffn_first,
    ffn_second,
    norm_gains,
    gains_first,
    gains_second,
    rel_bias,
    rel_first,
    rel_second,
):
    count = lax.axis_size("tok")
    mem_index = lax.axis_index("mem")
    heads = rel_bias.shape[0]
    own = heads * DK
    block = norm_gains.shape[1]
    pad = -(-block // 16) * 16
    rows = count * pad
    share = cross_weights.shape[1]
    enc = memory.shape[1]

    def widen(value, axis):
        shape = value.shape
        split = value.reshape(shape[:axis] + (shape[axis] // block, block) + shape[axis + 1 :])
        pads = [(0, 0)] * split.ndim
        pads[axis + 1] = (0, pad - block)
        return jnp.pad(split, pads).reshape(shape[:axis] + (-1,) + shape[axis + 1 :])

    def narrow(value, axis):
        shape = value.shape
        split = value.reshape(shape[:axis] + (shape[axis] // pad, pad) + shape[axis + 1 :])
        kept = lax.slice_in_dim(split, 0, block, axis=axis + 1)
        return kept.reshape(shape[:axis] + (-1,) + shape[axis + 1 :])

    owners = block_owners()
    self_wire = widen(jnp.transpose(self_weights, (2, 0, 1)).astype(BF).reshape(block, 4 * own), 0)
    share_pad = -(-share // 16) * 16
    self_wire = self_wire.at[block : block + 3, :block].set(norm_gains.astype(BF))
    self_w = Transfer(gather_steps(self_wire[None]))
    tick((), self_w)
    ffn_wire = widen(jnp.transpose(ffn_weights, (0, 2, 1)).astype(BF), 1)
    ffn_w = []
    start = 0
    for size in chunk_sizes(ffn_wire.shape[2]):
        ffn_w.append(lax.all_gather(ffn_wire[:, :, start : start + size], "tok", axis=0, tiled=False))
        start += size
    cross_wire = jnp.pad(widen(cross_weights.astype(BF), 2), ((0, 0), (0, share_pad - share), (0, 0)))[None]
    cross_w = Transfer(gather_steps(cross_wire))
    ffn_wire = tick(ffn_wire, cross_w)

    x_low = spread_rows(inputs.T, block, pad)
    resid_zero = x_low.astype(F32)
    inv_one = norm_stats(resid_zero)
    x_low, inv_one = tick((x_low, inv_one), self_w)
    resid_zero = x_low.astype(F32)
    og_low = spread_rows(out_grad.T, block, pad)
    og_low, inv_one = tick((og_low, inv_one), self_w, cross_w)
    mem_own = spread_rows(memory.reshape(enc, D).T, block, pad)
    mem_parts = core_pair(mem_own, mem_index)
    mem_full = jnp.concatenate(mem_parts, axis=1)
    kept_parts = core_pair(kept_mask.reshape(enc), mem_index)
    keep = jnp.where(jnp.concatenate(kept_parts) > 0, 0.0, NEG_FILL).astype(F32).reshape(LEN, 1)
    seg_row = segment_ids.reshape(1, LEN)
    seg_col = segment_ids.reshape(LEN, 1)
    bucket_hot = (bucket_ids[None, :] == jnp.arange(NB, dtype=jnp.int32)[:, None]).astype(F32)
    bias_vec = jnp.dot(rel_bias, bucket_hot, precision=lax.Precision.HIGHEST)
    vec = jnp.pad(bias_vec, ((0, 0), (QB, 0))).reshape(heads, 1, QB + LEN)
    mem_full, inv_one, vec, keep = tick((mem_full, inv_one, vec, keep), self_w)

    self_blocks = place_blocks(owners, self_w.finish())
    gain_blocks = self_blocks[:, block : block + 3, :block]
    gains = widen(jnp.transpose(gain_blocks, (1, 0, 2)).reshape(3, -1), 1).reshape(3, rows, 1).astype(F32)
    self_own = self_blocks.reshape(rows, 4 * own)
    self_low, self_high = core_pair(self_own, mem_index)
    normed_one = (resid_zero * inv_one * gains[0]).astype(BF)
    qkv = dot_tn(self_own[:, : 3 * own], normed_one).astype(BF)
    qkv = tick(qkv, cross_w)
    attn_self, lse_self = self_forward(qkv, seg_row, seg_col, vec, heads)
    attn_self = tick(attn_self, cross_w)
    attn_low, attn_high = core_pair(attn_self, mem_index)
    resid_one = resid_zero + (
        dot_nn(self_low[:, 3 * own :], attn_low) + dot_nn(self_high[:, 3 * own :], attn_high)
    )

    inv_two = norm_stats(resid_one)
    normed_two = (resid_one * inv_two * gains[1]).astype(BF)
    cross_blocks = place_blocks(owners, cross_w.finish())
    place = jnp.arange(INNER, dtype=jnp.int32)[:, None]
    spot = jnp.arange(count * share_pad, dtype=jnp.int32)[None, :]
    match = (place // (2 * share) == spot // share_pad) & (place % share == spot % share_pad)
    core_of = place // share % 2
    own_map = (match & (core_of == mem_index)).astype(BF)
    other_map = (match & (core_of != mem_index)).astype(BF)
    cross_full = merge_cores(own_map, other_map, cross_blocks, other_core(cross_blocks))
    cross_own = lax.dynamic_slice_in_dim(cross_full, mem_index * own, own, 1)
    keyval = dot_nn(cross_own[1:3].reshape(2 * own, rows), mem_full).astype(BF)
    query = dot_nn(cross_own[0], normed_two).astype(BF)
    attn_cross, lse_cross = cross_forward(query, keyval, keep, heads)
    attn_cross_other = other_core(attn_cross)
    attn_cross_full = jnp.concatenate(
        [jnp.where(mem_index == 0, attn_cross, attn_cross_other), jnp.where(mem_index == 0, attn_cross_other, attn_cross)]
    )
    resid_two = resid_one + dot_tn(cross_full[3], attn_cross_full)

    inv_three = norm_stats(resid_two)
    normed_three = (resid_two * inv_three * gains[2]).astype(BF)
    sums = None
    ffn_g = []
    for i, weights in enumerate(ffn_w):
        last = i == len(ffn_w) - 1
        sums, grads = feed_forward(owners, normed_three, og_low, weights, sums, not last, last)
        ffn_g.append(Transfer(scatter_steps(grads)))
        if not last:
            sums = tick(sums, ffn_g[i])
    out_low, back_low = sums
    back_other = other_core(back_low)
    back_low, back_other = tick((back_low, back_other), *ffn_g[1:])
    grad_two, gain_three, grad_two_low = norm_back(
        resid_two, inv_three, gains[2], og_low,
        lambda own, other: own[...].astype(F32) + other[...].astype(F32), (back_low, back_other), (False, False),
    )

    grad_cattn = dot_nn(cross_own[3], grad_two_low).astype(BF)
    (cross_d,) = cross_backward(query, keyval, grad_cattn, lse_cross, keep, heads)
    cross_d = tick(cross_d, ffn_g[0])
    cross_d_other = other_core(cross_d)
    grad_q_full = jnp.concatenate(
        [jnp.where(mem_index == 0, cross_d[0], cross_d_other[0]), jnp.where(mem_index == 0, cross_d_other[0], cross_d[0])]
    )
    grad_one, gain_two, grad_one_low = norm_back(
        resid_one, inv_two, gains[1], grad_two,
        lambda w, g: dot_tn(w[...], g[...]), (cross_full[0], grad_q_full), (True, False), flops=2 * INNER * rows * LEN,
    )

    grad_sattn = dot_tn(self_own[:, 3 * own :], grad_one_low).astype(BF)
    grad_qkv, diag = self_backward(qkv, grad_sattn, lse_self, seg_row, seg_col, vec, heads)
    self_g = Transfer(scatter_steps(self_weight_grads(owners, normed_one, grad_qkv, grad_one_low, attn_self)))
    grad_qkv = tick(grad_qkv, self_g, ffn_g[0])
    other_half = lax.dynamic_slice_in_dim(own_map, (1 - mem_index) * own, own, 0)
    own_half = lax.dynamic_slice_in_dim(own_map, mem_index * own, own, 0)
    cross_g = Transfer(
        scatter_steps(
            cross_weight_grads(
                owners, own_half, other_half, cross_d, cross_d_other, attn_cross, attn_cross_other,
                normed_two, mem_full, grad_two_low, share_pad,
            )
        )
    )
    grad_qkv = tick(grad_qkv, cross_g)

    grad_other = other_core(grad_qkv)
    qkv_low = jnp.where(mem_index == 0, grad_qkv, grad_other).reshape(3 * own, LEN)
    qkv_high = jnp.where(mem_index == 0, grad_other, grad_qkv).reshape(3 * own, LEN)
    input_grad, gain_one = norm_back(
        x_low, inv_one, gains[0], grad_one,
        lambda a, b, c, d: dot_nn(a[:, : 3 * own], c[...]) + dot_nn(b[:, : 3 * own], d[...]),
        (self_low, self_high, qkv_low, qkv_high), (True, True, False, False), (block, pad), 12 * own * rows * LEN,
    )
    input_grad, gain_one = tick((input_grad.T, gain_one), self_g)
    kv_own = lax.dynamic_slice_in_dim(cross_d[1:], mem_index * enc, enc, 2)
    kv_other = lax.dynamic_slice_in_dim(cross_d_other[1:], mem_index * enc, enc, 2)
    kv_all = jnp.concatenate(
        [jnp.where(mem_index == 0, kv_own, kv_other), jnp.where(mem_index == 0, kv_other, kv_own)], axis=1
    ).reshape(2 * INNER, enc)
    memory_grad = narrow(dot_tn(cross_full[1:3].reshape(2 * INNER, rows), kv_all), 0).T.reshape(1, enc, D)
    memory_grad = tick(memory_grad, cross_g, self_g, ffn_g[0])
    layer_out = layer_output(resid_two, out_low, other_core(out_low), block, pad).T
    spread = jnp.zeros((heads, QB + LEN), F32)
    diag = diag[:, :, ::-1]
    for d in range(diag.shape[1]):
        spread = spread.at[:, d * QB : d * QB + 2 * QB].add(diag[:, d])
    rel_grad = jnp.dot(spread[:, QB:], bucket_hot.T, precision=lax.Precision.HIGHEST)
    layer_out = tick(layer_out, cross_g)
    ffn_sum = jnp.concatenate([t.finish() for t in ffn_g], axis=2)
    cross_sum = cross_g.finish()[0, :, :share]
    self_sum = self_g.finish()[0, :block]

    self_grads = self_sum.reshape(block, 4, own).transpose(1, 2, 0)
    ffn_grads = ffn_sum[:, :block].transpose(0, 2, 1)
    cross_grads = narrow(cross_sum, 2)
    local_squares = (
        jnp.sum(jnp.square(self_sum)) + jnp.sum(jnp.square(ffn_sum)) + jnp.sum(jnp.square(cross_sum))
    )
    gain_rows = 3 * rows // 128
    gain_grad = jnp.where(mem_index == 0, jnp.concatenate([gain_one, gain_two, gain_three], axis=1).T, 0.0)
    rel_padded = lax.dynamic_update_slice_in_dim(
        jnp.zeros((8, 128), F32), jnp.pad(rel_grad, ((0, 0), (0, 128 - NB))), mem_index * heads, 0
    )
    totals = sum_all(
        jnp.concatenate([gain_grad.reshape(gain_rows, 128), rel_padded.at[H, 0].set(local_squares)])
    )
    gains_total, rel_total = totals[:gain_rows].reshape(3, rows), totals[gain_rows : gain_rows + H, :NB]
    gains_sum = lax.dynamic_slice_in_dim(gains_total, lax.axis_index("tok") * pad, pad, 1)[:, :block]
    total_squares = totals[gain_rows + H, 0] + jnp.sum(gains_total * gains_total)
    grad_norm = jnp.sqrt(total_squares + jnp.sum(rel_total * rel_total))
    rel_g = lax.dynamic_slice_in_dim(rel_total, mem_index * heads, heads, 0)
    clip_scale = CLIP_NORM / jnp.maximum(grad_norm, CLIP_NORM)
    self_new = adam_step(self_weights, self_first, self_second, self_grads, clip_scale, RATE_MATRIX, DECAY_MATRIX)
    cross_new = adam_step(cross_weights, cross_first, cross_second, cross_grads, clip_scale, RATE_MATRIX, DECAY_MATRIX)
    ffn_new = adam_step(ffn_weights, ffn_first, ffn_second, ffn_grads, clip_scale, RATE_MATRIX, DECAY_MATRIX)
    gains_new = adam_step(norm_gains, gains_first, gains_second, gains_sum, clip_scale, RATE_SMALL, 0.0)
    rel_new = adam_step(rel_bias, rel_first, rel_second, rel_g, clip_scale, RATE_SMALL, 0.0)
    return (
        layer_out,
        input_grad,
        memory_grad,
        grad_norm,
        *self_new,
        *cross_new,
        *ffn_new,
        *gains_new,
        *rel_new,
    )


def solution(mesh):
    placed = (
        P("tok", None),
        P("tok", "mem", None),
        P("tok", "mem"),
        P("tok"),
        P(),
        P("tok", None),
        P(None, "mem", "tok"),
        P(None, "mem", "tok"),
        P(None, "mem", "tok"),
        P(None, ("tok", "mem"), None),
        P(None, ("tok", "mem"), None),
        P(None, ("tok", "mem"), None),
        P(None, "mem", "tok"),
        P(None, "mem", "tok"),
        P(None, "mem", "tok"),
        P(None, "tok"),
        P(None, "tok"),
        P(None, "tok"),
        P("mem", None),
        P("mem", None),
        P("mem", None),
    )
    return jax.shard_map(
        shards,
        mesh=mesh,
        in_specs=placed,
        out_specs=(
            P("tok", None),
            P("tok", None),
            P("tok", "mem", None),
            P(),
            P(None, "mem", "tok"),
            P(None, "mem", "tok"),
            P(None, "mem", "tok"),
            P(None, ("tok", "mem"), None),
            P(None, ("tok", "mem"), None),
            P(None, ("tok", "mem"), None),
            P(None, "mem", "tok"),
            P(None, "mem", "tok"),
            P(None, "mem", "tok"),
            P(None, "tok"),
            P(None, "tok"),
            P(None, "tok"),
            P("mem", None),
            P("mem", None),
            P("mem", None),
        ),
        check_vma=False,
    )
```

time: 2560 us -> 655 us (0.26); the launches traced: 2520 us -> 647 us
  local copies, waits for them, and re-layouts: 1290 us -> 50 us
  waiting for transfers between devices: 682 us -> 187 us
  Pallas kernels: 0 us -> 218 us
  matrix products: 205 us -> 24.9 us
  blocking collectives: 173 us -> 0 us
  other arithmetic: 147 us -> 80.7 us
  starting transfers between devices: 0.93 us -> 66.7 us
    unnamed x207 -> x150, local copies, waits for them, and re-layouts: 1130 us -> 11.6 us
    unnamed x11 -> x3, waiting for transfers between devices: 434 us -> 0.05 us
    pallas_call x0 -> x18, Pallas kernels: none -> 218 us  [the longest x2 75.1 us: feed_forward(): pl.pallas_call(functools.partial(ffn_kernel, len(sizes), first, last), in...]
    all_gather x3 -> x2, waiting for transfers between devices: 228 us -> 24.1 us  [shards(): lax.all_gather(ffn_wire[:, :, start:start + size], 'tok', axis=0, tiled=F...]
    dot_general x34 -> x10, matrix products: 204 us -> 24.7 us  [the longest x4 13.4 us: dot_tn(): lax.dot_general(a, b, (((0,), (0,)), ((), ())), preferred_element_type=F32)]
    ppermute x0 -> x62, waiting for transfers between devices: none -> 163 us  [the longest x33 99.4 us: flipped(): return lax.ppermute(value, 'tok', [(t, t ^ bits) for t in range(16)])]
    unnamed x1 -> x0, blocking collectives: 78.5 us -> none
    reshape x5 -> x10, local copies, waits for them, and re-layouts: 76.7 us -> 6.15 us  [the longest x1 1.78 us: narrow(): return kept.reshape(shape[:axis] + (-1,) + shape[axis + 1:])]
  transfers between devices with their start and end apart: 9 -> 65, of which waited for: 4 -> 29; matrix products, arithmetic and copies ran while one was open for 57% -> 18% of each run, Pallas kernels for 0% -> 29%
where the time goes in v1:
time: 655 us; the launch traced here: 647 us
  Pallas kernels  218 us (33%)
  waiting for transfers between devices  187 us (29%)
  other arithmetic  80.7 us (12%)
  starting transfers between devices  66.7 us (10%)
  local copies, waits for them, and re-layouts  50 us (8%)
  matrix products  24.9 us (4%)
  between operations  20.4 us (3%)
    ppermute x33, waiting for transfers between devices, flipped(): return lax.ppermute(value, 'tok', [(t, t ^ bits) for t in range(16)])  99.4 us
    pallas_call x2, Pallas kernels, feed_forward(): pl.pallas_call(functools.partial(ffn_kernel, len(sizes), first, last), in...  75.1 us
    ppermute x18, waiting for transfers between devices, rotated(): lax.ppermute(value, 'tok', [(t, (t // 4 + step) % 4 * 4 + t % 4) for t in...  58.9 us
    pallas_call x4, Pallas kernels, attn_call(): pl.pallas_call(kernel, grid=(heads,), in_specs=in_specs, out_specs=out_sp...  49.4 us
    pallas_call x3, Pallas kernels, norm_back(): pl.pallas_call(functools.partial(norm_back_kernel, upstream, squeeze, len...  38.7 us
    ppermute x33, starting transfers between devices, flipped(): return lax.ppermute(value, 'tok', [(t, t ^ bits) for t in range(16)])  35.2 us
    ppermute x18, starting transfers between devices, rotated(): lax.ppermute(value, 'tok', [(t, (t // 4 + step) % 4 * 4 + t % 4) for t in...  29.3 us
    all_gather x2, waiting for transfers between devices, shards(): lax.all_gather(ffn_wire[:, :, start:start + size], 'tok', axis=0, tiled=F...  24.1 us
  transfers between devices with their start and end apart: 65, of which 29 were waited for; matrix products, arithmetic and copies ran while one was open for 18% of the time, Pallas kernels for 29%

profile of v1, /device:TPU:0, one launch (start us, length us, event | category | flops | bytes accessed | tf_op | source)
XLA Modules:
  0.0 647.1 jit_solution(15447995198313617663)
XLA Ops:
  10.7 3.1 collective-permute-start
  13.7 2.6 collective-permute-start.1
  17.7 2.4 shard_map.350
  21.5 4.5 shard_map.348.refs_0_
  26.0 2.6 multiply_reduce_fusion.2
  32.3 4.4 shard_map.349.refs_2_.refs_3_
  37.8 2.8 collective-permute-start.9
  44.0 3.0 collective-permute-done.7
  48.5 6.0 collective-permute-done.8
  59.9 11.4 %collective-permute-done.5.refs_4_ = bf16[2,1,96,768]{3,2,1,0:T(8,128)(2,1)} collective-permute-done((bf16[2,1,96,768]{3,2,1,0:T(8,128)(2,1)S(1)}, bf16[2,1,96,768]{3,2,1,0:T(8,128)(2,1)}, u32[]{:S(2)}, u32[]{:S(2)}) %collective-permute-start.5) | collective-permute-done | bytes 294944 | tf_op jit(solution)/shard_map/ppermute | solution.py:600
  71.3 6.8 %collective-permute-done.6.refs_5_ = bf16[2,1,96,768]{3,2,1,0:T(8,128)(2,1)} collective-permute-done((bf16[2,1,96,768]{3,2,1,0:T(8,128)(2,1)}, bf16[2,1,96,768]{3,2,1,0:T(8,128)(2,1)}, u32[]{:S(2)}, u32[]{:S(2)}) %collective-permute-start.6) | collective-permute-done | bytes 294944 | tf_op jit(solution)/shard_map/ppermute | solution.py:600
  83.4 2.0 pad_maximum_fusion.mem_ref
  85.4 4.5 collective-permute-done.12.refs_6_
  91.2 4.2 shard_map.351
  105.2 3.0 fusion.12.q_ref.k_ref.v_ref
  108.3 8.0 %collective-permute-done.15.refs_2_ = bf16[2,1,4,16,1536]{4,3,2,1,0:T(8,128)(2,1)} collective-permute-done((bf16[2,1,4,16,1536]{4,3,2,1,0:T(8,128)(2,1)}, bf16[2,1,4,16,1536]{4,3,2,1,0:T(8,128)(2,1)}, u32[]{:S(2)}, u32[]{:S(2)}) %collective-permute-start.15) | collective-permute-done | bytes 393248 | tf_op jit(solution)/shard_map/ppermute | solution.py:600
  116.3 16.7 %collective-permute-done.16.refs_3_ = bf16[2,1,4,16,1536]{4,3,2,1,0:T(8,128)(2,1)} collective-permute-done((bf16[2,1,4,16,1536]{4,3,2,1,0:T(8,128)(2,1)S(1)}, bf16[2,1,4,16,1536]{4,3,2,1,0:T(8,128)(2,1)}, u32[]{:S(2)}, u32[]{:S(2)}) %collective-permute-start.16) | collective-permute-done | bytes 393248 | tf_op jit(solution)/shard_map/ppermute | solution.py:600
  137.5 8.2 %shard_map.352 = (bf16[192,1024]{1,0:T(8,128)(2,1)}, f32[3,1,1024]{2,1,0:T(1,128)}) custom-call(bf16[576,1024]{1,0:T(8,128)(2,1)} %fusion.12.q_ref.k_ref.v_ref, bf16[576,1024]{1,0:T(8,128)(2,1)} %fusion.12.q_ref.k_ref.v_ref, bf16[576,1024]{1,0:T(8,128)(2,1)} %fusion.12.q_ref.k_ref.v_ref, s32[1,1024]{1,0:T(1,128)} %bitcast.210, s32[1024,1]{1,0:T(8,128)} %copy.75.segc_ref, ...), custom_call_target="tpu_custom_call" | custom-call | flops 805306368 | bytes 4194304 | tf_op jit(solution)/shard_map/pallas_call | solution.py:164
  145.7 6.4 collective-permute-done.19.refs_6_
  152.9 4.5 shard_map.353
  159.8 2.7 broadcast_select_fusion.1
  166.8 2.1 copy-done.1
  168.9 8.0 %shard_map.354 = bf16[4,384,1536]{2,1,0:T(8,128)(2,1)} custom-call(bf16[384,256]{1,0:T(8,128)(2,1)} %get-tuple-element.469.own_map, bf16[384,256]{1,0:T(8,128)(2,1)} %get-tuple-element.468.other_map, bf16[16,4,16,1536]{3,2,1,0:T(8,128)(2,1)} %bitcast.180, bf16[16,4,16,1536]{3,2,1,0:T(8,128)(2,1)} %collective-permute-done.22.other_ref), custom_call_target="tpu_custom_call" | custom-call | flops 2415919104 | bytes 12582912 | tf_op jit(solution)/shard_map/pallas_call | solution.py:426
  178.3 2.8 convolution_convert_fusion.3.q_ref
  181.1 2.3 convolution_convert_fusion.k_ref.v_ref
  183.4 12.5 %shard_map.355 = (bf16[192,1024]{1,0:T(8,128)(2,1)}, f32[3,1,1024]{2,1,0:T(1,128)}) custom-call(bf16[192,1024]{1,0:T(8,128)(2,1)} %convolution_convert_fusion.3.q_ref, bf16[384,1024]{1,0:T(8,128)(2,1)} %convolution_convert_fusion.k_ref.v_ref, bf16[384,1024]{1,0:T(8,128)(2,1)} %convolution_convert_fusion.k_ref.v_ref, f32[1024,1]{1,0:T(8,128)} %broadcast_select_fusion.10.keep_ref), custom_call_target="tpu_custom_call" | custom-call | flops 805306368 | bytes 4194304 | tf_op jit(solution)/shard_map/pallas_call | solution.py:164
  199.1 5.2 multiply_reduce_fusion
  204.3 2.6 copy-done
  206.9 2.3 multiply_convert_fusion.refs_1_
  209.1 41.9 %shard_map.356 = (f32[1536,1024]{1,0:T(8,128)}, f32[1536,1024]{1,0:T(8,128)}, bf16[2,3,96,1024]{3,2,1,0:T(8,128)(2,1)}, bf16[2,3,96,1024]{3,2,1,0:T(8,128)(2,1)}...) custom-call(s32[16]{0:T(128)} %stack.102.owners_ref.refs_0_, ...), custom_call_target="tpu_custom_call" | custom-call | flops 28991029248 | bytes 33554432 | tf_op jit(solution)/shard_map/pallas_call | solution.py:344
  251.1 24.1 %all-gather.5.cloned.1.call-done = bf16[48,96,768]{2,1,0:T(8,128)(2,1)} async-done(((bf16[3,96,768]{2,1,0:T(8,128)(2,1)}), bf16[48,96,768]{2,1,0:T(8,128)(2,1)}) %all-gather.5.cloned.1.call-update) | async-done | bytes 7077904 | tf_op jit(solution)/shard_map/all_gather | solution.py:779
  275.2 33.2 %shard_map.357 = (bf16[1536,1024]{1,0:T(8,128)(2,1)}, bf16[1536,1024]{1,0:T(8,128)(2,1)}, bf16[16,3,96,768]{3,2,1,0:T(8,128)(2,1)}) custom-call(s32[16]{0:T(128)} %stack.102.owners_ref.refs_0_, bf16[1536,1024]{1,0:T(8,128)(2,1)} %multiply_convert_fusion.refs_1_, bf16[1536,1024]{1,0:T(8,128)(2,1)} %shard_map.349.refs_2_.refs_3_, ...), custom_call_target="tpu_custom_call" | custom-call | flops 21743271936 | bytes 33554432 | tf_op jit(solution)/shard_map/pallas_call | solution.py:344
  316.1 12.0 %shard_map.359 = (f32[1536,1024]{1,0:T(8,128)}, f32[1536,1]{1,0:T(8,128)}, bf16[1536,1024]{1,0:T(8,128)(2,1)}) custom-call(f32[1536,1024]{1,0:T(8,128)} %copy-done, f32[1,1024]{1,0:T(1,128)} %bitcast.203, f32[1536,1]{1,0:T(8,128)} %squeeze.30.refs_2_, bf16[1536,1024]{1,0:T(8,128)(2,1)} %shard_map.349.refs_2_.refs_3_, ...), custom_call_target="tpu_custom_call" | custom-call | flops 18874368 | bytes 31457280 | tf_op jit(solution)/shard_map/pallas_call | solution.py:582
  328.1 3.7 convolution_convert_fusion.2.do_ref
  331.8 15.0 %shard_map.360.own_ref = bf16[3,192,1024]{2,1,0:T(8,128)(2,1)} custom-call(bf16[192,1024]{1,0:T(8,128)(2,1)} %convolution_convert_fusion.3.q_ref, bf16[384,1024]{1,0:T(8,128)(2,1)} %convolution_convert_fusion.k_ref.v_ref, bf16[384,1024]{1,0:T(8,128)(2,1)} %convolution_convert_fusion.k_ref.v_ref, bf16[192,1024]{1,0:T(8,128)(2,1)} %convolution_convert_fusion.2.do_ref, ...), custom_call_target="tpu_custom_call" | custom-call | flops 2013265920 | bytes 4194304 | tf_op jit(solution)/shard_map/pallas_call | solution.py:164
  346.8 2.4 collective-permute-done.27
  349.2 30.9 %collective-permute-done.28 = bf16[2,3,96,1024]{3,2,1,0:T(8,128)(2,1)} collective-permute-done((bf16[2,3,96,1024]{3,2,1,0:T(8,128)(2,1)}, bf16[2,3,96,1024]{3,2,1,0:T(8,128)(2,1)}, u32[]{:S(2)}, u32[]{:S(2)}) %collective-permute-start.28) | collective-permute-done | bytes 1179680 | tf_op jit(solution)/shard_map/ppermute | solution.py:600
  381.8 2.8 add_convert_fusion
  384.6 2.9 add_convert_fusion.1
  390.4 2.1 collective-permute-start.32
  392.5 2.4 slice_bitcast_fusion.refs_4_
  396.1 12.7 %shard_map.361 = (f32[1536,1024]{1,0:T(8,128)}, f32[1536,1]{1,0:T(8,128)}, bf16[1536,1024]{1,0:T(8,128)(2,1)}) custom-call(f32[1536,1024]{1,0:T(8,128)} %copy-done.1, f32[1,1024]{1,0:T(1,128)} %bitcast.202, f32[1536,1]{1,0:T(8,128)} %squeeze.31.refs_2_, f32[1536,1024]{1,0:T(8,128)} %get-tuple-element.327.refs_3_, ...), custom_call_target="tpu_custom_call" | custom-call | flops 1226833920 | bytes 31457280 | tf_op jit(solution)/shard_map/pallas_call | solution.py:582
  408.7 3.8 convolution_convert_fusion.1.do_ref
  412.5 13.7 %shard_map.362 = (bf16[3,192,1024]{2,1,0:T(8,128)(2,1)}, f32[3,3,512]{2,1,0:T(4,128)}) custom-call(bf16[576,1024]{1,0:T(8,128)(2,1)} %fusion.12.q_ref.k_ref.v_ref, bf16[576,1024]{1,0:T(8,128)(2,1)} %fusion.12.q_ref.k_ref.v_ref, bf16[576,1024]{1,0:T(8,128)(2,1)} %fusion.12.q_ref.k_ref.v_ref, bf16[192,1024]{1,0:T(8,128)(2,1)} %convolution_convert_fusion.1.do_ref, ...), custom_call_target="tpu_custom_call" | custom-call | flops 2013265920 | bytes 4194304 | tf_op jit(solution)/shard_map/pallas_call | solution.py:164
  426.2 8.4 %shard_map.363 = (bf16[2,1,96,768]{3,2,1,0:T(8,128)(2,1)}, bf16[2,1,96,768]{3,2,1,0:T(8,128)(2,1)}, bf16[2,1,96,768]{3,2,1,0:T(8,128)(2,1)}, bf16[2,1,96,768]{3,...) custom-call(s32[16]{0:T(128)} %stack.102.owners_ref.refs_0_, ...), custom_call_target="tpu_custom_call" | custom-call | flops 2415919104 | bytes 12582912 | tf_op jit(solution)/shard_map/pallas_call | solution.py:488
  434.7 2.5 fusion.24
  437.2 3.3 fusion.26
  440.5 11.2 %shard_map.364 = (bf16[2,1,4,16,1536]{4,3,2,1,0:T(8,128)(2,1)}, bf16[2,1,4,16,1536]{4,3,2,1,0:T(8,128)(2,1)}, bf16[2,1,4,16,1536]{4,3,2,1,0:T(8,128)(2,1)}, bf16...) custom-call(s32[16]{0:T(128)} %stack.102.owners_ref.refs_0_, ...), custom_call_target="tpu_custom_call" | custom-call | flops 3221225472 | bytes 16777216 | tf_op jit(solution)/shard_map/pallas_call | solution.py:457
  456.9 2.4 copy.76
  460.8 7.0 %shard_map.358 = bf16[1472,1024]{1,0:T(8,128)(2,1)} custom-call(f32[1536,1024]{1,0:T(8,128)} %copy-done, bf16[1536,1024]{1,0:T(8,128)(2,1)} %get-tuple-element.311.own_ref, bf16[1536,1024]{1,0:T(8,128)(2,1)} %collective-permute-done.24.other_ref), custom_call_target="tpu_custom_call" | custom-call | flops 6291456 | bytes 15728640 | tf_op jit(solution)/shard_map/pallas_call | solution.py:535
  476.7 3.2 broadcast_select_fusion.4
  481.5 14.0 %shard_map.365 = (f32[1472,1024]{1,0:T(8,128)}, f32[1536,1]{1,0:T(8,128)}) custom-call(bf16[1536,1024]{1,0:T(8,128)(2,1)} %shard_map.348.refs_0_, f32[1,1024]{1,0:T(1,128)} %bitcast.204, f32[1536,1]{1,0:T(8,128)} %squeeze.32.refs_2_, f32[1536,1024]{1,0:T(8,128)} %get-tuple-element.353.refs_3_, bf16[1536,768]{1,0:T(8,128)(2,1)} %copy-done.5, ...), custom_call_target="tpu_custom_call" | custom-call | flops 3642753024 | bytes 31457280 | tf_op jit(solution)/shard_map/pallas_call | solution.py:582
  513.4 35.7 %collective-permute-done.45 = bf16[3,96,1024]{2,1,0:T(8,128)(2,1)} collective-permute-done((bf16[3,96,1024]{2,1,0:T(8,128)(2,1)}, bf16[3,96,1024]{2,1,0:T(8,128)(2,1)}, u32[]{:S(2)}, u32[]{:S(2)}) %collective-permute-start.45) | collective-permute-done | bytes 589856 | tf_op jit(solution)/shard_map/ppermute | solution.py:596
  549.2 2.1 fusion.45
  551.3 2.1 fusion.46
  560.6 2.4 collective-permute-start.50
  563.0 2.0 collective-permute-start.51
  569.7 4.7 collective-permute-start.53
  576.3 2.4 fusion.16
  580.1 12.9 %collective-permute-done.53 = bf16[1,4,16,1536]{3,2,1,0:T(8,128)(2,1)S(1)} collective-permute-done((bf16[1,4,16,1536]{3,2,1,0:T(8,128)(2,1)S(1)}, bf16[1,4,16,1536]{3,2,1,0:T(8,128)(2,1)S(1)}, u32[]{:S(2)}, u32[]{:S(2)}) %collective-permute-start.53) | collective-permute-done | bytes 196640 | tf_op jit(solution)/shard_map/ppermute | solution.py:596
  607.8 3.8 collective-permute-start.61
  612.5 2.0 reshape_squeeze.8
  626.6 2.0 mul.377
  629.4 5.4 multiply_subtract_fusion
  (372 shorter events, 145.8 us)
Async XLA Ops:
  7.2 202.0 %all-gather.7.cloned.1.call-start = ((), (), s32[]{:S(2)}) async-start(), calls=%async_computation.3 | async-start | bytes 10027008 | tf_op jit(solution)/shard_map/all_gather | solution.py:779
  10.0 265.2 %all-gather.5.cloned.1.call-start = ((), (), s32[]{:S(2)}) async-start(), calls=%async_computation.2 | async-start | bytes 7520256 | tf_op jit(solution)/shard_map/all_gather | solution.py:779
  10.7 26.6 %collective-permute-start = (bf16[1,96,768]{2,1,0:T(8,128)(2,1)S(1)}, bf16[1,96,768]{2,1,0:T(8,128)(2,1)S(1)}, u32[]{:S(2)}, u32[]{:S(2)}) collective-permute-start(bf16[1,96,768]{2,1,0:T(8,128)(2,1)S(1)} %bitcast.195), channel_id=1, source_target_pairs={{0,8},{2,10},{4,12},{6,14},{8,16},{10,18},{12,20},{14,22},{16,24},... | collective-permute-start | bytes 442376 | tf_op jit(solution)/shard_map/ppermute | solution.py:596
  13.7 24.1 %collective-permute-start.1 = (bf16[1,96,768]{2,1,0:T(8,128)(2,1)S(1)}, bf16[1,96,768]{2,1,0:T(8,128)(2,1)}, u32[]{:S(2)}, u32[]{:S(2)}) collective-permute-start(bf16[1,96,768]{2,1,0:T(8,128)(2,1)S(1)} %bitcast.196), channel_id=1, source_target_pairs={{0,16},{2,18},{4,20},{6,22},{8,24},{10,26},{12,28},{14,30},{16,0},... | collective-permute-start | bytes 442376 | tf_op jit(solution)/shard_map/ppermute | solution.py:596
  16.3 24.2 %collective-permute-start.2 = (bf16[1,96,768]{2,1,0:T(8,128)(2,1)S(1)}, bf16[1,96,768]{2,1,0:T(8,128)(2,1)}, u32[]{:S(2)}, u32[]{:S(2)}) collective-permute-start(bf16[1,96,768]{2,1,0:T(8,128)(2,1)S(1)} %bitcast.197), channel_id=1, source_target_pairs={{0,24},{2,26},{4,28},{6,30},{8,0},{10,2},{12,4},{14,6},{16,8},{18,... | collective-permute-start | bytes 442376 | tf_op jit(solution)/shard_map/ppermute | solution.py:596
  20.0 63.1 %collective-permute-start.10 = (bf16[1536,512]{1,0:T(8,128)(2,1)}, bf16[1536,512]{1,0:T(8,128)(2,1)S(1)}, u32[]{:S(2)}, u32[]{:S(2)}) collective-permute-start(bf16[1536,512]{1,0:T(8,128)(2,1)} %shard_map.350), channel_id=1, source_target_pairs={{0,1},{1,0},{2,3},{3,2},{4,5},{5,4},{6,7},{7,6},{8,9},{9,8},{10,11... | collective-permute-start | bytes 4718600 | tf_op jit(solution)/shard_map/ppermute | solution.py:709
  20.0 16.6 %collective-permute-start.11 = (s32[512]{0:T(512)S(1)}, s32[512]{0:T(512)S(1)}, u32[]{:S(2)}, u32[]{:S(2)}) collective-permute-start(s32[512]{0:T(512)S(1)} %bitcast.213), channel_id=1, source_target_pairs={{0,1},{1,0},{2,3},{3,2},{4,5},{5,4},{6,7},{7,6},{8,9},{9,8},{10,11... | collective-permute-start | bytes 6152 | tf_op jit(solution)/shard_map/ppermute | solution.py:709
  21.4 572.4 %reduce-scatter.2.cloned.1.call-start = ((), (), s32[]{:S(2)}) async-start(), calls=%async_computation.1 | async-start | bytes 7520256 | tf_op jit(solution)/shard_map/reduce_scatter | solution.py:667
  36.7 10.3 %collective-permute-start.7 = (bf16[1,4,16,1536]{3,2,1,0:T(8,128)(2,1)}, bf16[1,4,16,1536]{3,2,1,0:T(8,128)(2,1)S(1)}, u32[]{:S(2)}, u32[]{:S(2)}) collective-permute-start(bf16[1,4,16,1536]{3,2,1,0:T(8,128)(2,1)} %get-tuple-element.260), channel_id=1, source_target_pairs={{0,8},{2,10},{4,12},{6,14},{8,16},{10,18},{12,20},{14,22},{16,24},... | collective-permute-start | bytes 589832 | tf_op jit(solution)/shard_map/ppermute | solution.py:596
  37.3 17.2 %collective-permute-start.8 = (bf16[1,4,16,1536]{3,2,1,0:T(8,128)(2,1)}, bf16[1,4,16,1536]{3,2,1,0:T(8,128)(2,1)S(1)}, u32[]{:S(2)}, u32[]{:S(2)}) collective-permute-start(bf16[1,4,16,1536]{3,2,1,0:T(8,128)(2,1)} %get-tuple-element.260), channel_id=1, source_target_pairs={{0,16},{2,18},{4,20},{6,22},{8,24},{10,26},{12,28},{14,30},{16,0},... | collective-permute-start | bytes 589832 | tf_op jit(solution)/shard_map/ppermute | solution.py:596
  37.8 19.0 %collective-permute-start.9 = (bf16[1,4,16,1536]{3,2,1,0:T(8,128)(2,1)}, bf16[1,4,16,1536]{3,2,1,0:T(8,128)(2,1)}, u32[]{:S(2)}, u32[]{:S(2)}) collective-permute-start(bf16[1,4,16,1536]{3,2,1,0:T(8,128)(2,1)} %get-tuple-element.260), channel_id=1, source_target_pairs={{0,24},{2,26},{4,28},{6,30},{8,0},{10,2},{12,4},{14,6},{16,8},{18,... | collective-permute-start | bytes 589832 | tf_op jit(solution)/shard_map/ppermute | solution.py:596
  42.4 17.4 %collective-permute-start.3 = (bf16[2,1,96,768]{3,2,1,0:T(8,128)(2,1)S(1)}, bf16[2,1,96,768]{3,2,1,0:T(8,128)(2,1)}, u32[]{:S(2)}, u32[]{:S(2)}) collective-permute-start(bf16[2,1,96,768]{3,2,1,0:T(8,128)(2,1)S(1)} %get-tuple-element.256.refs_0_), channel_id=1, source_target_pairs={{0,2},{2,0},{4,6},{6,4},{8,10},{10,8},{12,14},{14,12},{16,18},{18,... | collective-permute-start | bytes 884744 | tf_op jit(solution)/shard_map/ppermute | solution.py:600
  47.0 12.9 %collective-permute-start.4 = (bf16[2,1,96,768]{3,2,1,0:T(8,128)(2,1)}, bf16[2,1,96,768]{3,2,1,0:T(8,128)(2,1)}, u32[]{:S(2)}, u32[]{:S(2)}) collective-permute-start(bf16[2,1,96,768]{3,2,1,0:T(8,128)(2,1)} %get-tuple-element.257.refs_1_), channel_id=1, source_target_pairs={{0,2},{2,0},{4,6},{6,4},{8,10},{10,8},{12,14},{14,12},{16,18},{18,... | collective-permute-start | bytes 884744 | tf_op jit(solution)/shard_map/ppermute | solution.py:600
  55.2 16.1 %collective-permute-start.5 = (bf16[2,1,96,768]{3,2,1,0:T(8,128)(2,1)S(1)}, bf16[2,1,96,768]{3,2,1,0:T(8,128)(2,1)}, u32[]{:S(2)}, u32[]{:S(2)}) collective-permute-start(bf16[2,1,96,768]{3,2,1,0:T(8,128)(2,1)S(1)} %get-tuple-element.256.refs_0_), channel_id=1, source_target_pairs={{0,4},{2,6},{4,0},{6,2},{8,12},{10,14},{12,8},{14,10},{16,20},{18,... | collective-permute-start | bytes 884744 | tf_op jit(solution)/shard_map/ppermute | solution.py:600
  56.8 21.3 %collective-permute-start.6 = (bf16[2,1,96,768]{3,2,1,0:T(8,128)(2,1)}, bf16[2,1,96,768]{3,2,1,0:T(8,128)(2,1)}, u32[]{:S(2)}, u32[]{:S(2)}) collective-permute-start(bf16[2,1,96,768]{3,2,1,0:T(8,128)(2,1)} %get-tuple-element.257.refs_1_), channel_id=1, source_target_pairs={{0,4},{2,6},{4,0},{6,2},{8,12},{10,14},{12,8},{14,10},{16,20},{18,... | collective-permute-start | bytes 884744 | tf_op jit(solution)/shard_map/ppermute | solution.py:600
  81.1 8.8 %collective-permute-start.12 = (bf16[2,1,96,768]{3,2,1,0:T(8,128)(2,1)}, bf16[2,1,96,768]{3,2,1,0:T(8,128)(2,1)S(1)}, u32[]{:S(2)}, u32[]{:S(2)}) collective-permute-start(bf16[2,1,96,768]{3,2,1,0:T(8,128)(2,1)} %collective-permute-done.5.refs_4_), channel_id=1, source_target_pairs={{0,2},{2,0},{4,6},{6,4},{8,10},{10,8},{12,14},{14,12},{16,18},{18,... | collective-permute-start | bytes 884744 | tf_op jit(solution)/shard_map/ppermute | solution.py:600
  82.6 8.6 %collective-permute-start.13 = (bf16[2,1,96,768]{3,2,1,0:T(8,128)(2,1)}, bf16[2,1,96,768]{3,2,1,0:T(8,128)(2,1)}, u32[]{:S(2)}, u32[]{:S(2)}) collective-permute-start(bf16[2,1,96,768]{3,2,1,0:T(8,128)(2,1)} %collective-permute-done.4.refs_3_), channel_id=1, source_target_pairs={{0,4},{2,6},{4,0},{6,2},{8,12},{10,14},{12,8},{14,10},{16,20},{18,... | collective-permute-start | bytes 884744 | tf_op jit(solution)/shard_map/ppermute | solution.py:600
  95.4 64.4 %collective-permute-start.14 = (bf16[1536,768]{1,0:T(8,128)(2,1)}, bf16[1536,768]{1,0:T(8,128)(2,1)}, u32[]{:S(2)}, u32[]{:S(2)}) collective-permute-start(bf16[1536,768]{1,0:T(8,128)(2,1)} %bitcast.181), channel_id=1, source_target_pairs={{0,1},{1,0},{2,3},{3,2},{4,5},{5,4},{6,7},{7,6},{8,9},{9,8},{10,11... | collective-permute-start | bytes 7077896 | tf_op jit(solution)/shard_map/ppermute | solution.py:709
  95.5 20.8 %collective-permute-start.15 = (bf16[2,1,4,16,1536]{4,3,2,1,0:T(8,128)(2,1)}, bf16[2,1,4,16,1536]{4,3,2,1,0:T(8,128)(2,1)}, u32[]{:S(2)}, u32[]{:S(2)}) collective-permute-start(bf16[2,1,4,16,1536]{4,3,2,1,0:T(8,128)(2,1)} %pad_maximum_fusion.4.refs_0_), channel_id=1, source_target_pairs={{0,2},{2,0},{4,6},{6,4},{8,10},{10,8},{12,14},{14,12},{16,18},{18,... | collective-permute-start | bytes 1179656 | tf_op jit(solution)/shard_map/ppermute | solution.py:600
  97.0 36.0 %collective-permute-start.16 = (bf16[2,1,4,16,1536]{4,3,2,1,0:T(8,128)(2,1)S(1)}, bf16[2,1,4,16,1536]{4,3,2,1,0:T(8,128)(2,1)}, u32[]{:S(2)}, u32[]{:S(2)}) collective-permute-start(bf16[2,1,4,16,1536]{4,3,2,1,0:T(8,128)(2,1)S(1)} %pad_maximum_fusion.5.refs_1_), channel_id=1, source_target_pairs={{0,2},{2,0},{4,6},{6,4},{8,10},{10,8},{12,14},{14,12},{16,18},{18,... | collective-permute-start | bytes 1179656 | tf_op jit(solution)/shard_map/ppermute | solution.py:600
  97.6 35.3 %collective-permute-start.17 = (bf16[2,1,4,16,1536]{4,3,2,1,0:T(8,128)(2,1)}, bf16[2,1,4,16,1536]{4,3,2,1,0:T(8,128)(2,1)}, u32[]{:S(2)}, u32[]{:S(2)}) collective-permute-start(bf16[2,1,4,16,1536]{4,3,2,1,0:T(8,128)(2,1)} %pad_maximum_fusion.4.refs_0_), channel_id=1, source_target_pairs={{0,4},{2,6},{4,0},{6,2},{8,12},{10,14},{12,8},{14,10},{16,20},{18,... | collective-permute-start | bytes 1179656 | tf_op jit(solution)/shard_map/ppermute | solution.py:600
  98.7 36.1 %collective-permute-start.18 = (bf16[2,1,4,16,1536]{4,3,2,1,0:T(8,128)(2,1)S(1)}, bf16[2,1,4,16,1536]{4,3,2,1,0:T(8,128)(2,1)}, u32[]{:S(2)}, u32[]{:S(2)}) collective-permute-start(bf16[2,1,4,16,1536]{4,3,2,1,0:T(8,128)(2,1)S(1)} %pad_maximum_fusion.5.refs_1_), channel_id=1, source_target_pairs={{0,4},{2,6},{4,0},{6,2},{8,12},{10,14},{12,8},{14,10},{16,20},{18,... | collective-permute-start | bytes 1179656 | tf_op jit(solution)/shard_map/ppermute | solution.py:600
  134.8 17.4 %collective-permute-start.19 = (bf16[2,1,4,16,1536]{4,3,2,1,0:T(8,128)(2,1)}, bf16[2,1,4,16,1536]{4,3,2,1,0:T(8,128)(2,1)S(1)}, u32[]{:S(2)}, u32[]{:S(2)}) collective-permute-start(bf16[2,1,4,16,1536]{4,3,2,1,0:T(8,128)(2,1)} %collective-permute-done.17.refs_4_), channel_id=1, source_target_pairs={{0,2},{2,0},{4,6},{6,4},{8,10},{10,8},{12,14},{14,12},{16,18},{18,... | collective-permute-start | bytes 1179656 | tf_op jit(solution)/shard_map/ppermute | solution.py:600
  136.2 16.1 %collective-permute-start.20 = (bf16[2,1,4,16,1536]{4,3,2,1,0:T(8,128)(2,1)}, bf16[2,1,4,16,1536]{4,3,2,1,0:T(8,128)(2,1)}, u32[]{:S(2)}, u32[]{:S(2)}) collective-permute-start(bf16[2,1,4,16,1536]{4,3,2,1,0:T(8,128)(2,1)} %collective-permute-done.16.refs_3_), channel_id=1, source_target_pairs={{0,4},{2,6},{4,0},{6,2},{8,12},{10,14},{12,8},{14,10},{16,20},{18,... | collective-permute-start | bytes 1179656 | tf_op jit(solution)/shard_map/ppermute | solution.py:600
  157.5 11.4 %collective-permute-start.22 = (bf16[16,4,16,1536]{3,2,1,0:T(8,128)(2,1)}, bf16[16,4,16,1536]{3,2,1,0:T(8,128)(2,1)}, u32[]{:S(2)}, u32[]{:S(2)}) collective-permute-start(bf16[16,4,16,1536]{3,2,1,0:T(8,128)(2,1)} %bitcast.179), channel_id=1, source_target_pairs={{0,1},{1,0},{2,3},{3,2},{4,5},{5,4},{6,7},{7,6},{8,9},{9,8},{10,11... | collective-permute-start | bytes 9437192 | tf_op jit(solution)/shard_map/ppermute | solution.py:709
  159.3 4.4 collective-permute-start.21
  195.9 2.0 collective-permute-start.23
  310.3 5.8 collective-permute-start.25
  310.3 36.5 %collective-permute-start.26 = (bf16[2,3,96,1024]{3,2,1,0:T(8,128)(2,1)}, bf16[2,3,96,1024]{3,2,1,0:T(8,128)(2,1)}, u32[]{:S(2)}, u32[]{:S(2)}) collective-permute-start(bf16[2,3,96,1024]{3,2,1,0:T(8,128)(2,1)} %get-tuple-element.317), channel_id=1, source_target_pairs={{0,2},{2,0},{4,6},{6,4},{8,10},{10,8},{12,14},{14,12},{16,18},{18,... | collective-permute-start | bytes 3538952 | tf_op jit(solution)/shard_map/ppermute | solution.py:600
  311.7 37.5 %collective-permute-start.27 = (bf16[2,3,96,1024]{3,2,1,0:T(8,128)(2,1)}, bf16[2,3,96,1024]{3,2,1,0:T(8,128)(2,1)}, u32[]{:S(2)}, u32[]{:S(2)}) collective-permute-start(bf16[2,3,96,1024]{3,2,1,0:T(8,128)(2,1)} %get-tuple-element.318), channel_id=1, source_target_pairs={{0,4},{2,6},{4,0},{6,2},{8,12},{10,14},{12,8},{14,10},{16,20},{18,... | collective-permute-start | bytes 3538952 | tf_op jit(solution)/shard_map/ppermute | solution.py:600
  312.3 67.7 %collective-permute-start.28 = (bf16[2,3,96,1024]{3,2,1,0:T(8,128)(2,1)}, bf16[2,3,96,1024]{3,2,1,0:T(8,128)(2,1)}, u32[]{:S(2)}, u32[]{:S(2)}) collective-permute-start(bf16[2,3,96,1024]{3,2,1,0:T(8,128)(2,1)} %get-tuple-element.319), channel_id=1, source_target_pairs={{0,2},{2,0},{4,6},{6,4},{8,10},{10,8},{12,14},{14,12},{16,18},{18,... | collective-permute-start | bytes 3538952 | tf_op jit(solution)/shard_map/ppermute | solution.py:600
  313.8 68.0 %collective-permute-start.29 = (bf16[2,3,96,1024]{3,2,1,0:T(8,128)(2,1)}, bf16[2,3,96,1024]{3,2,1,0:T(8,128)(2,1)}, u32[]{:S(2)}, u32[]{:S(2)}) collective-permute-start(bf16[2,3,96,1024]{3,2,1,0:T(8,128)(2,1)} %get-tuple-element.320), channel_id=1, source_target_pairs={{0,4},{2,6},{4,0},{6,2},{8,12},{10,14},{12,8},{14,10},{16,20},{18,... | collective-permute-start | bytes 3538952 | tf_op jit(solution)/shard_map/ppermute | solution.py:600
  387.6 7.3 %collective-permute-start.30 = (bf16[3,192,1024]{2,1,0:T(8,128)(2,1)S(1)}, bf16[3,192,1024]{2,1,0:T(8,128)(2,1)S(1)}, u32[]{:S(2)}, u32[]{:S(2)}) collective-permute-start(bf16[3,192,1024]{2,1,0:T(8,128)(2,1)S(1)} %copy-done.12), channel_id=1, source_target_pairs={{0,1},{1,0},{2,3},{3,2},{4,5},{5,4},{6,7},{7,6},{8,9},{9,8},{10,11... | collective-permute-start | bytes 3538952 | tf_op jit(solution)/shard_map/ppermute | solution.py:709
  387.6 73.2 %collective-permute-start.24 = (bf16[1536,1024]{1,0:T(8,128)(2,1)}, bf16[1536,1024]{1,0:T(8,128)(2,1)}, u32[]{:S(2)}, u32[]{:S(2)}) collective-permute-start(bf16[1536,1024]{1,0:T(8,128)(2,1)} %get-tuple-element.311.own_ref), channel_id=1, source_target_pairs={{0,1},{1,0},{2,3},{3,2},{4,5},{5,4},{6,7},{7,6},{8,9},{9,8},{10,11... | collective-permute-start | bytes 9437192 | tf_op jit(solution)/shard_map/ppermute | solution.py:709
  390.4 35.9 %collective-permute-start.31 = (bf16[2,3,96,1024]{3,2,1,0:T(8,128)(2,1)}, bf16[2,3,96,1024]{3,2,1,0:T(8,128)(2,1)}, u32[]{:S(2)}, u32[]{:S(2)}) collective-permute-start(bf16[2,3,96,1024]{3,2,1,0:T(8,128)(2,1)} %add_convert_fusion.1), channel_id=1, source_target_pairs={{0,2},{2,0},{4,6},{6,4},{8,10},{10,8},{12,14},{14,12},{16,18},{18,... | collective-permute-start | bytes 3538952 | tf_op jit(solution)/shard_map/ppermute | solution.py:600
  390.4 35.9 %collective-permute-start.32 = (bf16[2,3,96,1024]{3,2,1,0:T(8,128)(2,1)}, bf16[2,3,96,1024]{3,2,1,0:T(8,128)(2,1)}, u32[]{:S(2)}, u32[]{:S(2)}) collective-permute-start(bf16[2,3,96,1024]{3,2,1,0:T(8,128)(2,1)} %add_convert_fusion), channel_id=1, source_target_pairs={{0,4},{2,6},{4,0},{6,2},{8,12},{10,14},{12,8},{14,10},{16,20},{18,... | collective-permute-start | bytes 3538952 | tf_op jit(solution)/shard_map/ppermute | solution.py:600
  451.7 24.6 %collective-permute-start.37 = (bf16[3,192,1024]{2,1,0:T(8,128)(2,1)}, bf16[3,192,1024]{2,1,0:T(8,128)(2,1)}, u32[]{:S(2)}, u32[]{:S(2)}) collective-permute-start(bf16[3,192,1024]{2,1,0:T(8,128)(2,1)} %get-tuple-element.354.qkv_ref), channel_id=1, source_target_pairs={{0,1},{1,0},{2,3},{3,2},{4,5},{5,4},{6,7},{7,6},{8,9},{9,8},{10,11... | collective-permute-start | bytes 3538952 | tf_op jit(solution)/shard_map/ppermute | solution.py:709
  467.8 12.1 %collective-permute-start.38 = (bf16[2,1,96,768]{3,2,1,0:T(8,128)(2,1)}, bf16[2,1,96,768]{3,2,1,0:T(8,128)(2,1)S(1)}, u32[]{:S(2)}, u32[]{:S(2)}) collective-permute-start(bf16[2,1,96,768]{3,2,1,0:T(8,128)(2,1)} %get-tuple-element.357), channel_id=1, source_target_pairs={{0,2},{2,0},{4,6},{6,4},{8,10},{10,8},{12,14},{14,12},{16,18},{18,... | collective-permute-start | bytes 884744 | tf_op jit(solution)/shard_map/ppermute | solution.py:600
  468.0 27.5 %collective-permute-start.39 = (bf16[2,1,96,768]{3,2,1,0:T(8,128)(2,1)}, bf16[2,1,96,768]{3,2,1,0:T(8,128)(2,1)}, u32[]{:S(2)}, u32[]{:S(2)}) collective-permute-start(bf16[2,1,96,768]{3,2,1,0:T(8,128)(2,1)} %get-tuple-element.358), channel_id=1, source_target_pairs={{0,4},{2,6},{4,0},{6,2},{8,12},{10,14},{12,8},{14,10},{16,20},{18,... | collective-permute-start | bytes 884744 | tf_op jit(solution)/shard_map/ppermute | solution.py:600
  469.7 26.8 %collective-permute-start.40 = (bf16[2,1,96,768]{3,2,1,0:T(8,128)(2,1)}, bf16[2,1,96,768]{3,2,1,0:T(8,128)(2,1)}, u32[]{:S(2)}, u32[]{:S(2)}) collective-permute-start(bf16[2,1,96,768]{3,2,1,0:T(8,128)(2,1)} %get-tuple-element.359), channel_id=1, source_target_pairs={{0,2},{2,0},{4,6},{6,4},{8,10},{10,8},{12,14},{14,12},{16,18},{18,... | collective-permute-start | bytes 884744 | tf_op jit(solution)/shard_map/ppermute | solution.py:600
  470.0 27.8 %collective-permute-start.41 = (bf16[2,1,96,768]{3,2,1,0:T(8,128)(2,1)}, bf16[2,1,96,768]{3,2,1,0:T(8,128)(2,1)}, u32[]{:S(2)}, u32[]{:S(2)}) collective-permute-start(bf16[2,1,96,768]{3,2,1,0:T(8,128)(2,1)} %get-tuple-element.360), channel_id=1, source_target_pairs={{0,4},{2,6},{4,0},{6,2},{8,12},{10,14},{12,8},{14,10},{16,20},{18,... | collective-permute-start | bytes 884744 | tf_op jit(solution)/shard_map/ppermute | solution.py:600
  476.4 24.6 %collective-permute-start.33 = (bf16[2,1,4,16,1536]{4,3,2,1,0:T(8,128)(2,1)}, bf16[2,1,4,16,1536]{4,3,2,1,0:T(8,128)(2,1)}, u32[]{:S(2)}, u32[]{:S(2)}) collective-permute-start(bf16[2,1,4,16,1536]{4,3,2,1,0:T(8,128)(2,1)} %get-tuple-element.349), channel_id=1, source_target_pairs={{0,2},{2,0},{4,6},{6,4},{8,10},{10,8},{12,14},{14,12},{16,18},{18,... | collective-permute-start | bytes 1179656 | tf_op jit(solution)/shard_map/ppermute | solution.py:600
  479.9 21.3 %collective-permute-start.34 = (bf16[2,1,4,16,1536]{4,3,2,1,0:T(8,128)(2,1)}, bf16[2,1,4,16,1536]{4,3,2,1,0:T(8,128)(2,1)}, u32[]{:S(2)}, u32[]{:S(2)}) collective-permute-start(bf16[2,1,4,16,1536]{4,3,2,1,0:T(8,128)(2,1)} %get-tuple-element.350), channel_id=1, source_target_pairs={{0,4},{2,6},{4,0},{6,2},{8,12},{10,14},{12,8},{14,10},{16,20},{18,... | collective-permute-start | bytes 1179656 | tf_op jit(solution)/shard_map/ppermute | solution.py:600
  495.6 10.2 %collective-permute-start.35 = (bf16[2,1,4,16,1536]{4,3,2,1,0:T(8,128)(2,1)}, bf16[2,1,4,16,1536]{4,3,2,1,0:T(8,128)(2,1)}, u32[]{:S(2)}, u32[]{:S(2)}) collective-permute-start(bf16[2,1,4,16,1536]{4,3,2,1,0:T(8,128)(2,1)} %get-tuple-element.351), channel_id=1, source_target_pairs={{0,2},{2,0},{4,6},{6,4},{8,10},{10,8},{12,14},{14,12},{16,18},{18,... | collective-permute-start | bytes 1179656 | tf_op jit(solution)/shard_map/ppermute | solution.py:600
  496.5 10.4 %collective-permute-start.36 = (bf16[2,1,4,16,1536]{4,3,2,1,0:T(8,128)(2,1)}, bf16[2,1,4,16,1536]{4,3,2,1,0:T(8,128)(2,1)}, u32[]{:S(2)}, u32[]{:S(2)}) collective-permute-start(bf16[2,1,4,16,1536]{4,3,2,1,0:T(8,128)(2,1)} %get-tuple-element.352), channel_id=1, source_target_pairs={{0,4},{2,6},{4,0},{6,2},{8,12},{10,14},{12,8},{14,10},{16,20},{18,... | collective-permute-start | bytes 1179656 | tf_op jit(solution)/shard_map/ppermute | solution.py:600
  497.8 15.6 %collective-permute-start.44 = (bf16[3,96,1024]{2,1,0:T(8,128)(2,1)}, bf16[3,96,1024]{2,1,0:T(8,128)(2,1)}, u32[]{:S(2)}, u32[]{:S(2)}) collective-permute-start(bf16[3,96,1024]{2,1,0:T(8,128)(2,1)} %fusion.24), channel_id=1, source_target_pairs={{0,24},{2,26},{4,28},{6,30},{8,0},{10,2},{12,4},{14,6},{16,8},{18,... | collective-permute-start | bytes 1769480 | tf_op jit(solution)/shard_map/ppermute | solution.py:596
  501.0 48.2 %collective-permute-start.45 = (bf16[3,96,1024]{2,1,0:T(8,128)(2,1)}, bf16[3,96,1024]{2,1,0:T(8,128)(2,1)}, u32[]{:S(2)}, u32[]{:S(2)}) collective-permute-start(bf16[3,96,1024]{2,1,0:T(8,128)(2,1)} %get-tuple-element.370), channel_id=1, source_target_pairs={{0,16},{2,18},{4,20},{6,22},{8,24},{10,26},{12,28},{14,30},{16,0},... | collective-permute-start | bytes 1769480 | tf_op jit(solution)/shard_map/ppermute | solution.py:596
  501.2 48.0 %collective-permute-start.46 = (bf16[3,96,1024]{2,1,0:T(8,128)(2,1)}, bf16[3,96,1024]{2,1,0:T(8,128)(2,1)}, u32[]{:S(2)}, u32[]{:S(2)}) collective-permute-start(bf16[3,96,1024]{2,1,0:T(8,128)(2,1)} %get-tuple-element.371), channel_id=1, source_target_pairs={{0,8},{2,10},{4,12},{6,14},{8,16},{10,18},{12,20},{14,22},{16,24},... | collective-permute-start | bytes 1769480 | tf_op jit(solution)/shard_map/ppermute | solution.py:596
  505.8 43.4 %collective-permute-start.42 = (bf16[2,1,96,768]{3,2,1,0:T(8,128)(2,1)S(1)}, bf16[2,1,96,768]{3,2,1,0:T(8,128)(2,1)}, u32[]{:S(2)}, u32[]{:S(2)}) collective-permute-start(bf16[2,1,96,768]{3,2,1,0:T(8,128)(2,1)S(1)} %add_convert_fusion.9), channel_id=1, source_target_pairs={{0,2},{2,0},{4,6},{6,4},{8,10},{10,8},{12,14},{14,12},{16,18},{18,... | collective-permute-start | bytes 884744 | tf_op jit(solution)/shard_map/ppermute | solution.py:600
  506.9 42.3 %collective-permute-start.43 = (bf16[2,1,96,768]{3,2,1,0:T(8,128)(2,1)}, bf16[2,1,96,768]{3,2,1,0:T(8,128)(2,1)}, u32[]{:S(2)}, u32[]{:S(2)}) collective-permute-start(bf16[2,1,96,768]{3,2,1,0:T(8,128)(2,1)} %add_convert_fusion.8), channel_id=1, source_target_pairs={{0,4},{2,6},{4,0},{6,2},{8,12},{10,14},{12,8},{14,10},{16,20},{18,... | collective-permute-start | bytes 884744 | tf_op jit(solution)/shard_map/ppermute | solution.py:600
  557.1 8.7 %collective-permute-start.47 = (bf16[2,1,4,16,1536]{4,3,2,1,0:T(8,128)(2,1)}, bf16[2,1,4,16,1536]{4,3,2,1,0:T(8,128)(2,1)}, u32[]{:S(2)}, u32[]{:S(2)}) collective-permute-start(bf16[2,1,4,16,1536]{4,3,2,1,0:T(8,128)(2,1)} %add_convert_fusion.7), channel_id=1, source_target_pairs={{0,2},{2,0},{4,6},{6,4},{8,10},{10,8},{12,14},{14,12},{16,18},{18,... | collective-permute-start | bytes 1179656 | tf_op jit(solution)/shard_map/ppermute | solution.py:600
  558.3 8.8 %collective-permute-start.48 = (bf16[2,1,4,16,1536]{4,3,2,1,0:T(8,128)(2,1)}, bf16[2,1,4,16,1536]{4,3,2,1,0:T(8,128)(2,1)S(1)}, u32[]{:S(2)}, u32[]{:S(2)}) collective-permute-start(bf16[2,1,4,16,1536]{4,3,2,1,0:T(8,128)(2,1)} %add_convert_fusion.6), channel_id=1, source_target_pairs={{0,4},{2,6},{4,0},{6,2},{8,12},{10,14},{12,8},{14,10},{16,20},{18,... | collective-permute-start | bytes 1179656 | tf_op jit(solution)/shard_map/ppermute | solution.py:600
  560.6 13.8 %collective-permute-start.49 = (bf16[1,96,768]{2,1,0:T(8,128)(2,1)}, bf16[1,96,768]{2,1,0:T(8,128)(2,1)S(1)}, u32[]{:S(2)}, u32[]{:S(2)}) collective-permute-start(bf16[1,96,768]{2,1,0:T(8,128)(2,1)} %get-tuple-element.399), channel_id=1, source_target_pairs={{0,24},{2,26},{4,28},{6,30},{8,0},{10,2},{12,4},{14,6},{16,8},{18,... | collective-permute-start | bytes 442376 | tf_op jit(solution)/shard_map/ppermute | solution.py:596
  560.6 18.2 %collective-permute-start.50 = (bf16[1,96,768]{2,1,0:T(8,128)(2,1)}, bf16[1,96,768]{2,1,0:T(8,128)(2,1)S(1)}, u32[]{:S(2)}, u32[]{:S(2)}) collective-permute-start(bf16[1,96,768]{2,1,0:T(8,128)(2,1)} %get-tuple-element.400), channel_id=1, source_target_pairs={{0,16},{2,18},{4,20},{6,22},{8,24},{10,26},{12,28},{14,30},{16,0},... | collective-permute-start | bytes 442376 | tf_op jit(solution)/shard_map/ppermute | solution.py:596
  563.0 15.8 %collective-permute-start.51 = (bf16[1,96,768]{2,1,0:T(8,128)(2,1)}, bf16[1,96,768]{2,1,0:T(8,128)(2,1)S(1)}, u32[]{:S(2)}, u32[]{:S(2)}) collective-permute-start(bf16[1,96,768]{2,1,0:T(8,128)(2,1)} %get-tuple-element.401), channel_id=1, source_target_pairs={{0,8},{2,10},{4,12},{6,14},{8,16},{10,18},{12,20},{14,22},{16,24},... | collective-permute-start | bytes 442376 | tf_op jit(solution)/shard_map/ppermute | solution.py:596
  569.6 10.5 %collective-permute-start.52 = (bf16[1,4,16,1536]{3,2,1,0:T(8,128)(2,1)S(1)}, bf16[1,4,16,1536]{3,2,1,0:T(8,128)(2,1)S(1)}, u32[]{:S(2)}, u32[]{:S(2)}) collective-permute-start(bf16[1,4,16,1536]{3,2,1,0:T(8,128)(2,1)S(1)} %get-tuple-element.406), channel_id=1, source_target_pairs={{0,24},{2,26},{4,28},{6,30},{8,0},{10,2},{12,4},{14,6},{16,8},{18,... | collective-permute-start | bytes 589832 | tf_op jit(solution)/shard_map/ppermute | solution.py:596
  569.7 23.4 %collective-permute-start.53 = (bf16[1,4,16,1536]{3,2,1,0:T(8,128)(2,1)S(1)}, bf16[1,4,16,1536]{3,2,1,0:T(8,128)(2,1)S(1)}, u32[]{:S(2)}, u32[]{:S(2)}) collective-permute-start(bf16[1,4,16,1536]{3,2,1,0:T(8,128)(2,1)S(1)} %get-tuple-element.407), channel_id=1, source_target_pairs={{0,16},{2,18},{4,20},{6,22},{8,24},{10,26},{12,28},{14,30},{16,0},... | collective-permute-start | bytes 589832 | tf_op jit(solution)/shard_map/ppermute | solution.py:596
  574.4 18.7 %collective-permute-start.54 = (bf16[1,4,16,1536]{3,2,1,0:T(8,128)(2,1)S(1)}, bf16[1,4,16,1536]{3,2,1,0:T(8,128)(2,1)S(1)}, u32[]{:S(2)}, u32[]{:S(2)}) collective-permute-start(bf16[1,4,16,1536]{3,2,1,0:T(8,128)(2,1)S(1)} %get-tuple-element.408), channel_id=1, source_target_pairs={{0,8},{2,10},{4,12},{6,14},{8,16},{10,18},{12,20},{14,22},{16,24},... | collective-permute-start | bytes 589832 | tf_op jit(solution)/shard_map/ppermute | solution.py:596
  600.2 3.8 collective-permute-start.56
  601.4 3.8 collective-permute-start.57
  602.4 4.7 collective-permute-start.58
  607.7 6.8 %collective-permute-start.59 = (f32[44,128]{1,0:T(8,128)}, f32[44,128]{1,0:T(8,128)}, u32[]{:S(2)}, u32[]{:S(2)}) collective-permute-start(f32[44,128]{1,0:T(8,128)} %add_add_fusion.1), channel_id=1, source_target_pairs={{0,16},{2,18},{4,20},{6,22},{8,24},{10,26},{12,28},{14,30},{16,0},... | collective-permute-start | bytes 67592 | tf_op jit(solution)/shard_map/ppermute | solution.py:596
  607.7 6.8 %collective-permute-start.60 = (f32[44,128]{1,0:T(8,128)}, f32[44,128]{1,0:T(8,128)}, u32[]{:S(2)}, u32[]{:S(2)}) collective-permute-start(f32[44,128]{1,0:T(8,128)} %add_add_fusion.1), channel_id=1, source_target_pairs={{0,8},{2,10},{4,12},{6,14},{8,16},{10,18},{12,20},{14,22},{16,24},... | collective-permute-start | bytes 67592 | tf_op jit(solution)/shard_map/ppermute | solution.py:596
  607.8 6.8 %collective-permute-start.61 = (f32[44,128]{1,0:T(8,128)}, f32[44,128]{1,0:T(8,128)}, u32[]{:S(2)}, u32[]{:S(2)}) collective-permute-start(f32[44,128]{1,0:T(8,128)} %add_add_fusion.1), channel_id=1, source_target_pairs={{0,24},{2,26},{4,28},{6,30},{8,0},{10,2},{12,4},{14,6},{16,8},{18,... | collective-permute-start | bytes 67592 | tf_op jit(solution)/shard_map/ppermute | solution.py:596
  (78 other events, 745.4 us)
Sparse Core Ops, SparseCore 0:
  11.4 160.6 all-gather.6
  174.9 100.2 all-gather.4
  308.6 160.9 reduce-scatter.1

commit v2 on v1

--- a/solution.py
+++ b/solution.py
@@ -552,11 +552,7 @@
     scaled = up * gain_ref[...]
     along = jnp.sum(values * scaled, axis=0, keepdims=True) * (inv_root * inv_root * (1.0 / D))
     total = base_ref[...].astype(F32) + inv_root * (scaled - values * along)
-    if squeeze:
-        outs[0][...] = squeeze_rows(total, *squeeze)
-    else:
-        outs[0][...] = total
-        outs[2][...] = total.astype(BF)
+    outs[0][...] = squeeze_rows(total, *squeeze) if squeeze else total.astype(BF)
     gain_part = jnp.sum(up * (values * inv_root), axis=1, keepdims=True)
 
     @pl.when(pl.program_id(0) == 0)
@@ -584,9 +580,8 @@
         grid=(tokens // QB,),
         in_specs=[part, pl.BlockSpec((1, QB), lambda j: (0, j)), column, part]
         + [spec(a, w) for a, w in zip(ups, fixed)],
-        out_specs=[pl.BlockSpec((height, QB), lambda j: (0, j)), column] + ([] if squeeze else [part]),
-        out_shape=[shape_of(height, tokens, dtype=F32), shape_of(rows, 1, dtype=F32)]
-        + ([] if squeeze else [shape_of(rows, tokens)]),
+        out_specs=[pl.BlockSpec((height, QB), lambda j: (0, j)), column],
+        out_shape=[shape_of(height, tokens, dtype=F32 if squeeze else BF), shape_of(rows, 1, dtype=F32)],
         compiler_params=pltpu.CompilerParams(vmem_limit_bytes=VMEM),
         cost_estimate=pl.CostEstimate(flops=flops + 12 * rows * tokens, bytes_accessed=20 * rows * tokens, transcendentals=0),
     )(values, inv_root, gain, base, *ups)
@@ -662,13 +657,17 @@
     return sum(term.astype(F32) for term in terms).astype(BF)
 
 
-def scatter_steps(blocks):
+def scatter_steps(blocks, wide=False):
     if len(blocks) == 1:
         return lax.psum_scatter(blocks[0], "tok", scatter_dimension=0, tiled=False).astype(F32)
     m_low, m_high, x_low, x_high, y_low, y_high, d_low, d_high = blocks
-    to_y, to_x, x_first, y_second = yield [
-        (d_low, flipped, (1,)), (d_high, flipped, (2,)), (x_low, flipped, (1,)), (y_high, flipped, (2,))
-    ]
+    if wide:
+        to_y, to_x = yield [(d_low, flipped, (1,)), (d_high, flipped, (2,))]
+        x_first, y_second = yield [(x_low, flipped, (1,)), (y_high, flipped, (2,))]
+    else:
+        to_y, to_x, x_first, y_second = yield [
+            (d_low, flipped, (1,)), (d_high, flipped, (2,)), (x_low, flipped, (1,)), (y_high, flipped, (2,))
+        ]
     x_second, y_first = yield [
         (low_sum(x_high, to_x), flipped, (1,)), (low_sum(y_low, to_y), flipped, (2,))
     ]
@@ -717,7 +716,7 @@
 def chunk_sizes(width):
     if lax.axis_size("tok") != 16:
         return [FC] * (width // FC)
-    return [4 * FC, width - 4 * FC]
+    return [5 * FC, width - 5 * FC]
 
 
 def shards(
@@ -780,13 +779,11 @@
         start += size
     cross_wire = jnp.pad(widen(cross_weights.astype(BF), 2), ((0, 0), (0, share_pad - share), (0, 0)))[None]
     cross_w = Transfer(gather_steps(cross_wire))
-    ffn_wire = tick(ffn_wire, cross_w)
 
     x_low = spread_rows(inputs.T, block, pad)
+    x_low = tick(x_low, self_w, cross_w)
     resid_zero = x_low.astype(F32)
     inv_one = norm_stats(resid_zero)
-    x_low, inv_one = tick((x_low, inv_one), self_w)
-    resid_zero = x_low.astype(F32)
     og_low = spread_rows(out_grad.T, block, pad)
     og_low, inv_one = tick((og_low, inv_one), self_w, cross_w)
     mem_own = spread_rows(memory.reshape(enc, D).T, block, pad)
@@ -803,7 +800,8 @@
 
     self_blocks = place_blocks(owners, self_w.finish())
     gain_blocks = self_blocks[:, block : block + 3, :block]
-    gains = widen(jnp.transpose(gain_blocks, (1, 0, 2)).reshape(3, -1), 1).reshape(3, rows, 1).astype(F32)
+    gain_rows = widen(jnp.transpose(gain_blocks, (1, 0, 2)).reshape(3, -1), 1).astype(F32)
+    gains = lax.optimization_barrier([gain_rows[c].reshape(rows, 1) for c in range(3)])
     self_own = self_blocks.reshape(rows, 4 * own)
     self_low, self_high = core_pair(self_own, mem_index)
     normed_one = (resid_zero * inv_one * gains[0]).astype(BF)
@@ -842,34 +840,32 @@
     ffn_g = []
     for i, weights in enumerate(ffn_w):
         last = i == len(ffn_w) - 1
-        sums, grads = feed_forward(owners, normed_three, og_low, weights, sums, not last, last)
-        ffn_g.append(Transfer(scatter_steps(grads)))
+        sums, grads = feed_forward(owners, normed_three, og_low, weights, sums, last and count == 16, last)
+        ffn_g.append(Transfer(scatter_steps(grads, True)))
         if not last:
             sums = tick(sums, ffn_g[i])
     out_low, back_low = sums
     back_other = other_core(back_low)
-    back_low, back_other = tick((back_low, back_other), *ffn_g[1:])
-    grad_two, gain_three, grad_two_low = norm_back(
+    back_low, back_other = tick((back_low, back_other), ffn_g[-1])
+    grad_two_low, gain_three = norm_back(
         resid_two, inv_three, gains[2], og_low,
         lambda own, other: own[...].astype(F32) + other[...].astype(F32), (back_low, back_other), (False, False),
     )
 
+    grad_two_low = tick(grad_two_low, ffn_g[-1])
     grad_cattn = dot_nn(cross_own[3], grad_two_low).astype(BF)
     (cross_d,) = cross_backward(query, keyval, grad_cattn, lse_cross, keep, heads)
-    cross_d = tick(cross_d, ffn_g[0])
+    cross_d = tick(cross_d, ffn_g[-1])
     cross_d_other = other_core(cross_d)
     grad_q_full = jnp.concatenate(
         [jnp.where(mem_index == 0, cross_d[0], cross_d_other[0]), jnp.where(mem_index == 0, cross_d_other[0], cross_d[0])]
     )
-    grad_one, gain_two, grad_one_low = norm_back(
-        resid_one, inv_two, gains[1], grad_two,
+    grad_one_low, gain_two = norm_back(
+        resid_one, inv_two, gains[1], grad_two_low,
         lambda w, g: dot_tn(w[...], g[...]), (cross_full[0], grad_q_full), (True, False), flops=2 * INNER * rows * LEN,
     )
 
-    grad_sattn = dot_tn(self_own[:, 3 * own :], grad_one_low).astype(BF)
-    grad_qkv, diag = self_backward(qkv, grad_sattn, lse_self, seg_row, seg_col, vec, heads)
-    self_g = Transfer(scatter_steps(self_weight_grads(owners, normed_one, grad_qkv, grad_one_low, attn_self)))
-    grad_qkv = tick(grad_qkv, self_g, ffn_g[0])
+    grad_one_low, cross_d, cross_d_other = tick((grad_one_low, cross_d, cross_d_other), ffn_g[-1])
     other_half = lax.dynamic_slice_in_dim(own_map, (1 - mem_index) * own, own, 0)
     own_half = lax.dynamic_slice_in_dim(own_map, mem_index * own, own, 0)
     cross_g = Transfer(
@@ -880,31 +876,39 @@
             )
         )
     )
+    grad_sattn = dot_tn(self_own[:, 3 * own :], grad_one_low).astype(BF)
+    grad_sattn = tick(grad_sattn, ffn_g[-1], cross_g)
+
+    grad_qkv, diag = self_backward(qkv, grad_sattn, lse_self, seg_row, seg_col, vec, heads)
     grad_qkv = tick(grad_qkv, cross_g)
-
-    grad_other = other_core(grad_qkv)
+    self_g = Transfer(scatter_steps(self_weight_grads(owners, normed_one, grad_qkv, grad_one_low, attn_self)))
+    grad_qkv, grad_other, out_low = tick((grad_qkv, other_core(grad_qkv), out_low), cross_g, self_g)
+
     qkv_low = jnp.where(mem_index == 0, grad_qkv, grad_other).reshape(3 * own, LEN)
     qkv_high = jnp.where(mem_index == 0, grad_other, grad_qkv).reshape(3 * own, LEN)
     input_grad, gain_one = norm_back(
-        x_low, inv_one, gains[0], grad_one,
+        x_low, inv_one, gains[0], grad_one_low,
         lambda a, b, c, d: dot_nn(a[:, : 3 * own], c[...]) + dot_nn(b[:, : 3 * own], d[...]),
         (self_low, self_high, qkv_low, qkv_high), (True, True, False, False), (block, pad), 12 * own * rows * LEN,
     )
-    input_grad, gain_one = tick((input_grad.T, gain_one), self_g)
+    input_grad, gain_one, out_low, cross_d, cross_d_other, diag = tick(
+        (input_grad.T, gain_one, out_low, cross_d, cross_d_other, diag), self_g
+    )
+    out_other = other_core(out_low)
     kv_own = lax.dynamic_slice_in_dim(cross_d[1:], mem_index * enc, enc, 2)
     kv_other = lax.dynamic_slice_in_dim(cross_d_other[1:], mem_index * enc, enc, 2)
     kv_all = jnp.concatenate(
         [jnp.where(mem_index == 0, kv_own, kv_other), jnp.where(mem_index == 0, kv_other, kv_own)], axis=1
     ).reshape(2 * INNER, enc)
     memory_grad = narrow(dot_tn(cross_full[1:3].reshape(2 * INNER, rows), kv_all), 0).T.reshape(1, enc, D)
-    memory_grad = tick(memory_grad, cross_g, self_g, ffn_g[0])
-    layer_out = layer_output(resid_two, out_low, other_core(out_low), block, pad).T
+    memory_grad, out_low, out_other, diag = tick((memory_grad, out_low, out_other, diag), cross_g, self_g)
+    layer_out = layer_output(resid_two, out_low, out_other, block, pad).T
     spread = jnp.zeros((heads, QB + LEN), F32)
     diag = diag[:, :, ::-1]
     for d in range(diag.shape[1]):
         spread = spread.at[:, d * QB : d * QB + 2 * QB].add(diag[:, d])
     rel_grad = jnp.dot(spread[:, QB:], bucket_hot.T, precision=lax.Precision.HIGHEST)
-    layer_out = tick(layer_out, cross_g)
+    layer_out, rel_grad = tick((layer_out, rel_grad), self_g, cross_g)
     ffn_sum = jnp.concatenate([t.finish() for t in ffn_g], axis=2)
     cross_sum = cross_g.finish()[0, :, :share]
     self_sum = self_g.finish()[0, :block]
@@ -915,17 +919,20 @@
     local_squares = (
         jnp.sum(jnp.square(self_sum)) + jnp.sum(jnp.square(ffn_sum)) + jnp.sum(jnp.square(cross_sum))
     )
-    gain_rows = 3 * rows // 128
+    self_grads, ffn_grads, cross_grads, local_squares = lax.optimization_barrier(
+        (self_grads, ffn_grads, cross_grads, local_squares)
+    )
+    gain_lines = 3 * rows // 128
     gain_grad = jnp.where(mem_index == 0, jnp.concatenate([gain_one, gain_two, gain_three], axis=1).T, 0.0)
     rel_padded = lax.dynamic_update_slice_in_dim(
         jnp.zeros((8, 128), F32), jnp.pad(rel_grad, ((0, 0), (0, 128 - NB))), mem_index * heads, 0
     )
     totals = sum_all(
-        jnp.concatenate([gain_grad.reshape(gain_rows, 128), rel_padded.at[H, 0].set(local_squares)])
-    )
-    gains_total, rel_total = totals[:gain_rows].reshape(3, rows), totals[gain_rows : gain_rows + H, :NB]
+        jnp.concatenate([gain_grad.reshape(gain_lines, 128), rel_padded.at[H, 0].set(local_squares)])
+    )
+    gains_total, rel_total = totals[:gain_lines].reshape(3, rows), totals[gain_lines : gain_lines + H, :NB]
     gains_sum = lax.dynamic_slice_in_dim(gains_total, lax.axis_index("tok") * pad, pad, 1)[:, :block]
-    total_squares = totals[gain_rows + H, 0] + jnp.sum(gains_total * gains_total)
+    total_squares = totals[gain_lines + H, 0] + jnp.sum(gains_total * gains_total)
     grad_norm = jnp.sqrt(total_squares + jnp.sum(rel_total * rel_total))
     rel_g = lax.dynamic_slice_in_dim(rel_total, mem_index * heads, heads, 0)
     clip_scale = CLIP_NORM / jnp.maximum(grad_norm, CLIP_NORM)

time: 655 us -> 593 us (0.905)
  waiting for transfers between devices: 187 us -> 148 us
  other arithmetic: 80.7 us -> 62.1 us
  local copies, waits for them, and re-layouts: 50 us -> 40.7 us
  starting transfers between devices: 66.7 us -> 75.2 us
    ppermute x18, waiting for transfers between devices: 58.9 us -> 28.4 us  [rotated(): lax.ppermute(value, 'tok', [(t, (t // 4 + step) % 4 * 4 + t % 4) for t in...]
    convert_element_type x10, other arithmetic: 21.5 us -> 12.2 us  [low_sum(): return sum((term.astype(F32) for term in terms)).astype(BF)]
    ppermute x33, waiting for transfers between devices: 99.4 us -> 92.1 us  [flipped(): return lax.ppermute(value, 'tok', [(t, t ^ bits) for t in range(16)])]
    all_gather x2, waiting for transfers between devices: 24.1 us -> 17.1 us  [shards(): lax.all_gather(ffn_wire[:, :, start:start + size], 'tok', axis=0, tiled=F...]
  transfers between devices with their start and end apart: 65 -> 65, of which waited for: 29 -> 33; matrix products, arithmetic and copies ran while one was open for 18% -> 17% of each run, Pallas kernels for 29% -> 36%
where the time goes in v2:
time: 593 us; the launch traced here: 585 us
  Pallas kernels  213 us (36%)
  waiting for transfers between devices  148 us (25%)
  starting transfers between devices  75.2 us (13%)
  other arithmetic  62.1 us (10%)
  local copies, waits for them, and re-layouts  40.7 us (7%)
  matrix products  25.5 us (4%)
  between operations  20.5 us (3%)
    ppermute x33, waiting for transfers between devices, flipped(): return lax.ppermute(value, 'tok', [(t, t ^ bits) for t in range(16)])  92.1 us
    pallas_call x2, Pallas kernels, feed_forward(): pl.pallas_call(functools.partial(ffn_kernel, len(sizes), first, last), in...  74.7 us
    pallas_call x4, Pallas kernels, attn_call(): pl.pallas_call(kernel, grid=(heads,), in_specs=in_specs, out_specs=out_sp...  49.1 us
    ppermute x33, starting transfers between devices, flipped(): return lax.ppermute(value, 'tok', [(t, t ^ bits) for t in range(16)])  38.8 us
    pallas_call x3, Pallas kernels, norm_back(): pl.pallas_call(functools.partial(norm_back_kernel, upstream, squeeze, len...  34.8 us
    ppermute x18, starting transfers between devices, rotated(): lax.ppermute(value, 'tok', [(t, (t // 4 + step) % 4 * 4 + t % 4) for t in...  34.6 us
    ppermute x18, waiting for transfers between devices, rotated(): lax.ppermute(value, 'tok', [(t, (t // 4 + step) % 4 * 4 + t % 4) for t in...  28.4 us
    all_gather x2, waiting for transfers between devices, shards(): lax.all_gather(ffn_wire[:, :, start:start + size], 'tok', axis=0, tiled=F...  17.1 us
  transfers between devices with their start and end apart: 65, of which 33 were waited for; matrix products, arithmetic and copies ran while one was open for 17% of the time, Pallas kernels for 36%

profile of v2, /device:TPU:0, one launch (start us, length us, event | category | flops | bytes accessed | tf_op | source)
XLA Modules:
  0.0 584.8 jit_solution(10714346285388691205)
XLA Ops:
  11.6 3.1 collective-permute-start
  14.7 2.6 collective-permute-start.1
  18.7 2.4 shard_map.350
  24.6 4.4 shard_map.348.refs_0_
  28.9 4.5 shard_map.349.refs_2_.refs_3_
  35.0 4.6 collective-permute-start.7
  39.5 3.5 collective-permute-start.8
  45.4 5.5 collective-permute-done.7
  52.4 6.3 %collective-permute-done.8 = bf16[1,4,16,1536]{3,2,1,0:T(8,128)(2,1)S(1)} collective-permute-done((bf16[1,4,16,1536]{3,2,1,0:T(8,128)(2,1)}, bf16[1,4,16,1536]{3,2,1,0:T(8,128)(2,1)S(1)}, u32[]{:S(2)}, u32[]{:S(2)}) %collective-permute-start.8) | collective-permute-done | bytes 196640 | tf_op jit(solution)/shard_map/ppermute | solution.py:591
  62.1 12.2 %collective-permute-done.5.refs_4_ = bf16[2,1,96,768]{3,2,1,0:T(8,128)(2,1)S(1)} collective-permute-done((bf16[2,1,96,768]{3,2,1,0:T(8,128)(2,1)S(1)}, bf16[2,1,96,768]{3,2,1,0:T(8,128)(2,1)S(1)}, u32[]{:S(2)}, u32[]{:S(2)}) %collective-permute-start.5) | collective-permute-done | bytes 294944 | tf_op jit(solution)/shard_map/ppermute | solution.py:595
  74.3 9.8 %collective-permute-done.6.refs_5_ = bf16[2,1,96,768]{3,2,1,0:T(8,128)(2,1)S(1)} collective-permute-done((bf16[2,1,96,768]{3,2,1,0:T(8,128)(2,1)S(1)}, bf16[2,1,96,768]{3,2,1,0:T(8,128)(2,1)S(1)}, u32[]{:S(2)}, u32[]{:S(2)}) %collective-permute-start.6) | collective-permute-done | bytes 294944 | tf_op jit(solution)/shard_map/ppermute | solution.py:595
  95.1 3.9 shard_map.351
  109.2 3.0 fusion.12.q_ref.k_ref.v_ref
  112.2 3.8 collective-permute-done.15.refs_2_
  116.1 16.4 %collective-permute-done.16.refs_3_ = bf16[2,1,4,16,1536]{4,3,2,1,0:T(8,128)(2,1)} collective-permute-done((bf16[2,1,4,16,1536]{4,3,2,1,0:T(8,128)(2,1)S(1)}, bf16[2,1,4,16,1536]{4,3,2,1,0:T(8,128)(2,1)}, u32[]{:S(2)}, u32[]{:S(2)}) %collective-permute-start.16) | collective-permute-done | bytes 393248 | tf_op jit(solution)/shard_map/ppermute | solution.py:595
  132.5 4.3 collective-permute-done.18.refs_5_
  137.1 2.6 collective-permute-start.20
  143.4 8.1 %shard_map.352 = (bf16[192,1024]{1,0:T(8,128)(2,1)}, f32[3,1,1024]{2,1,0:T(1,128)}) custom-call(bf16[576,1024]{1,0:T(8,128)(2,1)} %fusion.12.q_ref.k_ref.v_ref, bf16[576,1024]{1,0:T(8,128)(2,1)} %fusion.12.q_ref.k_ref.v_ref, bf16[576,1024]{1,0:T(8,128)(2,1)} %fusion.12.q_ref.k_ref.v_ref, s32[1,1024]{1,0:T(1,128)} %bitcast.193, s32[1024,1]{1,0:T(8,128)} %copy.75.segc_ref, ...), custom_call_target="tpu_custom_call" | custom-call | flops 805306368 | bytes 4194304 | tf_op jit(solution)/shard_map/pallas_call | solution.py:164
  151.4 4.6 collective-permute-done.19.refs_6_
  157.0 4.5 shard_map.353
  163.7 2.7 broadcast_select_fusion.1
  170.9 2.1 copy-done.1
  173.0 8.1 %shard_map.354 = bf16[4,384,1536]{2,1,0:T(8,128)(2,1)} custom-call(bf16[384,256]{1,0:T(8,128)(2,1)} %get-tuple-element.544.own_map, bf16[384,256]{1,0:T(8,128)(2,1)} %get-tuple-element.543.other_map, bf16[16,4,16,1536]{3,2,1,0:T(8,128)(2,1)} %bitcast.163, bf16[16,4,16,1536]{3,2,1,0:T(8,128)(2,1)} %collective-permute-done.22.other_ref), custom_call_target="tpu_custom_call" | custom-call | flops 2415919104 | bytes 12582912 | tf_op jit(solution)/shard_map/pallas_call | solution.py:426
  182.4 2.8 convolution_convert_fusion.3.q_ref
  185.2 2.3 convolution_convert_fusion.k_ref.v_ref
  187.5 12.5 %shard_map.355 = (bf16[192,1024]{1,0:T(8,128)(2,1)}, f32[3,1,1024]{2,1,0:T(1,128)}) custom-call(bf16[192,1024]{1,0:T(8,128)(2,1)} %convolution_convert_fusion.3.q_ref, bf16[384,1024]{1,0:T(8,128)(2,1)} %convolution_convert_fusion.k_ref.v_ref, bf16[384,1024]{1,0:T(8,128)(2,1)} %convolution_convert_fusion.k_ref.v_ref, f32[1024,1]{1,0:T(8,128)} %broadcast_select_fusion.10.keep_ref), custom_call_target="tpu_custom_call" | custom-call | flops 805306368 | bytes 4194304 | tf_op jit(solution)/shard_map/pallas_call | solution.py:164
  203.2 5.2 multiply_reduce_fusion
  208.4 2.7 copy-done
  211.1 2.3 multiply_convert_fusion.refs_1_
  213.4 50.4 %shard_map.356 = (f32[1536,1024]{1,0:T(8,128)}, f32[1536,1024]{1,0:T(8,128)}, bf16[16,3,96,1280]{3,2,1,0:T(8,128)(2,1)}) custom-call(s32[16]{0:T(128)} %stack.102.owners_ref.refs_0_, bf16[1536,1024]{1,0:T(8,128)(2,1)} %multiply_convert_fusion.refs_1_, bf16[1536,1024]{1,0:T(8,128)(2,1)} %shard_map.349.refs_2_.refs_3_, bf16[16,3,96,1280]{3,2,1,0:T(8,128)(2,1)} %bitcast.197), custom_call_target="tpu_custom_call" | custom-call | flops 36238786560 | bytes 33554432 | tf_op jit(solution)/shard_map/pallas_call | solution.py:344
  263.8 17.1 %all-gather.5.cloned.1.call-done = bf16[48,96,512]{2,1,0:T(8,128)(2,1)} async-done(((bf16[3,96,512]{2,1,0:T(8,128)(2,1)}), bf16[48,96,512]{2,1,0:T(8,128)(2,1)}) %all-gather.5.cloned.1.call-update) | async-done | bytes 4718608 | tf_op jit(solution)/shard_map/all_gather | solution.py:778
  281.0 24.3 %shard_map.357 = (bf16[1536,1024]{1,0:T(8,128)(2,1)}, bf16[1536,1024]{1,0:T(8,128)(2,1)}, bf16[2,3,96,512]{3,2,1,0:T(8,128)(2,1)}, bf16[2,3,96,512]{3,2,1,0:T(8,...) custom-call(s32[16]{0:T(128)} %stack.102.owners_ref.refs_0_, ...), custom_call_target="tpu_custom_call" | custom-call | flops 14495514624 | bytes 33554432 | tf_op jit(solution)/shard_map/pallas_call | solution.py:344
  305.4 5.9 %collective-permute-done.24.refs_5_ = bf16[1536,1024]{1,0:T(8,128)(2,1)S(1)} collective-permute-done((bf16[1536,1024]{1,0:T(8,128)(2,1)}, bf16[1536,1024]{1,0:T(8,128)(2,1)S(1)}, u32[]{:S(2)}, u32[]{:S(2)}) %collective-permute-start.24) | collective-permute-done | bytes 3145760 | tf_op jit(solution)/shard_map/ppermute | solution.py:708
  314.5 10.6 %shard_map.358 = (bf16[1536,1024]{1,0:T(8,128)(2,1)}, f32[1536,1]{1,0:T(8,128)}) custom-call(f32[1536,1024]{1,0:T(8,128)} %copy-done, f32[1,1024]{1,0:T(1,128)} %bitcast.188, f32[1536,1]{1,0:T(8,128)} %copy.77.refs_2_, bf16[1536,1024]{1,0:T(8,128)(2,1)} %shard_map.349.refs_2_.refs_3_, bf16[1536,1024]{1,0:T(8,128)(2,1)} %get-tuple-element.351.refs_4_, ...), custom_call_target="tpu_custom_call" | custom-call | flops 18874368 | bytes 31457280 | tf_op jit(solution)/shard_map/pallas_call | solution.py:578
  325.1 6.2 %collective-permute-done.25 = bf16[2,3,96,512]{3,2,1,0:T(8,128)(2,1)} collective-permute-done((bf16[2,3,96,512]{3,2,1,0:T(8,128)(2,1)}, bf16[2,3,96,512]{3,2,1,0:T(8,128)(2,1)}, u32[]{:S(2)}, u32[]{:S(2)}) %collective-permute-start.25) | collective-permute-done | bytes 589856 | tf_op jit(solution)/shard_map/ppermute | solution.py:595
  333.7 3.6 convolution_convert_fusion.2.do_ref
  337.4 14.8 %shard_map.359.own_ref = bf16[3,192,1024]{2,1,0:T(8,128)(2,1)} custom-call(bf16[192,1024]{1,0:T(8,128)(2,1)} %convolution_convert_fusion.3.q_ref, bf16[384,1024]{1,0:T(8,128)(2,1)} %convolution_convert_fusion.k_ref.v_ref, bf16[384,1024]{1,0:T(8,128)(2,1)} %convolution_convert_fusion.k_ref.v_ref, bf16[192,1024]{1,0:T(8,128)(2,1)} %convolution_convert_fusion.2.do_ref, ...), custom_call_target="tpu_custom_call" | custom-call | flops 2013265920 | bytes 4194304 | tf_op jit(solution)/shard_map/pallas_call | solution.py:164
  352.2 2.2 add_convert_fusion
  360.5 2.4 slice_bitcast_fusion.refs_4_
  364.1 10.6 %shard_map.360 = (bf16[1536,1024]{1,0:T(8,128)(2,1)}, f32[1536,1]{1,0:T(8,128)}) custom-call(f32[1536,1024]{1,0:T(8,128)} %copy-done.1, f32[1,1024]{1,0:T(1,128)} %bitcast.187, f32[1536,1]{1,0:T(8,128)} %copy.78.refs_2_, bf16[1536,1024]{1,0:T(8,128)(2,1)} %get-tuple-element.359.refs_3_.g_ref, bf16[384,1536]{1,0:T(8,128)(2,1)} %slice_bitcast_fusion.refs_4_, ...), custom_call_target="tpu_custom_call" | custom-call | flops 1226833920 | bytes 31457280 | tf_op jit(solution)/shard_map/pallas_call | solution.py:578
  374.7 7.8 %collective-permute-done.30 = bf16[2,3,96,512]{3,2,1,0:T(8,128)(2,1)} collective-permute-done((bf16[2,3,96,512]{3,2,1,0:T(8,128)(2,1)}, bf16[2,3,96,512]{3,2,1,0:T(8,128)(2,1)}, u32[]{:S(2)}, u32[]{:S(2)}) %collective-permute-start.30) | collective-permute-done | bytes 589856 | tf_op jit(solution)/shard_map/ppermute | solution.py:595
  388.5 2.8 convolution_convert_fusion.1.do_ref
  391.4 11.2 %shard_map.361 = (bf16[2,1,4,16,1536]{4,3,2,1,0:T(8,128)(2,1)}, bf16[2,1,4,16,1536]{4,3,2,1,0:T(8,128)(2,1)}, bf16[2,1,4,16,1536]{4,3,2,1,0:T(8,128)(2,1)}, bf16...) custom-call(s32[16]{0:T(128)} %stack.102.owners_ref.refs_0_, ...), custom_call_target="tpu_custom_call" | custom-call | flops 3221225472 | bytes 16777216 | tf_op jit(solution)/shard_map/pallas_call | solution.py:457
  402.6 9.9 %collective-permute-done.33 = bf16[3,96,512]{2,1,0:T(8,128)(2,1)S(1)} collective-permute-done((bf16[3,96,512]{2,1,0:T(8,128)(2,1)S(1)}, bf16[3,96,512]{2,1,0:T(8,128)(2,1)S(1)}, u32[]{:S(2)}, u32[]{:S(2)}) %collective-permute-start.33) | collective-permute-done | bytes 294944 | tf_op jit(solution)/shard_map/ppermute | solution.py:591
  412.5 2.7 collective-permute-start.35
  417.3 13.7 %shard_map.362 = (bf16[3,192,1024]{2,1,0:T(8,128)(2,1)}, f32[3,3,512]{2,1,0:T(4,128)}) custom-call(bf16[576,1024]{1,0:T(8,128)(2,1)} %fusion.12.q_ref.k_ref.v_ref, bf16[576,1024]{1,0:T(8,128)(2,1)} %fusion.12.q_ref.k_ref.v_ref, bf16[576,1024]{1,0:T(8,128)(2,1)} %fusion.12.q_ref.k_ref.v_ref, bf16[192,1024]{1,0:T(8,128)(2,1)} %convolution_convert_fusion.1.do_ref, ...), custom_call_target="tpu_custom_call" | custom-call | flops 2013265920 | bytes 4194304 | tf_op jit(solution)/shard_map/pallas_call | solution.py:164
  431.1 2.3 collective-permute-done.35
  433.3 2.4 collective-permute-done.36
  435.7 6.7 %collective-permute-done.37 = bf16[2,1,4,16,1536]{4,3,2,1,0:T(8,128)(2,1)S(1)} collective-permute-done((bf16[2,1,4,16,1536]{4,3,2,1,0:T(8,128)(2,1)}, bf16[2,1,4,16,1536]{4,3,2,1,0:T(8,128)(2,1)S(1)}, u32[]{:S(2)}, u32[]{:S(2)}) %collective-permute-start.37) | collective-permute-done | bytes 393248 | tf_op jit(solution)/shard_map/ppermute | solution.py:595
  448.9 8.4 %shard_map.363 = (bf16[2,1,96,768]{3,2,1,0:T(8,128)(2,1)}, bf16[2,1,96,768]{3,2,1,0:T(8,128)(2,1)}, bf16[2,1,96,768]{3,2,1,0:T(8,128)(2,1)}, bf16[2,1,96,768]{3,...) custom-call(s32[16]{0:T(128)} %stack.102.owners_ref.refs_0_, ...), custom_call_target="tpu_custom_call" | custom-call | flops 2415919104 | bytes 12582912 | tf_op jit(solution)/shard_map/pallas_call | solution.py:488
  457.4 5.6 collective-permute-done.41
  466.9 2.4 collective-permute-start.42
  473.0 13.6 %shard_map.364 = (f32[1472,1024]{1,0:T(8,128)}, f32[1536,1]{1,0:T(8,128)}) custom-call(bf16[1536,1024]{1,0:T(8,128)(2,1)} %shard_map.348.refs_0_, f32[1,1024]{1,0:T(1,128)} %bitcast.189, f32[1536,1]{1,0:T(8,128)} %copy.80.refs_2_, bf16[1536,1024]{1,0:T(8,128)(2,1)} %get-tuple-element.381.g_ref.refs_3_, bf16[1536,768]{1,0:T(8,128)(2,1)} %copy-done.5, ...), custom_call_target="tpu_custom_call" | custom-call | flops 3642753024 | bytes 31457280 | tf_op jit(solution)/shard_map/pallas_call | solution.py:578
  491.8 2.4 copy.76
  497.8 5.8 collective-permute-start.48
  503.6 2.2 collective-permute-start.49
  510.1 3.1 fusion.3
  513.2 4.2 reshape.963
  517.4 4.6 collective-permute-done.48
  528.8 6.8 %shard_map.365 = bf16[1472,1024]{1,0:T(8,128)(2,1)} custom-call(f32[1536,1024]{1,0:T(8,128)} %copy-done, bf16[1536,1024]{1,0:T(8,128)(2,1)} %get-tuple-element.460.own_ref, bf16[1536,1024]{1,0:T(8,128)(2,1)} %collective-permute-done.46.other_ref), custom_call_target="tpu_custom_call" | custom-call | flops 6291456 | bytes 15728640 | tf_op jit(solution)/shard_map/pallas_call | solution.py:535
  550.3 2.6 collective-permute-done.58
  553.0 3.4 collective-permute-start.59
  556.3 3.8 collective-permute-start.61
  566.5 6.7 %multiply_subtract_fusion = (f32[3,1792,92]{1,2,0:T(8,128)}, f32[3,1792,92]{1,2,0:T(8,128)}, f32[3,1792,92]{1,2,0:T(8,128)}) fusion(f32[3,1792,92]{1,2,0:T(8,128)S(1)} %copy-done.8, f32[3,1792,92]{1,2,0:T(8,128)} %fusion.6, f32[]{:T(128)S(6)} %div.145, f32[3,1792,92]{1,2,0:T(8,128)} %param.44, f32[3,1792,92]{1,2,0:T(8,128)} %param.45), kind=kLoop, calls=%fused_computation.25 | loop fusion | flops 7913472 | bytes 13848580 | tf_op jit(solution)/shard_map/sub | solution.py:701
  (391 shorter events, 130.2 us)
Async XLA Ops:
  7.2 206.2 %all-gather.7.cloned.1.call-start = ((), (), s32[]{:S(2)}) async-start(), calls=%async_computation.3 | async-start | bytes 12533760 | tf_op jit(solution)/shard_map/all_gather | solution.py:778
  10.9 270.0 %all-gather.5.cloned.1.call-start = ((), (), s32[]{:S(2)}) async-start(), calls=%async_computation.2 | async-start | bytes 5013504 | tf_op jit(solution)/shard_map/all_gather | solution.py:778
  11.6 22.1 %collective-permute-start = (bf16[1,96,768]{2,1,0:T(8,128)(2,1)S(1)}, bf16[1,96,768]{2,1,0:T(8,128)(2,1)}, u32[]{:S(2)}, u32[]{:S(2)}) collective-permute-start(bf16[1,96,768]{2,1,0:T(8,128)(2,1)S(1)} %bitcast.180), channel_id=1, source_target_pairs={{0,8},{2,10},{4,12},{6,14},{8,16},{10,18},{12,20},{14,22},{16,24},... | collective-permute-start | bytes 442376 | tf_op jit(solution)/shard_map/ppermute | solution.py:591
  14.7 19.1 %collective-permute-start.1 = (bf16[1,96,768]{2,1,0:T(8,128)(2,1)S(1)}, bf16[1,96,768]{2,1,0:T(8,128)(2,1)}, u32[]{:S(2)}, u32[]{:S(2)}) collective-permute-start(bf16[1,96,768]{2,1,0:T(8,128)(2,1)S(1)} %bitcast.181), channel_id=1, source_target_pairs={{0,16},{2,18},{4,20},{6,22},{8,24},{10,26},{12,28},{14,30},{16,0},... | collective-permute-start | bytes 442376 | tf_op jit(solution)/shard_map/ppermute | solution.py:591
  17.3 16.5 %collective-permute-start.2 = (bf16[1,96,768]{2,1,0:T(8,128)(2,1)S(1)}, bf16[1,96,768]{2,1,0:T(8,128)(2,1)}, u32[]{:S(2)}, u32[]{:S(2)}) collective-permute-start(bf16[1,96,768]{2,1,0:T(8,128)(2,1)S(1)} %bitcast.182), channel_id=1, source_target_pairs={{0,24},{2,26},{4,28},{6,30},{8,0},{10,2},{12,4},{14,6},{16,8},{18,... | collective-permute-start | bytes 442376 | tf_op jit(solution)/shard_map/ppermute | solution.py:591
  21.0 67.1 %collective-permute-start.10 = (bf16[1536,512]{1,0:T(8,128)(2,1)}, bf16[1536,512]{1,0:T(8,128)(2,1)}, u32[]{:S(2)}, u32[]{:S(2)}) collective-permute-start(bf16[1536,512]{1,0:T(8,128)(2,1)} %shard_map.350), channel_id=1, source_target_pairs={{0,1},{1,0},{2,3},{3,2},{4,5},{5,4},{6,7},{7,6},{8,9},{9,8},{10,11... | collective-permute-start | bytes 4718600 | tf_op jit(solution)/shard_map/ppermute | solution.py:708
  21.0 12.4 %collective-permute-start.11 = (s32[512]{0:T(512)S(1)}, s32[512]{0:T(512)S(1)}, u32[]{:S(2)}, u32[]{:S(2)}) collective-permute-start(s32[512]{0:T(512)S(1)} %bitcast.195), channel_id=1, source_target_pairs={{0,1},{1,0},{2,3},{3,2},{4,5},{5,4},{6,7},{7,6},{8,9},{9,8},{10,11... | collective-permute-start | bytes 6152 | tf_op jit(solution)/shard_map/ppermute | solution.py:708
  35.0 16.0 %collective-permute-start.7 = (bf16[1,4,16,1536]{3,2,1,0:T(8,128)(2,1)}, bf16[1,4,16,1536]{3,2,1,0:T(8,128)(2,1)S(1)}, u32[]{:S(2)}, u32[]{:S(2)}) collective-permute-start(bf16[1,4,16,1536]{3,2,1,0:T(8,128)(2,1)} %get-tuple-element.298), channel_id=1, source_target_pairs={{0,8},{2,10},{4,12},{6,14},{8,16},{10,18},{12,20},{14,22},{16,24},... | collective-permute-start | bytes 589832 | tf_op jit(solution)/shard_map/ppermute | solution.py:591
  39.5 19.2 %collective-permute-start.8 = (bf16[1,4,16,1536]{3,2,1,0:T(8,128)(2,1)}, bf16[1,4,16,1536]{3,2,1,0:T(8,128)(2,1)S(1)}, u32[]{:S(2)}, u32[]{:S(2)}) collective-permute-start(bf16[1,4,16,1536]{3,2,1,0:T(8,128)(2,1)} %get-tuple-element.298), channel_id=1, source_target_pairs={{0,16},{2,18},{4,20},{6,22},{8,24},{10,26},{12,28},{14,30},{16,0},... | collective-permute-start | bytes 589832 | tf_op jit(solution)/shard_map/ppermute | solution.py:591
  43.0 17.2 %collective-permute-start.9 = (bf16[1,4,16,1536]{3,2,1,0:T(8,128)(2,1)}, bf16[1,4,16,1536]{3,2,1,0:T(8,128)(2,1)S(1)}, u32[]{:S(2)}, u32[]{:S(2)}) collective-permute-start(bf16[1,4,16,1536]{3,2,1,0:T(8,128)(2,1)} %get-tuple-element.298), channel_id=1, source_target_pairs={{0,24},{2,26},{4,28},{6,30},{8,0},{10,2},{12,4},{14,6},{16,8},{18,... | collective-permute-start | bytes 589832 | tf_op jit(solution)/shard_map/ppermute | solution.py:591
  43.9 18.2 %collective-permute-start.3 = (bf16[2,1,96,768]{3,2,1,0:T(8,128)(2,1)S(1)}, bf16[2,1,96,768]{3,2,1,0:T(8,128)(2,1)S(1)}, u32[]{:S(2)}, u32[]{:S(2)}) collective-permute-start(bf16[2,1,96,768]{3,2,1,0:T(8,128)(2,1)S(1)} %get-tuple-element.294.refs_0_), channel_id=1, source_target_pairs={{0,2},{2,0},{4,6},{6,4},{8,10},{10,8},{12,14},{14,12},{16,18},{18,... | collective-permute-start | bytes 884744 | tf_op jit(solution)/shard_map/ppermute | solution.py:595
  50.9 11.1 %collective-permute-start.4 = (bf16[2,1,96,768]{3,2,1,0:T(8,128)(2,1)S(1)}, bf16[2,1,96,768]{3,2,1,0:T(8,128)(2,1)S(1)}, u32[]{:S(2)}, u32[]{:S(2)}) collective-permute-start(bf16[2,1,96,768]{3,2,1,0:T(8,128)(2,1)S(1)} %get-tuple-element.295.refs_1_), channel_id=1, source_target_pairs={{0,2},{2,0},{4,6},{6,4},{8,10},{10,8},{12,14},{14,12},{16,18},{18,... | collective-permute-start | bytes 884744 | tf_op jit(solution)/shard_map/ppermute | solution.py:595
  58.7 15.6 %collective-permute-start.5 = (bf16[2,1,96,768]{3,2,1,0:T(8,128)(2,1)S(1)}, bf16[2,1,96,768]{3,2,1,0:T(8,128)(2,1)S(1)}, u32[]{:S(2)}, u32[]{:S(2)}) collective-permute-start(bf16[2,1,96,768]{3,2,1,0:T(8,128)(2,1)S(1)} %get-tuple-element.294.refs_0_), channel_id=1, source_target_pairs={{0,4},{2,6},{4,0},{6,2},{8,12},{10,14},{12,8},{14,10},{16,20},{18,... | collective-permute-start | bytes 884744 | tf_op jit(solution)/shard_map/ppermute | solution.py:595
  60.2 23.9 %collective-permute-start.6 = (bf16[2,1,96,768]{3,2,1,0:T(8,128)(2,1)S(1)}, bf16[2,1,96,768]{3,2,1,0:T(8,128)(2,1)S(1)}, u32[]{:S(2)}, u32[]{:S(2)}) collective-permute-start(bf16[2,1,96,768]{3,2,1,0:T(8,128)(2,1)S(1)} %get-tuple-element.295.refs_1_), channel_id=1, source_target_pairs={{0,4},{2,6},{4,0},{6,2},{8,12},{10,14},{12,8},{14,10},{16,20},{18,... | collective-permute-start | bytes 884744 | tf_op jit(solution)/shard_map/ppermute | solution.py:595
  85.1 7.4 %collective-permute-start.12 = (bf16[2,1,96,768]{3,2,1,0:T(8,128)(2,1)S(1)}, bf16[2,1,96,768]{3,2,1,0:T(8,128)(2,1)S(1)}, u32[]{:S(2)}, u32[]{:S(2)}) collective-permute-start(bf16[2,1,96,768]{3,2,1,0:T(8,128)(2,1)S(1)} %collective-permute-done.5.refs_4_), channel_id=1, source_target_pairs={{0,2},{2,0},{4,6},{6,4},{8,10},{10,8},{12,14},{14,12},{16,18},{18,... | collective-permute-start | bytes 884744 | tf_op jit(solution)/shard_map/ppermute | solution.py:595
  86.6 7.8 %collective-permute-start.13 = (bf16[2,1,96,768]{3,2,1,0:T(8,128)(2,1)S(1)}, bf16[2,1,96,768]{3,2,1,0:T(8,128)(2,1)S(1)}, u32[]{:S(2)}, u32[]{:S(2)}) collective-permute-start(bf16[2,1,96,768]{3,2,1,0:T(8,128)(2,1)S(1)} %collective-permute-done.4.refs_3_), channel_id=1, source_target_pairs={{0,4},{2,6},{4,0},{6,2},{8,12},{10,14},{12,8},{14,10},{16,20},{18,... | collective-permute-start | bytes 884744 | tf_op jit(solution)/shard_map/ppermute | solution.py:595
  99.0 64.8 %collective-permute-start.14 = (bf16[1536,768]{1,0:T(8,128)(2,1)}, bf16[1536,768]{1,0:T(8,128)(2,1)}, u32[]{:S(2)}, u32[]{:S(2)}) collective-permute-start(bf16[1536,768]{1,0:T(8,128)(2,1)} %bitcast.164), channel_id=1, source_target_pairs={{0,1},{1,0},{2,3},{3,2},{4,5},{5,4},{6,7},{7,6},{8,9},{9,8},{10,11... | collective-permute-start | bytes 7077896 | tf_op jit(solution)/shard_map/ppermute | solution.py:708
  99.1 17.0 %collective-permute-start.15 = (bf16[2,1,4,16,1536]{4,3,2,1,0:T(8,128)(2,1)}, bf16[2,1,4,16,1536]{4,3,2,1,0:T(8,128)(2,1)}, u32[]{:S(2)}, u32[]{:S(2)}) collective-permute-start(bf16[2,1,4,16,1536]{4,3,2,1,0:T(8,128)(2,1)} %pad_maximum_fusion.4.refs_0_), channel_id=1, source_target_pairs={{0,2},{2,0},{4,6},{6,4},{8,10},{10,8},{12,14},{14,12},{16,18},{18,... | collective-permute-start | bytes 1179656 | tf_op jit(solution)/shard_map/ppermute | solution.py:595
  99.9 32.5 %collective-permute-start.16 = (bf16[2,1,4,16,1536]{4,3,2,1,0:T(8,128)(2,1)S(1)}, bf16[2,1,4,16,1536]{4,3,2,1,0:T(8,128)(2,1)}, u32[]{:S(2)}, u32[]{:S(2)}) collective-permute-start(bf16[2,1,4,16,1536]{4,3,2,1,0:T(8,128)(2,1)S(1)} %pad_maximum_fusion.5.refs_1_), channel_id=1, source_target_pairs={{0,2},{2,0},{4,6},{6,4},{8,10},{10,8},{12,14},{14,12},{16,18},{18,... | collective-permute-start | bytes 1179656 | tf_op jit(solution)/shard_map/ppermute | solution.py:595
  101.2 31.3 %collective-permute-start.17 = (bf16[2,1,4,16,1536]{4,3,2,1,0:T(8,128)(2,1)}, bf16[2,1,4,16,1536]{4,3,2,1,0:T(8,128)(2,1)}, u32[]{:S(2)}, u32[]{:S(2)}) collective-permute-start(bf16[2,1,4,16,1536]{4,3,2,1,0:T(8,128)(2,1)} %pad_maximum_fusion.4.refs_0_), channel_id=1, source_target_pairs={{0,4},{2,6},{4,0},{6,2},{8,12},{10,14},{12,8},{14,10},{16,20},{18,... | collective-permute-start | bytes 1179656 | tf_op jit(solution)/shard_map/ppermute | solution.py:595
  102.9 33.9 %collective-permute-start.18 = (bf16[2,1,4,16,1536]{4,3,2,1,0:T(8,128)(2,1)S(1)}, bf16[2,1,4,16,1536]{4,3,2,1,0:T(8,128)(2,1)}, u32[]{:S(2)}, u32[]{:S(2)}) collective-permute-start(bf16[2,1,4,16,1536]{4,3,2,1,0:T(8,128)(2,1)S(1)} %pad_maximum_fusion.5.refs_1_), channel_id=1, source_target_pairs={{0,4},{2,6},{4,0},{6,2},{8,12},{10,14},{12,8},{14,10},{16,20},{18,... | collective-permute-start | bytes 1179656 | tf_op jit(solution)/shard_map/ppermute | solution.py:595
  136.8 19.2 %collective-permute-start.19 = (bf16[2,1,4,16,1536]{4,3,2,1,0:T(8,128)(2,1)}, bf16[2,1,4,16,1536]{4,3,2,1,0:T(8,128)(2,1)S(1)}, u32[]{:S(2)}, u32[]{:S(2)}) collective-permute-start(bf16[2,1,4,16,1536]{4,3,2,1,0:T(8,128)(2,1)} %collective-permute-done.17.refs_4_), channel_id=1, source_target_pairs={{0,2},{2,0},{4,6},{6,4},{8,10},{10,8},{12,14},{14,12},{16,18},{18,... | collective-permute-start | bytes 1179656 | tf_op jit(solution)/shard_map/ppermute | solution.py:595
  137.1 19.9 %collective-permute-start.20 = (bf16[2,1,4,16,1536]{4,3,2,1,0:T(8,128)(2,1)}, bf16[2,1,4,16,1536]{4,3,2,1,0:T(8,128)(2,1)}, u32[]{:S(2)}, u32[]{:S(2)}) collective-permute-start(bf16[2,1,4,16,1536]{4,3,2,1,0:T(8,128)(2,1)} %collective-permute-done.16.refs_3_), channel_id=1, source_target_pairs={{0,4},{2,6},{4,0},{6,2},{8,12},{10,14},{12,8},{14,10},{16,20},{18,... | collective-permute-start | bytes 1179656 | tf_op jit(solution)/shard_map/ppermute | solution.py:595
  141.4 397.0 %reduce-scatter.2.cloned.1.call-start = ((), (), s32[]{:S(2)}) async-start(), calls=%async_computation.1 | async-start | bytes 12533760 | tf_op jit(solution)/shard_map/reduce_scatter | solution.py:662
  161.5 11.5 %collective-permute-start.22 = (bf16[16,4,16,1536]{3,2,1,0:T(8,128)(2,1)}, bf16[16,4,16,1536]{3,2,1,0:T(8,128)(2,1)}, u32[]{:S(2)}, u32[]{:S(2)}) collective-permute-start(bf16[16,4,16,1536]{3,2,1,0:T(8,128)(2,1)} %bitcast.162), channel_id=1, source_target_pairs={{0,1},{1,0},{2,3},{3,2},{4,5},{5,4},{6,7},{7,6},{8,9},{9,8},{10,11... | collective-permute-start | bytes 9437192 | tf_op jit(solution)/shard_map/ppermute | solution.py:708
  163.3 4.5 collective-permute-start.21
  200.0 2.0 collective-permute-start.23
  305.3 5.9 %collective-permute-start.24 = (bf16[1536,1024]{1,0:T(8,128)(2,1)}, bf16[1536,1024]{1,0:T(8,128)(2,1)S(1)}, u32[]{:S(2)}, u32[]{:S(2)}) collective-permute-start(bf16[1536,1024]{1,0:T(8,128)(2,1)} %get-tuple-element.351.refs_4_), channel_id=1, source_target_pairs={{0,1},{1,0},{2,3},{3,2},{4,5},{5,4},{6,7},{7,6},{8,9},{9,8},{10,11... | collective-permute-start | bytes 9437192 | tf_op jit(solution)/shard_map/ppermute | solution.py:708
  311.2 20.1 %collective-permute-start.25 = (bf16[2,3,96,512]{3,2,1,0:T(8,128)(2,1)}, bf16[2,3,96,512]{3,2,1,0:T(8,128)(2,1)}, u32[]{:S(2)}, u32[]{:S(2)}) collective-permute-start(bf16[2,3,96,512]{3,2,1,0:T(8,128)(2,1)} %get-tuple-element.354), channel_id=1, source_target_pairs={{0,2},{2,0},{4,6},{6,4},{8,10},{10,8},{12,14},{14,12},{16,18},{18,... | collective-permute-start | bytes 1769480 | tf_op jit(solution)/shard_map/ppermute | solution.py:595
  312.7 19.0 %collective-permute-start.26 = (bf16[2,3,96,512]{3,2,1,0:T(8,128)(2,1)}, bf16[2,3,96,512]{3,2,1,0:T(8,128)(2,1)}, u32[]{:S(2)}, u32[]{:S(2)}) collective-permute-start(bf16[2,3,96,512]{3,2,1,0:T(8,128)(2,1)} %get-tuple-element.355), channel_id=1, source_target_pairs={{0,4},{2,6},{4,0},{6,2},{8,12},{10,14},{12,8},{14,10},{16,20},{18,... | collective-permute-start | bytes 1769480 | tf_op jit(solution)/shard_map/ppermute | solution.py:595
  331.7 24.7 %collective-permute-start.27 = (bf16[2,3,96,512]{3,2,1,0:T(8,128)(2,1)}, bf16[2,3,96,512]{3,2,1,0:T(8,128)(2,1)S(1)}, u32[]{:S(2)}, u32[]{:S(2)}) collective-permute-start(bf16[2,3,96,512]{3,2,1,0:T(8,128)(2,1)} %get-tuple-element.361), channel_id=1, source_target_pairs={{0,2},{2,0},{4,6},{6,4},{8,10},{10,8},{12,14},{14,12},{16,18},{18,... | collective-permute-start | bytes 1769480 | tf_op jit(solution)/shard_map/ppermute | solution.py:595
  333.1 23.3 %collective-permute-start.28 = (bf16[2,3,96,512]{3,2,1,0:T(8,128)(2,1)}, bf16[2,3,96,512]{3,2,1,0:T(8,128)(2,1)}, u32[]{:S(2)}, u32[]{:S(2)}) collective-permute-start(bf16[2,3,96,512]{3,2,1,0:T(8,128)(2,1)} %get-tuple-element.362), channel_id=1, source_target_pairs={{0,4},{2,6},{4,0},{6,2},{8,12},{10,14},{12,8},{14,10},{16,20},{18,... | collective-permute-start | bytes 1769480 | tf_op jit(solution)/shard_map/ppermute | solution.py:595
  356.5 6.5 %collective-permute-start.29 = (bf16[3,192,1024]{2,1,0:T(8,128)(2,1)S(1)}, bf16[3,192,1024]{2,1,0:T(8,128)(2,1)S(1)}, u32[]{:S(2)}, u32[]{:S(2)}) collective-permute-start(bf16[3,192,1024]{2,1,0:T(8,128)(2,1)S(1)} %copy-done.10), channel_id=1, source_target_pairs={{0,1},{1,0},{2,3},{3,2},{4,5},{5,4},{6,7},{7,6},{8,9},{9,8},{10,11... | collective-permute-start | bytes 3538952 | tf_op jit(solution)/shard_map/ppermute | solution.py:708
  358.5 24.0 %collective-permute-start.30 = (bf16[2,3,96,512]{3,2,1,0:T(8,128)(2,1)}, bf16[2,3,96,512]{3,2,1,0:T(8,128)(2,1)}, u32[]{:S(2)}, u32[]{:S(2)}) collective-permute-start(bf16[2,3,96,512]{3,2,1,0:T(8,128)(2,1)} %add_convert_fusion.1), channel_id=1, source_target_pairs={{0,2},{2,0},{4,6},{6,4},{8,10},{10,8},{12,14},{14,12},{16,18},{18,... | collective-permute-start | bytes 1769480 | tf_op jit(solution)/shard_map/ppermute | solution.py:595
  359.7 24.1 %collective-permute-start.31 = (bf16[2,3,96,512]{3,2,1,0:T(8,128)(2,1)}, bf16[2,3,96,512]{3,2,1,0:T(8,128)(2,1)}, u32[]{:S(2)}, u32[]{:S(2)}) collective-permute-start(bf16[2,3,96,512]{3,2,1,0:T(8,128)(2,1)} %add_convert_fusion), channel_id=1, source_target_pairs={{0,4},{2,6},{4,0},{6,2},{8,12},{10,14},{12,8},{14,10},{16,20},{18,... | collective-permute-start | bytes 1769480 | tf_op jit(solution)/shard_map/ppermute | solution.py:595
  386.4 16.2 %collective-permute-start.32 = (bf16[3,96,512]{2,1,0:T(8,128)(2,1)S(1)}, bf16[3,96,512]{2,1,0:T(8,128)(2,1)S(1)}, u32[]{:S(2)}, u32[]{:S(2)}) collective-permute-start(bf16[3,96,512]{2,1,0:T(8,128)(2,1)S(1)} %fusion.32), channel_id=1, source_target_pairs={{0,24},{2,26},{4,28},{6,30},{8,0},{10,2},{12,4},{14,6},{16,8},{18,... | collective-permute-start | bytes 884744 | tf_op jit(solution)/shard_map/ppermute | solution.py:591
  387.9 24.6 %collective-permute-start.33 = (bf16[3,96,512]{2,1,0:T(8,128)(2,1)S(1)}, bf16[3,96,512]{2,1,0:T(8,128)(2,1)S(1)}, u32[]{:S(2)}, u32[]{:S(2)}) collective-permute-start(bf16[3,96,512]{2,1,0:T(8,128)(2,1)S(1)} %get-tuple-element.383), channel_id=1, source_target_pairs={{0,16},{2,18},{4,20},{6,22},{8,24},{10,26},{12,28},{14,30},{16,0},... | collective-permute-start | bytes 884744 | tf_op jit(solution)/shard_map/ppermute | solution.py:591
  387.9 24.6 %collective-permute-start.34 = (bf16[3,96,512]{2,1,0:T(8,128)(2,1)S(1)}, bf16[3,96,512]{2,1,0:T(8,128)(2,1)S(1)}, u32[]{:S(2)}, u32[]{:S(2)}) collective-permute-start(bf16[3,96,512]{2,1,0:T(8,128)(2,1)S(1)} %get-tuple-element.384), channel_id=1, source_target_pairs={{0,8},{2,10},{4,12},{6,14},{8,16},{10,18},{12,20},{14,22},{16,24},... | collective-permute-start | bytes 884744 | tf_op jit(solution)/shard_map/ppermute | solution.py:591
  412.5 20.8 %collective-permute-start.35 = (bf16[2,1,4,16,1536]{4,3,2,1,0:T(8,128)(2,1)}, bf16[2,1,4,16,1536]{4,3,2,1,0:T(8,128)(2,1)S(1)}, u32[]{:S(2)}, u32[]{:S(2)}) collective-permute-start(bf16[2,1,4,16,1536]{4,3,2,1,0:T(8,128)(2,1)} %get-tuple-element.395), channel_id=1, source_target_pairs={{0,2},{2,0},{4,6},{6,4},{8,10},{10,8},{12,14},{14,12},{16,18},{18,... | collective-permute-start | bytes 1179656 | tf_op jit(solution)/shard_map/ppermute | solution.py:595
  415.2 20.6 %collective-permute-start.36 = (bf16[2,1,4,16,1536]{4,3,2,1,0:T(8,128)(2,1)}, bf16[2,1,4,16,1536]{4,3,2,1,0:T(8,128)(2,1)S(1)}, u32[]{:S(2)}, u32[]{:S(2)}) collective-permute-start(bf16[2,1,4,16,1536]{4,3,2,1,0:T(8,128)(2,1)} %get-tuple-element.396), channel_id=1, source_target_pairs={{0,4},{2,6},{4,0},{6,2},{8,12},{10,14},{12,8},{14,10},{16,20},{18,... | collective-permute-start | bytes 1179656 | tf_op jit(solution)/shard_map/ppermute | solution.py:595
  415.2 27.3 %collective-permute-start.37 = (bf16[2,1,4,16,1536]{4,3,2,1,0:T(8,128)(2,1)}, bf16[2,1,4,16,1536]{4,3,2,1,0:T(8,128)(2,1)S(1)}, u32[]{:S(2)}, u32[]{:S(2)}) collective-permute-start(bf16[2,1,4,16,1536]{4,3,2,1,0:T(8,128)(2,1)} %get-tuple-element.397), channel_id=1, source_target_pairs={{0,2},{2,0},{4,6},{6,4},{8,10},{10,8},{12,14},{14,12},{16,18},{18,... | collective-permute-start | bytes 1179656 | tf_op jit(solution)/shard_map/ppermute | solution.py:595
  417.1 26.8 %collective-permute-start.38 = (bf16[2,1,4,16,1536]{4,3,2,1,0:T(8,128)(2,1)}, bf16[2,1,4,16,1536]{4,3,2,1,0:T(8,128)(2,1)S(1)}, u32[]{:S(2)}, u32[]{:S(2)}) collective-permute-start(bf16[2,1,4,16,1536]{4,3,2,1,0:T(8,128)(2,1)} %get-tuple-element.398), channel_id=1, source_target_pairs={{0,4},{2,6},{4,0},{6,2},{8,12},{10,14},{12,8},{14,10},{16,20},{18,... | collective-permute-start | bytes 1179656 | tf_op jit(solution)/shard_map/ppermute | solution.py:595
  445.6 17.4 %collective-permute-start.39 = (bf16[3,192,1024]{2,1,0:T(8,128)(2,1)S(1)}, bf16[3,192,1024]{2,1,0:T(8,128)(2,1)S(1)}, u32[]{:S(2)}, u32[]{:S(2)}) collective-permute-start(bf16[3,192,1024]{2,1,0:T(8,128)(2,1)S(1)} %copy-done.26), channel_id=1, source_target_pairs={{0,1},{1,0},{2,3},{3,2},{4,5},{5,4},{6,7},{7,6},{8,9},{9,8},{10,11... | collective-permute-start | bytes 3538952 | tf_op jit(solution)/shard_map/ppermute | solution.py:708
  445.6 11.8 %collective-permute-start.40 = (bf16[2,1,4,16,1536]{4,3,2,1,0:T(8,128)(2,1)}, bf16[2,1,4,16,1536]{4,3,2,1,0:T(8,128)(2,1)}, u32[]{:S(2)}, u32[]{:S(2)}) collective-permute-start(bf16[2,1,4,16,1536]{4,3,2,1,0:T(8,128)(2,1)} %add_convert_fusion.3), channel_id=1, source_target_pairs={{0,2},{2,0},{4,6},{6,4},{8,10},{10,8},{12,14},{14,12},{16,18},{18,... | collective-permute-start | bytes 1179656 | tf_op jit(solution)/shard_map/ppermute | solution.py:595
  446.0 17.1 %collective-permute-start.41 = (bf16[2,1,4,16,1536]{4,3,2,1,0:T(8,128)(2,1)}, bf16[2,1,4,16,1536]{4,3,2,1,0:T(8,128)(2,1)}, u32[]{:S(2)}, u32[]{:S(2)}) collective-permute-start(bf16[2,1,4,16,1536]{4,3,2,1,0:T(8,128)(2,1)} %add_convert_fusion.2), channel_id=1, source_target_pairs={{0,4},{2,6},{4,0},{6,2},{8,12},{10,14},{12,8},{14,10},{16,20},{18,... | collective-permute-start | bytes 1179656 | tf_op jit(solution)/shard_map/ppermute | solution.py:595
  466.9 19.6 %collective-permute-start.42 = (bf16[2,1,96,768]{3,2,1,0:T(8,128)(2,1)}, bf16[2,1,96,768]{3,2,1,0:T(8,128)(2,1)S(1)}, u32[]{:S(2)}, u32[]{:S(2)}) collective-permute-start(bf16[2,1,96,768]{3,2,1,0:T(8,128)(2,1)} %get-tuple-element.427), channel_id=1, source_target_pairs={{0,2},{2,0},{4,6},{6,4},{8,10},{10,8},{12,14},{14,12},{16,18},{18,... | collective-permute-start | bytes 884744 | tf_op jit(solution)/shard_map/ppermute | solution.py:595
  469.3 17.2 %collective-permute-start.43 = (bf16[2,1,96,768]{3,2,1,0:T(8,128)(2,1)}, bf16[2,1,96,768]{3,2,1,0:T(8,128)(2,1)S(1)}, u32[]{:S(2)}, u32[]{:S(2)}) collective-permute-start(bf16[2,1,96,768]{3,2,1,0:T(8,128)(2,1)} %get-tuple-element.428), channel_id=1, source_target_pairs={{0,4},{2,6},{4,0},{6,2},{8,12},{10,14},{12,8},{14,10},{16,20},{18,... | collective-permute-start | bytes 884744 | tf_op jit(solution)/shard_map/ppermute | solution.py:595
  469.4 17.2 %collective-permute-start.44 = (bf16[2,1,96,768]{3,2,1,0:T(8,128)(2,1)}, bf16[2,1,96,768]{3,2,1,0:T(8,128)(2,1)S(1)}, u32[]{:S(2)}, u32[]{:S(2)}) collective-permute-start(bf16[2,1,96,768]{3,2,1,0:T(8,128)(2,1)} %get-tuple-element.429), channel_id=1, source_target_pairs={{0,2},{2,0},{4,6},{6,4},{8,10},{10,8},{12,14},{14,12},{16,18},{18,... | collective-permute-start | bytes 884744 | tf_op jit(solution)/shard_map/ppermute | solution.py:595
  471.4 15.2 %collective-permute-start.45 = (bf16[2,1,96,768]{3,2,1,0:T(8,128)(2,1)}, bf16[2,1,96,768]{3,2,1,0:T(8,128)(2,1)S(1)}, u32[]{:S(2)}, u32[]{:S(2)}) collective-permute-start(bf16[2,1,96,768]{3,2,1,0:T(8,128)(2,1)} %get-tuple-element.430), channel_id=1, source_target_pairs={{0,4},{2,6},{4,0},{6,2},{8,12},{10,14},{12,8},{14,10},{16,20},{18,... | collective-permute-start | bytes 884744 | tf_op jit(solution)/shard_map/ppermute | solution.py:595
  488.2 33.8 %collective-permute-start.46 = (bf16[1536,1024]{1,0:T(8,128)(2,1)}, bf16[1536,1024]{1,0:T(8,128)(2,1)}, u32[]{:S(2)}, u32[]{:S(2)}) collective-permute-start(bf16[1536,1024]{1,0:T(8,128)(2,1)} %get-tuple-element.460.own_ref), channel_id=1, source_target_pairs={{0,1},{1,0},{2,3},{3,2},{4,5},{5,4},{6,7},{7,6},{8,9},{9,8},{10,11... | collective-permute-start | bytes 9437192 | tf_op jit(solution)/shard_map/ppermute | solution.py:708
  497.7 10.6 %collective-permute-start.47 = (bf16[1,4,16,1536]{3,2,1,0:T(8,128)(2,1)}, bf16[1,4,16,1536]{3,2,1,0:T(8,128)(2,1)}, u32[]{:S(2)}, u32[]{:S(2)}) collective-permute-start(bf16[1,4,16,1536]{3,2,1,0:T(8,128)(2,1)} %get-tuple-element.445), channel_id=1, source_target_pairs={{0,24},{2,26},{4,28},{6,30},{8,0},{10,2},{12,4},{14,6},{16,8},{18,... | collective-permute-start | bytes 589832 | tf_op jit(solution)/shard_map/ppermute | solution.py:591
  497.8 24.3 %collective-permute-start.48 = (bf16[1,4,16,1536]{3,2,1,0:T(8,128)(2,1)}, bf16[1,4,16,1536]{3,2,1,0:T(8,128)(2,1)}, u32[]{:S(2)}, u32[]{:S(2)}) collective-permute-start(bf16[1,4,16,1536]{3,2,1,0:T(8,128)(2,1)} %get-tuple-element.446), channel_id=1, source_target_pairs={{0,16},{2,18},{4,20},{6,22},{8,24},{10,26},{12,28},{14,30},{16,0},... | collective-permute-start | bytes 589832 | tf_op jit(solution)/shard_map/ppermute | solution.py:591
  503.6 18.5 %collective-permute-start.49 = (bf16[1,4,16,1536]{3,2,1,0:T(8,128)(2,1)}, bf16[1,4,16,1536]{3,2,1,0:T(8,128)(2,1)}, u32[]{:S(2)}, u32[]{:S(2)}) collective-permute-start(bf16[1,4,16,1536]{3,2,1,0:T(8,128)(2,1)} %get-tuple-element.447), channel_id=1, source_target_pairs={{0,8},{2,10},{4,12},{6,14},{8,16},{10,18},{12,20},{14,22},{16,24},... | collective-permute-start | bytes 589832 | tf_op jit(solution)/shard_map/ppermute | solution.py:591
  507.0 15.1 %collective-permute-start.50 = (bf16[2,1,96,768]{3,2,1,0:T(8,128)(2,1)S(1)}, bf16[2,1,96,768]{3,2,1,0:T(8,128)(2,1)S(1)}, u32[]{:S(2)}, u32[]{:S(2)}) collective-permute-start(bf16[2,1,96,768]{3,2,1,0:T(8,128)(2,1)S(1)} %copy-done.58), channel_id=1, source_target_pairs={{0,2},{2,0},{4,6},{6,4},{8,10},{10,8},{12,14},{14,12},{16,18},{18,... | collective-permute-start | bytes 884744 | tf_op jit(solution)/shard_map/ppermute | solution.py:595
  508.3 13.8 %collective-permute-start.51 = (bf16[2,1,96,768]{3,2,1,0:T(8,128)(2,1)S(1)}, bf16[2,1,96,768]{3,2,1,0:T(8,128)(2,1)S(1)}, u32[]{:S(2)}, u32[]{:S(2)}) collective-permute-start(bf16[2,1,96,768]{3,2,1,0:T(8,128)(2,1)S(1)} %copy-done.57), channel_id=1, source_target_pairs={{0,4},{2,6},{4,0},{6,2},{8,12},{10,14},{12,8},{14,10},{16,20},{18,... | collective-permute-start | bytes 884744 | tf_op jit(solution)/shard_map/ppermute | solution.py:595
  524.2 12.9 %collective-permute-start.52 = (bf16[1,96,768]{2,1,0:T(8,128)(2,1)S(1)}, bf16[1,96,768]{2,1,0:T(8,128)(2,1)S(1)}, u32[]{:S(2)}, u32[]{:S(2)}) collective-permute-start(bf16[1,96,768]{2,1,0:T(8,128)(2,1)S(1)} %get-tuple-element.463), channel_id=1, source_target_pairs={{0,24},{2,26},{4,28},{6,30},{8,0},{10,2},{12,4},{14,6},{16,8},{18,... | collective-permute-start | bytes 442376 | tf_op jit(solution)/shard_map/ppermute | solution.py:591
  524.2 13.0 %collective-permute-start.53 = (bf16[1,96,768]{2,1,0:T(8,128)(2,1)S(1)}, bf16[1,96,768]{2,1,0:T(8,128)(2,1)S(1)}, u32[]{:S(2)}, u32[]{:S(2)}) collective-permute-start(bf16[1,96,768]{2,1,0:T(8,128)(2,1)S(1)} %get-tuple-element.464), channel_id=1, source_target_pairs={{0,16},{2,18},{4,20},{6,22},{8,24},{10,26},{12,28},{14,30},{16,0},... | collective-permute-start | bytes 442376 | tf_op jit(solution)/shard_map/ppermute | solution.py:591
  524.3 12.9 %collective-permute-start.54 = (bf16[1,96,768]{2,1,0:T(8,128)(2,1)S(1)}, bf16[1,96,768]{2,1,0:T(8,128)(2,1)S(1)}, u32[]{:S(2)}, u32[]{:S(2)}) collective-permute-start(bf16[1,96,768]{2,1,0:T(8,128)(2,1)S(1)} %get-tuple-element.465), channel_id=1, source_target_pairs={{0,8},{2,10},{4,12},{6,14},{8,16},{10,18},{12,20},{14,22},{16,24},... | collective-permute-start | bytes 442376 | tf_op jit(solution)/shard_map/ppermute | solution.py:591
  545.6 3.8 collective-permute-start.56
  546.5 3.8 collective-permute-start.57
  548.2 4.7 collective-permute-start.58
  553.0 7.2 %collective-permute-start.59 = (f32[44,128]{1,0:T(8,128)S(1)}, f32[44,128]{1,0:T(8,128)S(1)}, u32[]{:S(2)}, u32[]{:S(2)}) collective-permute-start(f32[44,128]{1,0:T(8,128)S(1)} %add_add_fusion.1), channel_id=1, source_target_pairs={{0,16},{2,18},{4,20},{6,22},{8,24},{10,26},{12,28},{14,30},{16,0},... | collective-permute-start | bytes 67592 | tf_op jit(solution)/shard_map/ppermute | solution.py:591
  556.3 5.6 collective-permute-start.60
  556.3 5.6 collective-permute-start.61
  (87 other events, 1014.4 us)
Sparse Core Ops, SparseCore 0:
  11.4 182.1 all-gather.6
  196.9 84.0 all-gather.4
  286.9 213.6 reduce-scatter.1

commit v3 on v2

--- a/solution.py
+++ b/solution.py
@@ -271,9 +271,10 @@
     normed = x_ref[...]
     slope = 0.7978845608028654
     stores = []
-    for step in range(width // FC):
-        cols = slice(step * FC, (step + 1) * FC)
-        w_gate = weights[0, :, :, cols].reshape(rows, FC)
+    for step in range(-(-width // FC)):
+        cols = slice(step * FC, min((step + 1) * FC, width))
+        units = cols.stop - cols.start
+        w_gate = weights[0, :, :, cols].reshape(rows, units)
         gate = dot_tn(w_gate, normed)
         square = gate * gate
         tanh = jnp.tanh(slope * gate * (1.0 + 0.044715 * square))
@@ -282,13 +283,13 @@
         act_grad = half + 0.5 * gate * (1.0 - tanh * tanh) * (slope * (1.0 + 0.134145 * square))
         if step == 0:
             loads[1].wait()
-        w_up = weights[1, :, :, cols].reshape(rows, FC)
+        w_up = weights[1, :, :, cols].reshape(rows, units)
         upward = dot_tn(w_up, normed)
         hidden = (act * upward).astype(BF)
         if step == 0:
             loads[2].wait()
             inputs[1].wait()
-        w_down = weights[2, :, :, cols].reshape(rows, FC)
+        w_down = weights[2, :, :, cols].reshape(rows, units)
         out_grad = og_ref[...]
         grad_hidden = dot_tn(w_down, out_grad)
         grad_gate = (grad_hidden * upward * act_grad).astype(BF)
@@ -301,7 +302,7 @@
         if step > 0 or not first:
             back = back_acc[...] + back
             out = out_acc[...] + out
-        final = step == width // FC - 1
+        final = cols.stop == width
         if final and last:
             out_low, back_low = refs[10:]
             back_low[...] = back.astype(BF)
@@ -315,7 +316,7 @@
             stores = [pltpu.make_async_copy(src, dst, acc_sems.at[i]) for i, (src, dst) in enumerate(zip(sources, out_refs))]
             for copy in stores:
                 copy.start()
-        shape = (count, block, FC)
+        shape = (count, block, units)
         grads[0, :, :, cols] = dot_nt(normed, grad_gate).astype(BF).reshape(shape)
         grads[1, :, :, cols] = dot_nt(normed, grad_up).astype(BF).reshape(shape)
         grads[2, :, :, cols] = dot_nt(out_grad, hidden).astype(BF).reshape(shape)
@@ -543,6 +544,29 @@
     )(resid, own, other)
 
 
+def memory_kernel(block, pad, key_map, value_map, kv_ref, out_ref):
+    total = dot_tn(key_map[0], kv_ref[0]) + dot_tn(value_map[0], kv_ref[1])
+    out_ref[...] = squeeze_rows(total, block, pad)
+
+
+def memory_gradient(maps, grad_kv, block, pad):
+    unused, inner, rows = maps.shape
+    enc = grad_kv.shape[2]
+    return pl.pallas_call(
+        functools.partial(memory_kernel, block, pad),
+        grid=(enc // QB,),
+        in_specs=[
+            pl.BlockSpec((1, inner, rows), lambda j: (1, 0, 0)),
+            pl.BlockSpec((1, inner, rows), lambda j: (2, 0, 0)),
+            pl.BlockSpec((2, inner, QB), lambda j: (0, 0, j)),
+        ],
+        out_specs=pl.BlockSpec((rows // pad * block, QB), lambda j: (0, j)),
+        out_shape=shape_of(rows // pad * block, enc, dtype=F32),
+        compiler_params=pltpu.CompilerParams(vmem_limit_bytes=VMEM),
+        cost_estimate=pl.CostEstimate(flops=4 * inner * rows * enc, bytes_accessed=8 << 20, transcendentals=0),
+    )(maps, maps, grad_kv)
+
+
 def norm_back_kernel(upstream, squeeze, n_ups, *refs):
     values_ref, inv_ref, gain_ref, base_ref = refs[:4]
     outs = refs[4 + n_ups :]
@@ -569,6 +593,8 @@
     part = pl.BlockSpec((rows, QB), lambda j: (0, j))
 
     def spec(array, whole):
+        if whole is None:
+            return pl.BlockSpec((1,) + array.shape[1:], lambda j: (0,) * array.ndim)
         if whole:
             return pl.BlockSpec(array.shape, lambda j: (0,) * array.ndim)
         return pl.BlockSpec(array.shape[:-1] + (QB,), lambda j: (0,) * (array.ndim - 1) + (j,))
@@ -716,7 +742,7 @@
 def chunk_sizes(width):
     if lax.axis_size("tok") != 16:
         return [FC] * (width // FC)
-    return [5 * FC, width - 5 * FC]
+    return [5 * FC + FC // 2, width - 5 * FC - FC // 2]
 
 
 def shards(
@@ -796,7 +822,10 @@
     bucket_hot = (bucket_ids[None, :] == jnp.arange(NB, dtype=jnp.int32)[:, None]).astype(F32)
     bias_vec = jnp.dot(rel_bias, bucket_hot, precision=lax.Precision.HIGHEST)
     vec = jnp.pad(bias_vec, ((0, 0), (QB, 0))).reshape(heads, 1, QB + LEN)
-    mem_full, inv_one, vec, keep = tick((mem_full, inv_one, vec, keep), self_w)
+    far_ids = jnp.pad(bucket_ids, (QB, 0), constant_values=-1)
+    diag_ids = jnp.concatenate([far_ids[d * QB : (d + 2) * QB][::-1] for d in range(LEN // 2 // QB + 1)])
+    diag_hot = (diag_ids[:, None] == jnp.arange(NB, dtype=jnp.int32)[None, :]).astype(F32)
+    mem_full, inv_one, vec, keep, diag_hot = tick((mem_full, inv_one, vec, keep, diag_hot), self_w)
 
     self_blocks = place_blocks(owners, self_w.finish())
     gain_blocks = self_blocks[:, block : block + 3, :block]
@@ -862,7 +891,7 @@
     )
     grad_one_low, gain_two = norm_back(
         resid_one, inv_two, gains[1], grad_two_low,
-        lambda w, g: dot_tn(w[...], g[...]), (cross_full[0], grad_q_full), (True, False), flops=2 * INNER * rows * LEN,
+        lambda w, g: dot_tn(w[0], g[...]), (cross_full, grad_q_full), (None, False), flops=2 * INNER * rows * LEN,
     )
 
     grad_one_low, cross_d, cross_d_other = tick((grad_one_low, cross_d, cross_d_other), ffn_g[-1])
@@ -899,15 +928,11 @@
     kv_other = lax.dynamic_slice_in_dim(cross_d_other[1:], mem_index * enc, enc, 2)
     kv_all = jnp.concatenate(
         [jnp.where(mem_index == 0, kv_own, kv_other), jnp.where(mem_index == 0, kv_other, kv_own)], axis=1
-    ).reshape(2 * INNER, enc)
-    memory_grad = narrow(dot_tn(cross_full[1:3].reshape(2 * INNER, rows), kv_all), 0).T.reshape(1, enc, D)
+    )
+    memory_grad = memory_gradient(cross_full, kv_all, block, pad).T.reshape(1, enc, D)
     memory_grad, out_low, out_other, diag = tick((memory_grad, out_low, out_other, diag), cross_g, self_g)
     layer_out = layer_output(resid_two, out_low, out_other, block, pad).T
-    spread = jnp.zeros((heads, QB + LEN), F32)
-    diag = diag[:, :, ::-1]
-    for d in range(diag.shape[1]):
-        spread = spread.at[:, d * QB : d * QB + 2 * QB].add(diag[:, d])
-    rel_grad = jnp.dot(spread[:, QB:], bucket_hot.T, precision=lax.Precision.HIGHEST)
+    rel_grad = jnp.dot(diag.reshape(heads, -1), diag_hot, precision=lax.Precision.HIGHEST)
     layer_out, rel_grad = tick((layer_out, rel_grad), self_g, cross_g)
     ffn_sum = jnp.concatenate([t.finish() for t in ffn_g], axis=2)
     cross_sum = cross_g.finish()[0, :, :share]
@@ -917,7 +942,9 @@
     ffn_grads = ffn_sum[:, :block].transpose(0, 2, 1)
     cross_grads = narrow(cross_sum, 2)
     local_squares = (
-        jnp.sum(jnp.square(self_sum)) + jnp.sum(jnp.square(ffn_sum)) + jnp.sum(jnp.square(cross_sum))
+        jnp.sum(jnp.square(self_sum), keepdims=True)
+        + jnp.sum(jnp.square(ffn_sum), keepdims=True)[0]
+        + jnp.sum(jnp.square(cross_sum), keepdims=True)[0]
     )
     self_grads, ffn_grads, cross_grads, local_squares = lax.optimization_barrier(
         (self_grads, ffn_grads, cross_grads, local_squares)
@@ -928,12 +955,12 @@
         jnp.zeros((8, 128), F32), jnp.pad(rel_grad, ((0, 0), (0, 128 - NB))), mem_index * heads, 0
     )
     totals = sum_all(
-        jnp.concatenate([gain_grad.reshape(gain_lines, 128), rel_padded.at[H, 0].set(local_squares)])
+        jnp.concatenate([gain_grad.reshape(gain_lines, 128), rel_padded.at[H : H + 1, :1].set(local_squares)])
     )
     gains_total, rel_total = totals[:gain_lines].reshape(3, rows), totals[gain_lines : gain_lines + H, :NB]
     gains_sum = lax.dynamic_slice_in_dim(gains_total, lax.axis_index("tok") * pad, pad, 1)[:, :block]
-    total_squares = totals[gain_lines + H, 0] + jnp.sum(gains_total * gains_total)
-    grad_norm = jnp.sqrt(total_squares + jnp.sum(rel_total * rel_total))
+    total_squares = totals[gain_lines + H : gain_lines + H + 1, :1] + jnp.sum(gains_total * gains_total, keepdims=True)
+    grad_norm = jnp.sqrt(total_squares + jnp.sum(rel_total * rel_total, keepdims=True))
     rel_g = lax.dynamic_slice_in_dim(rel_total, mem_index * heads, heads, 0)
     clip_scale = CLIP_NORM / jnp.maximum(grad_norm, CLIP_NORM)
     self_new = adam_step(self_weights, self_first, self_second, self_grads, clip_scale, RATE_MATRIX, DECAY_MATRIX)
@@ -945,7 +972,7 @@
         layer_out,
         input_grad,
         memory_grad,
-        grad_norm,
+        grad_norm.reshape(()),
         *self_new,
         *cross_new,
         *ffn_new,

time: 593 us -> 572 us (0.965)
  local copies, waits for them, and re-layouts: 40.7 us -> 27.6 us
  Pallas kernels: 213 us -> 224 us
  waiting for transfers between devices: 148 us -> 139 us
  starting transfers between devices: 75.2 us -> 68.2 us
    ppermute x33, waiting for transfers between devices: 92.1 us -> 68.6 us  [flipped(): return lax.ppermute(value, 'tok', [(t, t ^ bits) for t in range(16)])]
    reduce_scatter x1, waiting for transfers between devices: 0.02 us -> 11.1 us  [scatter_steps(): lax.psum_scatter(blocks[0], 'tok', scatter_dimension=0, tiled=False)]
    ppermute x18, waiting for transfers between devices: 28.4 us -> 35.1 us  [rotated(): lax.ppermute(value, 'tok', [(t, (t // 4 + step) % 4 * 4 + t % 4) for t in...]
    dot_general x4 -> x3, matrix products: 14.1 us -> 12 us  [dot_tn(): lax.dot_general(a, b, (((0,), (0,)), ((), ())), preferred_element_type=F32)]
  transfers between devices with their start and end apart: 65 -> 65, of which waited for: 33 -> 32; matrix products, arithmetic and copies ran while one was open for 17% -> 15% of each run, Pallas kernels for 36% -> 40%
where the time goes in v3:
time: 572 us; the launch traced here: 564 us
  Pallas kernels  224 us (39%)
  waiting for transfers between devices  139 us (24%)
  starting transfers between devices  68.2 us (12%)
  other arithmetic  60.5 us (11%)
  local copies, waits for them, and re-layouts  27.6 us (5%)
  matrix products  24.1 us (4%)
  between operations  20.4 us (4%)
    pallas_call x2, Pallas kernels, feed_forward(): pl.pallas_call(functools.partial(ffn_kernel, len(sizes), first, last), in...  79.7 us
    ppermute x33, waiting for transfers between devices, flipped(): return lax.ppermute(value, 'tok', [(t, t ^ bits) for t in range(16)])  68.6 us
    pallas_call x4, Pallas kernels, attn_call(): pl.pallas_call(kernel, grid=(heads,), in_specs=in_specs, out_specs=out_sp...  49.1 us
    ppermute x33, starting transfers between devices, flipped(): return lax.ppermute(value, 'tok', [(t, t ^ bits) for t in range(16)])  36.6 us
    ppermute x18, waiting for transfers between devices, rotated(): lax.ppermute(value, 'tok', [(t, (t // 4 + step) % 4 * 4 + t % 4) for t in...  35.1 us
    pallas_call x3, Pallas kernels, norm_back(): pl.pallas_call(functools.partial(norm_back_kernel, upstream, squeeze, len...  35 us
    ppermute x18, starting transfers between devices, rotated(): lax.ppermute(value, 'tok', [(t, (t // 4 + step) % 4 * 4 + t % 4) for t in...  29.7 us
    all_gather x2, waiting for transfers between devices, shards(): lax.all_gather(ffn_wire[:, :, start:start + size], 'tok', axis=0, tiled=F...  14.3 us
  transfers between devices with their start and end apart: 65, of which 32 were waited for; matrix products, arithmetic and copies ran while one was open for 15% of the time, Pallas kernels for 40%

profile of v3, /device:TPU:0, one launch (start us, length us, event | category | flops | bytes accessed | tf_op | source)
XLA Modules:
  0.0 564.1 jit_solution(8711586868299158455)
XLA Ops:
  11.7 3.1 collective-permute-start
  14.7 2.6 collective-permute-start.1
  18.7 2.4 shard_map.350
  26.1 4.4 shard_map.348.refs_0_
  30.5 4.6 shard_map.349.refs_2_.refs_3_
  36.6 3.3 collective-permute-start.7
  40.0 3.0 collective-permute-start.8
  45.3 6.4 %collective-permute-done.7 = bf16[1,4,16,1536]{3,2,1,0:T(8,128)(2,1)S(1)} collective-permute-done((bf16[1,4,16,1536]{3,2,1,0:T(8,128)(2,1)}, bf16[1,4,16,1536]{3,2,1,0:T(8,128)(2,1)S(1)}, u32[]{:S(2)}, u32[]{:S(2)}) %collective-permute-start.7) | collective-permute-done | bytes 196640 | tf_op jit(solution)/shard_map/ppermute | solution.py:617
  53.2 7.1 %collective-permute-done.8 = bf16[1,4,16,1536]{3,2,1,0:T(8,128)(2,1)S(1)} collective-permute-done((bf16[1,4,16,1536]{3,2,1,0:T(8,128)(2,1)}, bf16[1,4,16,1536]{3,2,1,0:T(8,128)(2,1)S(1)}, u32[]{:S(2)}, u32[]{:S(2)}) %collective-permute-start.8) | collective-permute-done | bytes 196640 | tf_op jit(solution)/shard_map/ppermute | solution.py:617
  63.7 11.9 %collective-permute-done.5.refs_4_ = bf16[2,1,96,768]{3,2,1,0:T(8,128)(2,1)S(1)} collective-permute-done((bf16[2,1,96,768]{3,2,1,0:T(8,128)(2,1)S(1)}, bf16[2,1,96,768]{3,2,1,0:T(8,128)(2,1)S(1)}, u32[]{:S(2)}, u32[]{:S(2)}) %collective-permute-start.5) | collective-permute-done | bytes 294944 | tf_op jit(solution)/shard_map/ppermute | solution.py:621
  75.5 11.2 %collective-permute-done.6.refs_5_ = bf16[2,1,96,768]{3,2,1,0:T(8,128)(2,1)S(1)} collective-permute-done((bf16[2,1,96,768]{3,2,1,0:T(8,128)(2,1)S(1)}, bf16[2,1,96,768]{3,2,1,0:T(8,128)(2,1)S(1)}, u32[]{:S(2)}, u32[]{:S(2)}) %collective-permute-start.6) | collective-permute-done | bytes 294944 | tf_op jit(solution)/shard_map/ppermute | solution.py:621
  92.5 2.0 pad_maximum_fusion.mem_ref
  96.6 3.9 shard_map.351
  110.7 3.0 fusion.10.q_ref.k_ref.v_ref
  113.7 15.4 %collective-permute-done.16.refs_3_ = bf16[2,1,4,16,1536]{4,3,2,1,0:T(8,128)(2,1)} collective-permute-done((bf16[2,1,4,16,1536]{4,3,2,1,0:T(8,128)(2,1)S(1)}, bf16[2,1,4,16,1536]{4,3,2,1,0:T(8,128)(2,1)}, u32[]{:S(2)}, u32[]{:S(2)}) %collective-permute-start.16) | collective-permute-done | bytes 393248 | tf_op jit(solution)/shard_map/ppermute | solution.py:621
  129.1 4.1 collective-permute-done.18.refs_5_
  133.2 2.6 collective-permute-start.20
  139.4 8.1 %shard_map.352 = (bf16[192,1024]{1,0:T(8,128)(2,1)}, f32[3,1,1024]{2,1,0:T(1,128)}) custom-call(bf16[576,1024]{1,0:T(8,128)(2,1)} %fusion.10.q_ref.k_ref.v_ref, bf16[576,1024]{1,0:T(8,128)(2,1)} %fusion.10.q_ref.k_ref.v_ref, bf16[576,1024]{1,0:T(8,128)(2,1)} %fusion.10.q_ref.k_ref.v_ref, s32[1,1024]{1,0:T(1,128)} %bitcast.183, s32[1024,1]{1,0:T(8,128)} %copy.66.segc_ref, ...), custom_call_target="tpu_custom_call" | custom-call | flops 805306368 | bytes 4194304 | tf_op jit(solution)/shard_map/pallas_call | solution.py:164
  147.5 4.9 collective-permute-done.19.refs_6_
  153.1 4.6 shard_map.353
  159.9 2.7 broadcast_select_fusion.1
  167.2 2.0 copy-done.1
  169.2 8.0 %shard_map.354.refs_4_.key_map.value_map = bf16[4,384,1536]{2,1,0:T(8,128)(2,1)} custom-call(bf16[384,256]{1,0:T(8,128)(2,1)} %get-tuple-element.510.own_map, bf16[384,256]{1,0:T(8,128)(2,1)} %get-tuple-element.509.other_map, bf16[16,4,16,1536]{3,2,1,0:T(8,128)(2,1)} %bitcast.153, bf16[16,4,16,1536]{3,2,1,0:T(8,128)(2,1)} %collective-permute-done.22.other_ref), custom_call_target="tpu_custom_call" | custom-call | flops 2415919104 | bytes 12582912 | tf_op jit(solution)/shard_map/pallas_call | solution.py:427
  177.3 2.8 convolution_convert_fusion.3.q_ref
  181.4 2.3 convolution_convert_fusion.k_ref.v_ref
  183.7 12.5 %shard_map.355 = (bf16[192,1024]{1,0:T(8,128)(2,1)}, f32[3,1,1024]{2,1,0:T(1,128)}) custom-call(bf16[192,1024]{1,0:T(8,128)(2,1)} %convolution_convert_fusion.3.q_ref, bf16[384,1024]{1,0:T(8,128)(2,1)} %convolution_convert_fusion.k_ref.v_ref, bf16[384,1024]{1,0:T(8,128)(2,1)} %convolution_convert_fusion.k_ref.v_ref, f32[1024,1]{1,0:T(8,128)} %broadcast_select_fusion.10.keep_ref), custom_call_target="tpu_custom_call" | custom-call | flops 805306368 | bytes 4194304 | tf_op jit(solution)/shard_map/pallas_call | solution.py:164
  199.4 5.2 multiply_reduce_fusion
  204.7 2.6 copy-done
  207.2 2.3 multiply_convert_fusion.refs_1_
  209.5 57.3 %shard_map.356 = (f32[1536,1024]{1,0:T(8,128)}, f32[1536,1024]{1,0:T(8,128)}, bf16[16,3,96,1408]{3,2,1,0:T(8,128)(2,1)}) custom-call(s32[16]{0:T(128)} %stack.102.owners_ref.refs_0_, bf16[1536,1024]{1,0:T(8,128)(2,1)} %multiply_convert_fusion.refs_1_, bf16[1536,1024]{1,0:T(8,128)(2,1)} %shard_map.349.refs_2_.refs_3_, bf16[16,3,96,1408]{3,2,1,0:T(8,128)(2,1)} %bitcast.187), custom_call_target="tpu_custom_call" | custom-call | flops 39862665216 | bytes 33554432 | tf_op jit(solution)/shard_map/pallas_call | solution.py:345
  266.9 14.3 %all-gather.5.cloned.1.call-done = bf16[48,96,384]{2,1,0:T(8,128)(2,1)} async-done(((bf16[3,96,384]{2,1,0:T(8,128)(2,1)}), bf16[48,96,384]{2,1,0:T(8,128)(2,1)}) %all-gather.5.cloned.1.call-update) | async-done | bytes 3538960 | tf_op jit(solution)/shard_map/all_gather | solution.py:804
  281.2 22.3 %shard_map.357 = (bf16[1536,1024]{1,0:T(8,128)(2,1)}, bf16[1536,1024]{1,0:T(8,128)(2,1)}, bf16[2,3,96,384]{3,2,1,0:T(8,128)(2,1)}, bf16[2,3,96,384]{3,2,1,0:T(8,...) custom-call(s32[16]{0:T(128)} %stack.102.owners_ref.refs_0_, ...), custom_call_target="tpu_custom_call" | custom-call | flops 10871635968 | bytes 33554432 | tf_op jit(solution)/shard_map/pallas_call | solution.py:345
  303.6 5.9 %collective-permute-done.24.refs_5_ = bf16[1536,1024]{1,0:T(8,128)(2,1)S(1)} collective-permute-done((bf16[1536,1024]{1,0:T(8,128)(2,1)}, bf16[1536,1024]{1,0:T(8,128)(2,1)S(1)}, u32[]{:S(2)}, u32[]{:S(2)}) %collective-permute-start.24) | collective-permute-done | bytes 3145760 | tf_op jit(solution)/shard_map/ppermute | solution.py:734
  312.7 10.9 %shard_map.358 = (bf16[1536,1024]{1,0:T(8,128)(2,1)}, f32[1536,1]{1,0:T(8,128)}) custom-call(f32[1536,1024]{1,0:T(8,128)} %copy-done, f32[1,1024]{1,0:T(1,128)} %bitcast.177, f32[1536,1]{1,0:T(8,128)} %copy.67.refs_2_, bf16[1536,1024]{1,0:T(8,128)(2,1)} %shard_map.349.refs_2_.refs_3_, bf16[1536,1024]{1,0:T(8,128)(2,1)} %get-tuple-element.318.refs_4_, ...), custom_call_target="tpu_custom_call" | custom-call | flops 18874368 | bytes 31457280 | tf_op jit(solution)/shard_map/pallas_call | solution.py:604
  323.7 3.4 collective-permute-done.25
  329.8 1.9 add_convert_fusion
  331.7 3.7 convolution_convert_fusion.2.do_ref
  335.4 14.9 %shard_map.359.own_ref = bf16[3,192,1024]{2,1,0:T(8,128)(2,1)} custom-call(bf16[192,1024]{1,0:T(8,128)(2,1)} %convolution_convert_fusion.3.q_ref, bf16[384,1024]{1,0:T(8,128)(2,1)} %convolution_convert_fusion.k_ref.v_ref, bf16[384,1024]{1,0:T(8,128)(2,1)} %convolution_convert_fusion.k_ref.v_ref, bf16[192,1024]{1,0:T(8,128)(2,1)} %convolution_convert_fusion.2.do_ref, ...), custom_call_target="tpu_custom_call" | custom-call | flops 2013265920 | bytes 4194304 | tf_op jit(solution)/shard_map/pallas_call | solution.py:164
  350.3 1.9 add_convert_fusion.1
  358.5 10.5 %shard_map.360 = (bf16[1536,1024]{1,0:T(8,128)(2,1)}, f32[1536,1]{1,0:T(8,128)}) custom-call(f32[1536,1024]{1,0:T(8,128)} %copy-done.1, f32[1,1024]{1,0:T(1,128)} %bitcast.176, f32[1536,1]{1,0:T(8,128)} %copy.68.refs_2_, bf16[1536,1024]{1,0:T(8,128)(2,1)} %get-tuple-element.326.refs_3_.g_ref, bf16[4,384,1536]{2,1,0:T(8,128)(2,1)} %shard_map.354.refs_4_.key_map.value_map, ...), custom_call_target="tpu_custom_call" | custom-call | flops 1226833920 | bytes 31457280 | tf_op jit(solution)/shard_map/pallas_call | solution.py:604
  370.9 2.0 collective-permute-start.32
  374.6 3.8 convolution_convert_fusion.1.do_ref
  378.4 11.5 %shard_map.361 = (bf16[2,1,4,16,1536]{4,3,2,1,0:T(8,128)(2,1)}, bf16[2,1,4,16,1536]{4,3,2,1,0:T(8,128)(2,1)}, bf16[2,1,4,16,1536]{4,3,2,1,0:T(8,128)(2,1)}, bf16...) custom-call(s32[16]{0:T(128)} %stack.102.owners_ref.refs_0_, ...), custom_call_target="tpu_custom_call" | custom-call | flops 3221225472 | bytes 16777216 | tf_op jit(solution)/shard_map/pallas_call | solution.py:458
  389.9 2.3 collective-permute-done.33
  396.4 13.7 %shard_map.362 = (bf16[3,192,1024]{2,1,0:T(8,128)(2,1)}, f32[3,3,512]{2,1,0:T(4,128)}) custom-call(bf16[576,1024]{1,0:T(8,128)(2,1)} %fusion.10.q_ref.k_ref.v_ref, bf16[576,1024]{1,0:T(8,128)(2,1)} %fusion.10.q_ref.k_ref.v_ref, bf16[576,1024]{1,0:T(8,128)(2,1)} %fusion.10.q_ref.k_ref.v_ref, bf16[192,1024]{1,0:T(8,128)(2,1)} %convolution_convert_fusion.1.do_ref, ...), custom_call_target="tpu_custom_call" | custom-call | flops 2013265920 | bytes 4194304 | tf_op jit(solution)/shard_map/pallas_call | solution.py:164
  410.3 8.9 %collective-permute-done.37 = bf16[2,1,4,16,1536]{4,3,2,1,0:T(8,128)(2,1)S(1)} collective-permute-done((bf16[2,1,4,16,1536]{4,3,2,1,0:T(8,128)(2,1)}, bf16[2,1,4,16,1536]{4,3,2,1,0:T(8,128)(2,1)S(1)}, u32[]{:S(2)}, u32[]{:S(2)}) %collective-permute-start.37) | collective-permute-done | bytes 393248 | tf_op jit(solution)/shard_map/ppermute | solution.py:621
  424.3 8.3 %shard_map.363 = (bf16[2,1,96,768]{3,2,1,0:T(8,128)(2,1)}, bf16[2,1,96,768]{3,2,1,0:T(8,128)(2,1)}, bf16[2,1,96,768]{3,2,1,0:T(8,128)(2,1)}, bf16[2,1,96,768]{3,...) custom-call(s32[16]{0:T(128)} %stack.102.owners_ref.refs_0_, ...), custom_call_target="tpu_custom_call" | custom-call | flops 2415919104 | bytes 12582912 | tf_op jit(solution)/shard_map/pallas_call | solution.py:489
  433.8 1.8 collective-permute-done.41
  435.6 1.9 fusion.39
  437.5 1.9 fusion.40
  445.1 13.6 %shard_map.364 = (f32[1472,1024]{1,0:T(8,128)}, f32[1536,1]{1,0:T(8,128)}) custom-call(bf16[1536,1024]{1,0:T(8,128)(2,1)} %shard_map.348.refs_0_, f32[1,1024]{1,0:T(1,128)} %bitcast.178, f32[1536,1]{1,0:T(8,128)} %copy.70.refs_2_, bf16[1536,1024]{1,0:T(8,128)(2,1)} %get-tuple-element.348.g_ref.refs_3_, bf16[1536,768]{1,0:T(8,128)(2,1)} %copy-done.5, ...), custom_call_target="tpu_custom_call" | custom-call | flops 3642753024 | bytes 31457280 | tf_op jit(solution)/shard_map/pallas_call | solution.py:604
  460.2 1.8 add_convert_fusion.5
  469.2 3.4 collective-permute-done.47
  474.3 5.3 shard_map.365
  479.6 5.7 %collective-permute-done.48 = bf16[1,4,16,1536]{3,2,1,0:T(8,128)(2,1)} collective-permute-done((bf16[1,4,16,1536]{3,2,1,0:T(8,128)(2,1)}, bf16[1,4,16,1536]{3,2,1,0:T(8,128)(2,1)}, u32[]{:S(2)}, u32[]{:S(2)}) %collective-permute-start.48) | collective-permute-done | bytes 196640 | tf_op jit(solution)/shard_map/ppermute | solution.py:617
  487.0 1.9 collective-permute-start.54
  491.4 7.3 %shard_map.366 = bf16[1472,1024]{1,0:T(8,128)(2,1)} custom-call(f32[1536,1024]{1,0:T(8,128)} %copy-done, bf16[1536,1024]{1,0:T(8,128)(2,1)} %get-tuple-element.427.own_ref, bf16[1536,1024]{1,0:T(8,128)(2,1)} %collective-permute-done.46.other_ref), custom_call_target="tpu_custom_call" | custom-call | flops 6291456 | bytes 15728640 | tf_op jit(solution)/shard_map/pallas_call | solution.py:536
  499.2 8.0 %collective-permute-done.53 = bf16[1,96,768]{2,1,0:T(8,128)(2,1)S(1)} collective-permute-done((bf16[1,96,768]{2,1,0:T(8,128)(2,1)S(1)}, bf16[1,96,768]{2,1,0:T(8,128)(2,1)S(1)}, u32[]{:S(2)}, u32[]{:S(2)}) %collective-permute-start.53) | collective-permute-done | bytes 147488 | tf_op jit(solution)/shard_map/ppermute | solution.py:617
  508.4 11.1 %reduce-scatter.2.cloned.1.call-done = bf16[1,3,96,1408]{3,2,1,0:T(8,128)(2,1)} async-done(((bf16[16,3,96,1408]{3,2,1,0:T(8,128)(2,1)}), bf16[1,3,96,1408]{3,2,1,0:T(8,128)(2,1)}) %reduce-scatter.2.cloned.1.call-update) | async-done | bytes 811024 | tf_op jit(solution)/shard_map/reduce_scatter | solution.py:688
  530.7 2.4 collective-permute-done.58
  533.1 2.2 collective-permute-start.59
  535.3 2.1 collective-permute-start.60
  539.1 1.8 collective-permute-done.60
  545.7 6.7 %multiply_subtract_fusion = (f32[3,1792,92]{1,2,0:T(8,128)}, f32[3,1792,92]{1,2,0:T(8,128)}, f32[3,1792,92]{1,2,0:T(8,128)}) fusion(f32[3,1792,92]{1,2,0:T(8,128)S(1)} %copy-done.8, f32[3,1792,92]{1,2,0:T(8,128)} %fusion.4, f32[]{:T(128)} %bitcast.83, f32[3,1792,92]{1,2,0:T(8,128)} %param.38, f32[3,1792,92]{1,2,0:T(8,128)} %param.39), kind=kLoop, calls=%fused_computation.23 | loop fusion | flops 7913472 | bytes 13848580 | tf_op jit(solution)/shard_map/sub | solution.py:727
  (376 shorter events, 118.3 us)
Async XLA Ops:
  7.2 202.3 %all-gather.7.cloned.1.call-start = ((), (), s32[]{:S(2)}) async-start(), calls=%async_computation.3 | async-start | bytes 13787136 | tf_op jit(solution)/shard_map/all_gather | solution.py:804
  11.0 270.3 %all-gather.5.cloned.1.call-start = ((), (), s32[]{:S(2)}) async-start(), calls=%async_computation.2 | async-start | bytes 3760128 | tf_op jit(solution)/shard_map/all_gather | solution.py:804
  11.7 23.8 %collective-permute-start = (bf16[1,96,768]{2,1,0:T(8,128)(2,1)S(1)}, bf16[1,96,768]{2,1,0:T(8,128)(2,1)}, u32[]{:S(2)}, u32[]{:S(2)}) collective-permute-start(bf16[1,96,768]{2,1,0:T(8,128)(2,1)S(1)} %bitcast.168), channel_id=1, source_target_pairs={{0,8},{2,10},{4,12},{6,14},{8,16},{10,18},{12,20},{14,22},{16,24},... | collective-permute-start | bytes 442376 | tf_op jit(solution)/shard_map/ppermute | solution.py:617
  14.7 20.7 %collective-permute-start.1 = (bf16[1,96,768]{2,1,0:T(8,128)(2,1)S(1)}, bf16[1,96,768]{2,1,0:T(8,128)(2,1)}, u32[]{:S(2)}, u32[]{:S(2)}) collective-permute-start(bf16[1,96,768]{2,1,0:T(8,128)(2,1)S(1)} %bitcast.169), channel_id=1, source_target_pairs={{0,16},{2,18},{4,20},{6,22},{8,24},{10,26},{12,28},{14,30},{16,0},... | collective-permute-start | bytes 442376 | tf_op jit(solution)/shard_map/ppermute | solution.py:617
  17.3 18.1 %collective-permute-start.2 = (bf16[1,96,768]{2,1,0:T(8,128)(2,1)S(1)}, bf16[1,96,768]{2,1,0:T(8,128)(2,1)}, u32[]{:S(2)}, u32[]{:S(2)}) collective-permute-start(bf16[1,96,768]{2,1,0:T(8,128)(2,1)S(1)} %bitcast.170), channel_id=1, source_target_pairs={{0,24},{2,26},{4,28},{6,30},{8,0},{10,2},{12,4},{14,6},{16,8},{18,... | collective-permute-start | bytes 442376 | tf_op jit(solution)/shard_map/ppermute | solution.py:617
  21.1 69.8 %collective-permute-start.10 = (bf16[1536,512]{1,0:T(8,128)(2,1)}, bf16[1536,512]{1,0:T(8,128)(2,1)}, u32[]{:S(2)}, u32[]{:S(2)}) collective-permute-start(bf16[1536,512]{1,0:T(8,128)(2,1)} %shard_map.350), channel_id=1, source_target_pairs={{0,1},{1,0},{2,3},{3,2},{4,5},{5,4},{6,7},{7,6},{8,9},{9,8},{10,11... | collective-permute-start | bytes 4718600 | tf_op jit(solution)/shard_map/ppermute | solution.py:734
  21.1 14.0 %collective-permute-start.11 = (s32[512]{0:T(512)S(1)}, s32[512]{0:T(512)S(1)}, u32[]{:S(2)}, u32[]{:S(2)}) collective-permute-start(s32[512]{0:T(512)S(1)} %bitcast.185), channel_id=1, source_target_pairs={{0,1},{1,0},{2,3},{3,2},{4,5},{5,4},{6,7},{7,6},{8,9},{9,8},{10,11... | collective-permute-start | bytes 6152 | tf_op jit(solution)/shard_map/ppermute | solution.py:734
  36.6 15.1 %collective-permute-start.7 = (bf16[1,4,16,1536]{3,2,1,0:T(8,128)(2,1)}, bf16[1,4,16,1536]{3,2,1,0:T(8,128)(2,1)S(1)}, u32[]{:S(2)}, u32[]{:S(2)}) collective-permute-start(bf16[1,4,16,1536]{3,2,1,0:T(8,128)(2,1)} %get-tuple-element.264), channel_id=1, source_target_pairs={{0,8},{2,10},{4,12},{6,14},{8,16},{10,18},{12,20},{14,22},{16,24},... | collective-permute-start | bytes 589832 | tf_op jit(solution)/shard_map/ppermute | solution.py:617
  40.0 20.3 %collective-permute-start.8 = (bf16[1,4,16,1536]{3,2,1,0:T(8,128)(2,1)}, bf16[1,4,16,1536]{3,2,1,0:T(8,128)(2,1)S(1)}, u32[]{:S(2)}, u32[]{:S(2)}) collective-permute-start(bf16[1,4,16,1536]{3,2,1,0:T(8,128)(2,1)} %get-tuple-element.264), channel_id=1, source_target_pairs={{0,16},{2,18},{4,20},{6,22},{8,24},{10,26},{12,28},{14,30},{16,0},... | collective-permute-start | bytes 589832 | tf_op jit(solution)/shard_map/ppermute | solution.py:617
  42.9 18.9 %collective-permute-start.9 = (bf16[1,4,16,1536]{3,2,1,0:T(8,128)(2,1)}, bf16[1,4,16,1536]{3,2,1,0:T(8,128)(2,1)S(1)}, u32[]{:S(2)}, u32[]{:S(2)}) collective-permute-start(bf16[1,4,16,1536]{3,2,1,0:T(8,128)(2,1)} %get-tuple-element.264), channel_id=1, source_target_pairs={{0,24},{2,26},{4,28},{6,30},{8,0},{10,2},{12,4},{14,6},{16,8},{18,... | collective-permute-start | bytes 589832 | tf_op jit(solution)/shard_map/ppermute | solution.py:617
  43.8 19.9 %collective-permute-start.3 = (bf16[2,1,96,768]{3,2,1,0:T(8,128)(2,1)S(1)}, bf16[2,1,96,768]{3,2,1,0:T(8,128)(2,1)S(1)}, u32[]{:S(2)}, u32[]{:S(2)}) collective-permute-start(bf16[2,1,96,768]{3,2,1,0:T(8,128)(2,1)S(1)} %get-tuple-element.260.refs_0_), channel_id=1, source_target_pairs={{0,2},{2,0},{4,6},{6,4},{8,10},{10,8},{12,14},{14,12},{16,18},{18,... | collective-permute-start | bytes 884744 | tf_op jit(solution)/shard_map/ppermute | solution.py:621
  51.7 12.0 %collective-permute-start.4 = (bf16[2,1,96,768]{3,2,1,0:T(8,128)(2,1)S(1)}, bf16[2,1,96,768]{3,2,1,0:T(8,128)(2,1)S(1)}, u32[]{:S(2)}, u32[]{:S(2)}) collective-permute-start(bf16[2,1,96,768]{3,2,1,0:T(8,128)(2,1)S(1)} %get-tuple-element.261.refs_1_), channel_id=1, source_target_pairs={{0,2},{2,0},{4,6},{6,4},{8,10},{10,8},{12,14},{14,12},{16,18},{18,... | collective-permute-start | bytes 884744 | tf_op jit(solution)/shard_map/ppermute | solution.py:621
  60.3 15.2 %collective-permute-start.5 = (bf16[2,1,96,768]{3,2,1,0:T(8,128)(2,1)S(1)}, bf16[2,1,96,768]{3,2,1,0:T(8,128)(2,1)S(1)}, u32[]{:S(2)}, u32[]{:S(2)}) collective-permute-start(bf16[2,1,96,768]{3,2,1,0:T(8,128)(2,1)S(1)} %get-tuple-element.260.refs_0_), channel_id=1, source_target_pairs={{0,4},{2,6},{4,0},{6,2},{8,12},{10,14},{12,8},{14,10},{16,20},{18,... | collective-permute-start | bytes 884744 | tf_op jit(solution)/shard_map/ppermute | solution.py:621
  61.8 24.9 %collective-permute-start.6 = (bf16[2,1,96,768]{3,2,1,0:T(8,128)(2,1)S(1)}, bf16[2,1,96,768]{3,2,1,0:T(8,128)(2,1)S(1)}, u32[]{:S(2)}, u32[]{:S(2)}) collective-permute-start(bf16[2,1,96,768]{3,2,1,0:T(8,128)(2,1)S(1)} %get-tuple-element.261.refs_1_), channel_id=1, source_target_pairs={{0,4},{2,6},{4,0},{6,2},{8,12},{10,14},{12,8},{14,10},{16,20},{18,... | collective-permute-start | bytes 884744 | tf_op jit(solution)/shard_map/ppermute | solution.py:621
  87.6 6.9 %collective-permute-start.12 = (bf16[2,1,96,768]{3,2,1,0:T(8,128)(2,1)S(1)}, bf16[2,1,96,768]{3,2,1,0:T(8,128)(2,1)S(1)}, u32[]{:S(2)}, u32[]{:S(2)}) collective-permute-start(bf16[2,1,96,768]{3,2,1,0:T(8,128)(2,1)S(1)} %collective-permute-done.5.refs_4_), channel_id=1, source_target_pairs={{0,2},{2,0},{4,6},{6,4},{8,10},{10,8},{12,14},{14,12},{16,18},{18,... | collective-permute-start | bytes 884744 | tf_op jit(solution)/shard_map/ppermute | solution.py:621
  89.2 6.7 %collective-permute-start.13 = (bf16[2,1,96,768]{3,2,1,0:T(8,128)(2,1)S(1)}, bf16[2,1,96,768]{3,2,1,0:T(8,128)(2,1)S(1)}, u32[]{:S(2)}, u32[]{:S(2)}) collective-permute-start(bf16[2,1,96,768]{3,2,1,0:T(8,128)(2,1)S(1)} %collective-permute-done.4.refs_3_), channel_id=1, source_target_pairs={{0,4},{2,6},{4,0},{6,2},{8,12},{10,14},{12,8},{14,10},{16,20},{18,... | collective-permute-start | bytes 884744 | tf_op jit(solution)/shard_map/ppermute | solution.py:621
  100.5 59.4 %collective-permute-start.14 = (bf16[1536,768]{1,0:T(8,128)(2,1)}, bf16[1536,768]{1,0:T(8,128)(2,1)}, u32[]{:S(2)}, u32[]{:S(2)}) collective-permute-start(bf16[1536,768]{1,0:T(8,128)(2,1)} %bitcast.154), channel_id=1, source_target_pairs={{0,1},{1,0},{2,3},{3,2},{4,5},{5,4},{6,7},{7,6},{8,9},{9,8},{10,11... | collective-permute-start | bytes 7077896 | tf_op jit(solution)/shard_map/ppermute | solution.py:734
  100.6 13.1 %collective-permute-start.15 = (bf16[2,1,4,16,1536]{4,3,2,1,0:T(8,128)(2,1)}, bf16[2,1,4,16,1536]{4,3,2,1,0:T(8,128)(2,1)}, u32[]{:S(2)}, u32[]{:S(2)}) collective-permute-start(bf16[2,1,4,16,1536]{4,3,2,1,0:T(8,128)(2,1)} %pad_maximum_fusion.4.refs_0_), channel_id=1, source_target_pairs={{0,2},{2,0},{4,6},{6,4},{8,10},{10,8},{12,14},{14,12},{16,18},{18,... | collective-permute-start | bytes 1179656 | tf_op jit(solution)/shard_map/ppermute | solution.py:621
  101.4 27.7 %collective-permute-start.16 = (bf16[2,1,4,16,1536]{4,3,2,1,0:T(8,128)(2,1)S(1)}, bf16[2,1,4,16,1536]{4,3,2,1,0:T(8,128)(2,1)}, u32[]{:S(2)}, u32[]{:S(2)}) collective-permute-start(bf16[2,1,4,16,1536]{4,3,2,1,0:T(8,128)(2,1)S(1)} %pad_maximum_fusion.5.refs_1_), channel_id=1, source_target_pairs={{0,2},{2,0},{4,6},{6,4},{8,10},{10,8},{12,14},{14,12},{16,18},{18,... | collective-permute-start | bytes 1179656 | tf_op jit(solution)/shard_map/ppermute | solution.py:621
  102.7 26.4 %collective-permute-start.17 = (bf16[2,1,4,16,1536]{4,3,2,1,0:T(8,128)(2,1)}, bf16[2,1,4,16,1536]{4,3,2,1,0:T(8,128)(2,1)}, u32[]{:S(2)}, u32[]{:S(2)}) collective-permute-start(bf16[2,1,4,16,1536]{4,3,2,1,0:T(8,128)(2,1)} %pad_maximum_fusion.4.refs_0_), channel_id=1, source_target_pairs={{0,4},{2,6},{4,0},{6,2},{8,12},{10,14},{12,8},{14,10},{16,20},{18,... | collective-permute-start | bytes 1179656 | tf_op jit(solution)/shard_map/ppermute | solution.py:621
  104.4 28.8 %collective-permute-start.18 = (bf16[2,1,4,16,1536]{4,3,2,1,0:T(8,128)(2,1)S(1)}, bf16[2,1,4,16,1536]{4,3,2,1,0:T(8,128)(2,1)}, u32[]{:S(2)}, u32[]{:S(2)}) collective-permute-start(bf16[2,1,4,16,1536]{4,3,2,1,0:T(8,128)(2,1)S(1)} %pad_maximum_fusion.5.refs_1_), channel_id=1, source_target_pairs={{0,4},{2,6},{4,0},{6,2},{8,12},{10,14},{12,8},{14,10},{16,20},{18,... | collective-permute-start | bytes 1179656 | tf_op jit(solution)/shard_map/ppermute | solution.py:621
  133.2 19.2 %collective-permute-start.19 = (bf16[2,1,4,16,1536]{4,3,2,1,0:T(8,128)(2,1)}, bf16[2,1,4,16,1536]{4,3,2,1,0:T(8,128)(2,1)S(1)}, u32[]{:S(2)}, u32[]{:S(2)}) collective-permute-start(bf16[2,1,4,16,1536]{4,3,2,1,0:T(8,128)(2,1)} %collective-permute-done.17.refs_4_), channel_id=1, source_target_pairs={{0,2},{2,0},{4,6},{6,4},{8,10},{10,8},{12,14},{14,12},{16,18},{18,... | collective-permute-start | bytes 1179656 | tf_op jit(solution)/shard_map/ppermute | solution.py:621
  133.2 19.9 %collective-permute-start.20 = (bf16[2,1,4,16,1536]{4,3,2,1,0:T(8,128)(2,1)}, bf16[2,1,4,16,1536]{4,3,2,1,0:T(8,128)(2,1)}, u32[]{:S(2)}, u32[]{:S(2)}) collective-permute-start(bf16[2,1,4,16,1536]{4,3,2,1,0:T(8,128)(2,1)} %collective-permute-done.16.refs_3_), channel_id=1, source_target_pairs={{0,4},{2,6},{4,0},{6,2},{8,12},{10,14},{12,8},{14,10},{16,20},{18,... | collective-permute-start | bytes 1179656 | tf_op jit(solution)/shard_map/ppermute | solution.py:621
  137.4 382.0 %reduce-scatter.2.cloned.1.call-start = ((), (), s32[]{:S(2)}) async-start(), calls=%async_computation.1 | async-start | bytes 13787136 | tf_op jit(solution)/shard_map/reduce_scatter | solution.py:688
  157.7 11.5 %collective-permute-start.22 = (bf16[16,4,16,1536]{3,2,1,0:T(8,128)(2,1)}, bf16[16,4,16,1536]{3,2,1,0:T(8,128)(2,1)}, u32[]{:S(2)}, u32[]{:S(2)}) collective-permute-start(bf16[16,4,16,1536]{3,2,1,0:T(8,128)(2,1)} %bitcast.152), channel_id=1, source_target_pairs={{0,1},{1,0},{2,3},{3,2},{4,5},{5,4},{6,7},{7,6},{8,9},{9,8},{10,11... | collective-permute-start | bytes 9437192 | tf_op jit(solution)/shard_map/ppermute | solution.py:734
  159.4 4.5 collective-permute-start.21
  196.2 2.0 collective-permute-start.23
  303.6 5.9 %collective-permute-start.24 = (bf16[1536,1024]{1,0:T(8,128)(2,1)}, bf16[1536,1024]{1,0:T(8,128)(2,1)S(1)}, u32[]{:S(2)}, u32[]{:S(2)}) collective-permute-start(bf16[1536,1024]{1,0:T(8,128)(2,1)} %get-tuple-element.318.refs_4_), channel_id=1, source_target_pairs={{0,1},{1,0},{2,3},{3,2},{4,5},{5,4},{6,7},{7,6},{8,9},{9,8},{10,11... | collective-permute-start | bytes 9437192 | tf_op jit(solution)/shard_map/ppermute | solution.py:734
  309.5 17.6 %collective-permute-start.25 = (bf16[2,3,96,384]{3,2,1,0:T(8,128)(2,1)}, bf16[2,3,96,384]{3,2,1,0:T(8,128)(2,1)}, u32[]{:S(2)}, u32[]{:S(2)}) collective-permute-start(bf16[2,3,96,384]{3,2,1,0:T(8,128)(2,1)} %get-tuple-element.321), channel_id=1, source_target_pairs={{0,2},{2,0},{4,6},{6,4},{8,10},{10,8},{12,14},{14,12},{16,18},{18,... | collective-permute-start | bytes 1327112 | tf_op jit(solution)/shard_map/ppermute | solution.py:621
  311.0 16.8 %collective-permute-start.26 = (bf16[2,3,96,384]{3,2,1,0:T(8,128)(2,1)}, bf16[2,3,96,384]{3,2,1,0:T(8,128)(2,1)}, u32[]{:S(2)}, u32[]{:S(2)}) collective-permute-start(bf16[2,3,96,384]{3,2,1,0:T(8,128)(2,1)} %get-tuple-element.322), channel_id=1, source_target_pairs={{0,4},{2,6},{4,0},{6,2},{8,12},{10,14},{12,8},{14,10},{16,20},{18,... | collective-permute-start | bytes 1327112 | tf_op jit(solution)/shard_map/ppermute | solution.py:621
  327.8 24.5 %collective-permute-start.27 = (bf16[2,3,96,384]{3,2,1,0:T(8,128)(2,1)}, bf16[2,3,96,384]{3,2,1,0:T(8,128)(2,1)S(1)}, u32[]{:S(2)}, u32[]{:S(2)}) collective-permute-start(bf16[2,3,96,384]{3,2,1,0:T(8,128)(2,1)} %get-tuple-element.328), channel_id=1, source_target_pairs={{0,2},{2,0},{4,6},{6,4},{8,10},{10,8},{12,14},{14,12},{16,18},{18,... | collective-permute-start | bytes 1327112 | tf_op jit(solution)/shard_map/ppermute | solution.py:621
  328.8 23.4 %collective-permute-start.28 = (bf16[2,3,96,384]{3,2,1,0:T(8,128)(2,1)}, bf16[2,3,96,384]{3,2,1,0:T(8,128)(2,1)S(1)}, u32[]{:S(2)}, u32[]{:S(2)}) collective-permute-start(bf16[2,3,96,384]{3,2,1,0:T(8,128)(2,1)} %get-tuple-element.329), channel_id=1, source_target_pairs={{0,4},{2,6},{4,0},{6,2},{8,12},{10,14},{12,8},{14,10},{16,20},{18,... | collective-permute-start | bytes 1327112 | tf_op jit(solution)/shard_map/ppermute | solution.py:621
  352.3 4.0 collective-permute-start.29
  354.3 15.4 %collective-permute-start.30 = (bf16[2,3,96,384]{3,2,1,0:T(8,128)(2,1)}, bf16[2,3,96,384]{3,2,1,0:T(8,128)(2,1)S(1)}, u32[]{:S(2)}, u32[]{:S(2)}) collective-permute-start(bf16[2,3,96,384]{3,2,1,0:T(8,128)(2,1)} %add_convert_fusion.1), channel_id=1, source_target_pairs={{0,2},{2,0},{4,6},{6,4},{8,10},{10,8},{12,14},{14,12},{16,18},{18,... | collective-permute-start | bytes 1327112 | tf_op jit(solution)/shard_map/ppermute | solution.py:621
  355.0 14.6 %collective-permute-start.31 = (bf16[2,3,96,384]{3,2,1,0:T(8,128)(2,1)}, bf16[2,3,96,384]{3,2,1,0:T(8,128)(2,1)}, u32[]{:S(2)}, u32[]{:S(2)}) collective-permute-start(bf16[2,3,96,384]{3,2,1,0:T(8,128)(2,1)} %add_convert_fusion), channel_id=1, source_target_pairs={{0,4},{2,6},{4,0},{6,2},{8,12},{10,14},{12,8},{14,10},{16,20},{18,... | collective-permute-start | bytes 1327112 | tf_op jit(solution)/shard_map/ppermute | solution.py:621
  370.9 19.0 %collective-permute-start.32 = (bf16[3,96,384]{2,1,0:T(8,128)(2,1)S(1)}, bf16[3,96,384]{2,1,0:T(8,128)(2,1)S(1)}, u32[]{:S(2)}, u32[]{:S(2)}) collective-permute-start(bf16[3,96,384]{2,1,0:T(8,128)(2,1)S(1)} %fusion.33), channel_id=1, source_target_pairs={{0,24},{2,26},{4,28},{6,30},{8,0},{10,2},{12,4},{14,6},{16,8},{18,... | collective-permute-start | bytes 663560 | tf_op jit(solution)/shard_map/ppermute | solution.py:617
  372.9 19.3 %collective-permute-start.33 = (bf16[3,96,384]{2,1,0:T(8,128)(2,1)S(1)}, bf16[3,96,384]{2,1,0:T(8,128)(2,1)S(1)}, u32[]{:S(2)}, u32[]{:S(2)}) collective-permute-start(bf16[3,96,384]{2,1,0:T(8,128)(2,1)S(1)} %get-tuple-element.350), channel_id=1, source_target_pairs={{0,16},{2,18},{4,20},{6,22},{8,24},{10,26},{12,28},{14,30},{16,0},... | collective-permute-start | bytes 663560 | tf_op jit(solution)/shard_map/ppermute | solution.py:617
  373.5 18.7 %collective-permute-start.34 = (bf16[3,96,384]{2,1,0:T(8,128)(2,1)S(1)}, bf16[3,96,384]{2,1,0:T(8,128)(2,1)S(1)}, u32[]{:S(2)}, u32[]{:S(2)}) collective-permute-start(bf16[3,96,384]{2,1,0:T(8,128)(2,1)S(1)} %get-tuple-element.351), channel_id=1, source_target_pairs={{0,8},{2,10},{4,12},{6,14},{8,16},{10,18},{12,20},{14,22},{16,24},... | collective-permute-start | bytes 663560 | tf_op jit(solution)/shard_map/ppermute | solution.py:617
  392.2 17.8 %collective-permute-start.35 = (bf16[2,1,4,16,1536]{4,3,2,1,0:T(8,128)(2,1)}, bf16[2,1,4,16,1536]{4,3,2,1,0:T(8,128)(2,1)S(1)}, u32[]{:S(2)}, u32[]{:S(2)}) collective-permute-start(bf16[2,1,4,16,1536]{4,3,2,1,0:T(8,128)(2,1)} %get-tuple-element.362), channel_id=1, source_target_pairs={{0,2},{2,0},{4,6},{6,4},{8,10},{10,8},{12,14},{14,12},{16,18},{18,... | collective-permute-start | bytes 1179656 | tf_op jit(solution)/shard_map/ppermute | solution.py:621
  393.8 16.5 %collective-permute-start.36 = (bf16[2,1,4,16,1536]{4,3,2,1,0:T(8,128)(2,1)}, bf16[2,1,4,16,1536]{4,3,2,1,0:T(8,128)(2,1)S(1)}, u32[]{:S(2)}, u32[]{:S(2)}) collective-permute-start(bf16[2,1,4,16,1536]{4,3,2,1,0:T(8,128)(2,1)} %get-tuple-element.363), channel_id=1, source_target_pairs={{0,4},{2,6},{4,0},{6,2},{8,12},{10,14},{12,8},{14,10},{16,20},{18,... | collective-permute-start | bytes 1179656 | tf_op jit(solution)/shard_map/ppermute | solution.py:621
  394.4 24.7 %collective-permute-start.37 = (bf16[2,1,4,16,1536]{4,3,2,1,0:T(8,128)(2,1)}, bf16[2,1,4,16,1536]{4,3,2,1,0:T(8,128)(2,1)S(1)}, u32[]{:S(2)}, u32[]{:S(2)}) collective-permute-start(bf16[2,1,4,16,1536]{4,3,2,1,0:T(8,128)(2,1)} %get-tuple-element.364), channel_id=1, source_target_pairs={{0,2},{2,0},{4,6},{6,4},{8,10},{10,8},{12,14},{14,12},{16,18},{18,... | collective-permute-start | bytes 1179656 | tf_op jit(solution)/shard_map/ppermute | solution.py:621
  395.7 23.7 %collective-permute-start.38 = (bf16[2,1,4,16,1536]{4,3,2,1,0:T(8,128)(2,1)}, bf16[2,1,4,16,1536]{4,3,2,1,0:T(8,128)(2,1)S(1)}, u32[]{:S(2)}, u32[]{:S(2)}) collective-permute-start(bf16[2,1,4,16,1536]{4,3,2,1,0:T(8,128)(2,1)} %get-tuple-element.365), channel_id=1, source_target_pairs={{0,4},{2,6},{4,0},{6,2},{8,12},{10,14},{12,8},{14,10},{16,20},{18,... | collective-permute-start | bytes 1179656 | tf_op jit(solution)/shard_map/ppermute | solution.py:621
  421.1 14.5 %collective-permute-start.39 = (bf16[3,192,1024]{2,1,0:T(8,128)(2,1)S(1)}, bf16[3,192,1024]{2,1,0:T(8,128)(2,1)S(1)}, u32[]{:S(2)}, u32[]{:S(2)}) collective-permute-start(bf16[3,192,1024]{2,1,0:T(8,128)(2,1)S(1)} %copy-done.24), channel_id=1, source_target_pairs={{0,1},{1,0},{2,3},{3,2},{4,5},{5,4},{6,7},{7,6},{8,9},{9,8},{10,11... | collective-permute-start | bytes 3538952 | tf_op jit(solution)/shard_map/ppermute | solution.py:734
  421.1 12.6 %collective-permute-start.40 = (bf16[2,1,4,16,1536]{4,3,2,1,0:T(8,128)(2,1)}, bf16[2,1,4,16,1536]{4,3,2,1,0:T(8,128)(2,1)}, u32[]{:S(2)}, u32[]{:S(2)}) collective-permute-start(bf16[2,1,4,16,1536]{4,3,2,1,0:T(8,128)(2,1)} %add_convert_fusion.3), channel_id=1, source_target_pairs={{0,2},{2,0},{4,6},{6,4},{8,10},{10,8},{12,14},{14,12},{16,18},{18,... | collective-permute-start | bytes 1179656 | tf_op jit(solution)/shard_map/ppermute | solution.py:621
  422.1 13.4 %collective-permute-start.41 = (bf16[2,1,4,16,1536]{4,3,2,1,0:T(8,128)(2,1)}, bf16[2,1,4,16,1536]{4,3,2,1,0:T(8,128)(2,1)}, u32[]{:S(2)}, u32[]{:S(2)}) collective-permute-start(bf16[2,1,4,16,1536]{4,3,2,1,0:T(8,128)(2,1)} %add_convert_fusion.2), channel_id=1, source_target_pairs={{0,4},{2,6},{4,0},{6,2},{8,12},{10,14},{12,8},{14,10},{16,20},{18,... | collective-permute-start | bytes 1179656 | tf_op jit(solution)/shard_map/ppermute | solution.py:621
  439.5 19.2 %collective-permute-start.42 = (bf16[2,1,96,768]{3,2,1,0:T(8,128)(2,1)}, bf16[2,1,96,768]{3,2,1,0:T(8,128)(2,1)S(1)}, u32[]{:S(2)}, u32[]{:S(2)}) collective-permute-start(bf16[2,1,96,768]{3,2,1,0:T(8,128)(2,1)} %get-tuple-element.394), channel_id=1, source_target_pairs={{0,2},{2,0},{4,6},{6,4},{8,10},{10,8},{12,14},{14,12},{16,18},{18,... | collective-permute-start | bytes 884744 | tf_op jit(solution)/shard_map/ppermute | solution.py:621
  440.0 18.6 %collective-permute-start.43 = (bf16[2,1,96,768]{3,2,1,0:T(8,128)(2,1)}, bf16[2,1,96,768]{3,2,1,0:T(8,128)(2,1)S(1)}, u32[]{:S(2)}, u32[]{:S(2)}) collective-permute-start(bf16[2,1,96,768]{3,2,1,0:T(8,128)(2,1)} %get-tuple-element.395), channel_id=1, source_target_pairs={{0,4},{2,6},{4,0},{6,2},{8,12},{10,14},{12,8},{14,10},{16,20},{18,... | collective-permute-start | bytes 884744 | tf_op jit(solution)/shard_map/ppermute | solution.py:621
  441.6 17.1 %collective-permute-start.44 = (bf16[2,1,96,768]{3,2,1,0:T(8,128)(2,1)}, bf16[2,1,96,768]{3,2,1,0:T(8,128)(2,1)S(1)}, u32[]{:S(2)}, u32[]{:S(2)}) collective-permute-start(bf16[2,1,96,768]{3,2,1,0:T(8,128)(2,1)} %get-tuple-element.396), channel_id=1, source_target_pairs={{0,2},{2,0},{4,6},{6,4},{8,10},{10,8},{12,14},{14,12},{16,18},{18,... | collective-permute-start | bytes 884744 | tf_op jit(solution)/shard_map/ppermute | solution.py:621
  443.2 15.5 %collective-permute-start.45 = (bf16[2,1,96,768]{3,2,1,0:T(8,128)(2,1)}, bf16[2,1,96,768]{3,2,1,0:T(8,128)(2,1)S(1)}, u32[]{:S(2)}, u32[]{:S(2)}) collective-permute-start(bf16[2,1,96,768]{3,2,1,0:T(8,128)(2,1)} %get-tuple-element.397), channel_id=1, source_target_pairs={{0,4},{2,6},{4,0},{6,2},{8,12},{10,14},{12,8},{14,10},{16,20},{18,... | collective-permute-start | bytes 884744 | tf_op jit(solution)/shard_map/ppermute | solution.py:621
  462.1 23.2 %collective-permute-start.46 = (bf16[1536,1024]{1,0:T(8,128)(2,1)}, bf16[1536,1024]{1,0:T(8,128)(2,1)}, u32[]{:S(2)}, u32[]{:S(2)}) collective-permute-start(bf16[1536,1024]{1,0:T(8,128)(2,1)} %get-tuple-element.427.own_ref), channel_id=1, source_target_pairs={{0,1},{1,0},{2,3},{3,2},{4,5},{5,4},{6,7},{7,6},{8,9},{9,8},{10,11... | collective-permute-start | bytes 9437192 | tf_op jit(solution)/shard_map/ppermute | solution.py:734
  464.2 8.4 %collective-permute-start.47 = (bf16[1,4,16,1536]{3,2,1,0:T(8,128)(2,1)}, bf16[1,4,16,1536]{3,2,1,0:T(8,128)(2,1)}, u32[]{:S(2)}, u32[]{:S(2)}) collective-permute-start(bf16[1,4,16,1536]{3,2,1,0:T(8,128)(2,1)} %get-tuple-element.412), channel_id=1, source_target_pairs={{0,24},{2,26},{4,28},{6,30},{8,0},{10,2},{12,4},{14,6},{16,8},{18,... | collective-permute-start | bytes 589832 | tf_op jit(solution)/shard_map/ppermute | solution.py:617
  465.4 19.8 %collective-permute-start.48 = (bf16[1,4,16,1536]{3,2,1,0:T(8,128)(2,1)}, bf16[1,4,16,1536]{3,2,1,0:T(8,128)(2,1)}, u32[]{:S(2)}, u32[]{:S(2)}) collective-permute-start(bf16[1,4,16,1536]{3,2,1,0:T(8,128)(2,1)} %get-tuple-element.413), channel_id=1, source_target_pairs={{0,16},{2,18},{4,20},{6,22},{8,24},{10,26},{12,28},{14,30},{16,0},... | collective-permute-start | bytes 589832 | tf_op jit(solution)/shard_map/ppermute | solution.py:617
  466.9 18.4 %collective-permute-start.50 = (bf16[2,1,96,768]{3,2,1,0:T(8,128)(2,1)}, bf16[2,1,96,768]{3,2,1,0:T(8,128)(2,1)S(1)}, u32[]{:S(2)}, u32[]{:S(2)}) collective-permute-start(bf16[2,1,96,768]{3,2,1,0:T(8,128)(2,1)} %add_convert_fusion.5), channel_id=1, source_target_pairs={{0,2},{2,0},{4,6},{6,4},{8,10},{10,8},{12,14},{14,12},{16,18},{18,... | collective-permute-start | bytes 884744 | tf_op jit(solution)/shard_map/ppermute | solution.py:621
  467.3 18.0 %collective-permute-start.51 = (bf16[2,1,96,768]{3,2,1,0:T(8,128)(2,1)}, bf16[2,1,96,768]{3,2,1,0:T(8,128)(2,1)S(1)}, u32[]{:S(2)}, u32[]{:S(2)}) collective-permute-start(bf16[2,1,96,768]{3,2,1,0:T(8,128)(2,1)} %add_convert_fusion.4), channel_id=1, source_target_pairs={{0,4},{2,6},{4,0},{6,2},{8,12},{10,14},{12,8},{14,10},{16,20},{18,... | collective-permute-start | bytes 884744 | tf_op jit(solution)/shard_map/ppermute | solution.py:621
  472.6 12.7 %collective-permute-start.49 = (bf16[1,4,16,1536]{3,2,1,0:T(8,128)(2,1)S(1)}, bf16[1,4,16,1536]{3,2,1,0:T(8,128)(2,1)S(1)}, u32[]{:S(2)}, u32[]{:S(2)}) collective-permute-start(bf16[1,4,16,1536]{3,2,1,0:T(8,128)(2,1)S(1)} %copy-done.65), channel_id=1, source_target_pairs={{0,8},{2,10},{4,12},{6,14},{8,16},{10,18},{12,20},{14,22},{16,24},... | collective-permute-start | bytes 589832 | tf_op jit(solution)/shard_map/ppermute | solution.py:617
  485.6 13.6 %collective-permute-start.52 = (bf16[1,96,768]{2,1,0:T(8,128)(2,1)S(1)}, bf16[1,96,768]{2,1,0:T(8,128)(2,1)S(1)}, u32[]{:S(2)}, u32[]{:S(2)}) collective-permute-start(bf16[1,96,768]{2,1,0:T(8,128)(2,1)S(1)} %get-tuple-element.431), channel_id=1, source_target_pairs={{0,24},{2,26},{4,28},{6,30},{8,0},{10,2},{12,4},{14,6},{16,8},{18,... | collective-permute-start | bytes 442376 | tf_op jit(solution)/shard_map/ppermute | solution.py:617
  486.0 21.3 %collective-permute-start.53 = (bf16[1,96,768]{2,1,0:T(8,128)(2,1)S(1)}, bf16[1,96,768]{2,1,0:T(8,128)(2,1)S(1)}, u32[]{:S(2)}, u32[]{:S(2)}) collective-permute-start(bf16[1,96,768]{2,1,0:T(8,128)(2,1)S(1)} %get-tuple-element.432), channel_id=1, source_target_pairs={{0,16},{2,18},{4,20},{6,22},{8,24},{10,26},{12,28},{14,30},{16,0},... | collective-permute-start | bytes 442376 | tf_op jit(solution)/shard_map/ppermute | solution.py:617
  487.0 20.3 %collective-permute-start.54 = (bf16[1,96,768]{2,1,0:T(8,128)(2,1)S(1)}, bf16[1,96,768]{2,1,0:T(8,128)(2,1)S(1)}, u32[]{:S(2)}, u32[]{:S(2)}) collective-permute-start(bf16[1,96,768]{2,1,0:T(8,128)(2,1)S(1)} %get-tuple-element.433), channel_id=1, source_target_pairs={{0,8},{2,10},{4,12},{6,14},{8,16},{10,18},{12,20},{14,22},{16,24},... | collective-permute-start | bytes 442376 | tf_op jit(solution)/shard_map/ppermute | solution.py:617
  526.6 3.8 collective-permute-start.56
  526.9 3.8 collective-permute-start.57
  528.4 4.7 collective-permute-start.58
  533.1 6.0 %collective-permute-start.59 = (f32[44,128]{1,0:T(8,128)S(1)}, f32[44,128]{1,0:T(8,128)S(1)}, u32[]{:S(2)}, u32[]{:S(2)}) collective-permute-start(f32[44,128]{1,0:T(8,128)S(1)} %add_add_fusion.1), channel_id=1, source_target_pairs={{0,16},{2,18},{4,20},{6,22},{8,24},{10,26},{12,28},{14,30},{16,0},... | collective-permute-start | bytes 67592 | tf_op jit(solution)/shard_map/ppermute | solution.py:617
  535.3 5.6 collective-permute-start.60
  537.4 3.8 collective-permute-start.61
  (84 other events, 960.7 us)
Sparse Core Ops, SparseCore 0:
  11.4 192.6 all-gather.6
  207.5 73.7 all-gather.4
  287.0 232.4 reduce-scatter.1

commit v4 on v3

--- a/solution.py
+++ b/solution.py
@@ -85,7 +85,7 @@
 def cross_fwd_kernel(q_ref, k_ref, v_ref, keep_ref, o_ref, lse_ref):
     for block in range(LEN // QB):
         cols = slice(block * QB, (block + 1) * QB)
-        scores = dot_tn(k_ref[...], q_ref[:, cols]) + keep_ref[...]
+        scores = jnp.where(keep_ref[...] > 0.0, dot_tn(k_ref[...], q_ref[:, cols]), NEG_FILL)
         softmax_store(scores, v_ref[...], o_ref, lse_ref, cols)
 
 
@@ -141,7 +141,7 @@
     dv_acc[...] = jnp.zeros_like(dv_acc)
     for block in range(LEN // QB):
         cols = slice(block * QB, (block + 1) * QB)
-        scores = dot_tn(k_ref[...], q_ref[:, cols]) + keep_ref[...]
+        scores = jnp.where(keep_ref[...] > 0.0, dot_tn(k_ref[...], q_ref[:, cols]), NEG_FILL)
         grads, grad_q, grad_k, grad_v = score_grads(
             scores, lse_ref[0, :, cols], k_ref[...], v_ref[...], q_ref[:, cols], do_ref[:, cols]
         )
@@ -816,7 +816,7 @@
     mem_parts = core_pair(mem_own, mem_index)
     mem_full = jnp.concatenate(mem_parts, axis=1)
     kept_parts = core_pair(kept_mask.reshape(enc), mem_index)
-    keep = jnp.where(jnp.concatenate(kept_parts) > 0, 0.0, NEG_FILL).astype(F32).reshape(LEN, 1)
+    keep = (jnp.concatenate(kept_parts) > 0).astype(F32).reshape(LEN, 1)
     seg_row = segment_ids.reshape(1, LEN)
     seg_col = segment_ids.reshape(LEN, 1)
     bucket_hot = (bucket_ids[None, :] == jnp.arange(NB, dtype=jnp.int32)[:, None]).astype(F32)
@@ -934,21 +934,19 @@
     layer_out = layer_output(resid_two, out_low, out_other, block, pad).T
     rel_grad = jnp.dot(diag.reshape(heads, -1), diag_hot, precision=lax.Precision.HIGHEST)
     layer_out, rel_grad = tick((layer_out, rel_grad), self_g, cross_g)
-    ffn_sum = jnp.concatenate([t.finish() for t in ffn_g], axis=2)
+    ffn_sums = [t.finish() for t in ffn_g]
     cross_sum = cross_g.finish()[0, :, :share]
     self_sum = self_g.finish()[0, :block]
 
     self_grads = self_sum.reshape(block, 4, own).transpose(1, 2, 0)
-    ffn_grads = ffn_sum[:, :block].transpose(0, 2, 1)
+    ffn_grads = jnp.concatenate(ffn_sums, axis=2)[:, :block].transpose(0, 2, 1)
     cross_grads = narrow(cross_sum, 2)
     local_squares = (
         jnp.sum(jnp.square(self_sum), keepdims=True)
-        + jnp.sum(jnp.square(ffn_sum), keepdims=True)[0]
+        + sum(jnp.sum(jnp.square(part), keepdims=True)[0] for part in ffn_sums[::-1])
         + jnp.sum(jnp.square(cross_sum), keepdims=True)[0]
     )
-    self_grads, ffn_grads, cross_grads, local_squares = lax.optimization_barrier(
-        (self_grads, ffn_grads, cross_grads, local_squares)
-    )
+    self_grads, cross_grads, local_squares = lax.optimization_barrier((self_grads, cross_grads, local_squares))
     gain_lines = 3 * rows // 128
     gain_grad = jnp.where(mem_index == 0, jnp.concatenate([gain_one, gain_two, gain_three], axis=1).T, 0.0)
     rel_padded = lax.dynamic_update_slice_in_dim(

time: 572 us -> 574 us (level)
  transfers between devices with their start and end apart: 65 -> 65, of which waited for: 32 -> 33; matrix products, arithmetic and copies ran while one was open for 15% -> 16% of each run, Pallas kernels for 40% -> 40%
where the time goes in v4:
time: 574 us; the launch traced here: 566 us
  Pallas kernels  224 us (39%)
  waiting for transfers between devices  134 us (23%)
  starting transfers between devices  68.6 us (12%)
  other arithmetic  65.5 us (11%)
  local copies, waits for them, and re-layouts  28.3 us (5%)
  matrix products  24 us (4%)
  between operations  21.1 us (4%)
    pallas_call x2, Pallas kernels, feed_forward(): pl.pallas_call(functools.partial(ffn_kernel, len(sizes), first, last), in...  79.8 us
    ppermute x33, waiting for transfers between devices, flipped(): return lax.ppermute(value, 'tok', [(t, t ^ bits) for t in range(16)])  72.5 us
    pallas_call x4, Pallas kernels, attn_call(): pl.pallas_call(kernel, grid=(heads,), in_specs=in_specs, out_specs=out_sp...  48.9 us
    ppermute x33, starting transfers between devices, flipped(): return lax.ppermute(value, 'tok', [(t, t ^ bits) for t in range(16)])  37.1 us
    pallas_call x3, Pallas kernels, norm_back(): pl.pallas_call(functools.partial(norm_back_kernel, upstream, squeeze, len...  35.1 us
    ppermute x18, waiting for transfers between devices, rotated(): lax.ppermute(value, 'tok', [(t, (t // 4 + step) % 4 * 4 + t % 4) for t in...  32.7 us
    ppermute x18, starting transfers between devices, rotated(): lax.ppermute(value, 'tok', [(t, (t // 4 + step) % 4 * 4 + t % 4) for t in...  29.5 us
    dot_general x3, matrix products, dot_tn(): lax.dot_general(a, b, (((0,), (0,)), ((), ())), preferred_element_type=F32)  12 us
  transfers between devices with their start and end apart: 65, of which 33 were waited for; matrix products, arithmetic and copies ran while one was open for 16% of the time, Pallas kernels for 40%

profile of v4, /device:TPU:0, one launch (start us, length us, event | category | flops | bytes accessed | tf_op | source)
XLA Modules:
  0.0 566.0 jit_solution(8066136406660726518)
XLA Ops:
  11.7 3.1 collective-permute-start
  14.8 2.6 collective-permute-start.1
  18.7 2.4 shard_map.350
  26.2 4.4 shard_map.348.refs_0_
  30.6 4.6 shard_map.349.refs_2_.refs_3_
  37.7 2.9 collective-permute-start.7
  40.6 3.0 collective-permute-start.8
  47.8 4.0 collective-permute-done.7
  53.2 7.2 %collective-permute-done.8 = bf16[1,4,16,1536]{3,2,1,0:T(8,128)(2,1)} collective-permute-done((bf16[1,4,16,1536]{3,2,1,0:T(8,128)(2,1)}, bf16[1,4,16,1536]{3,2,1,0:T(8,128)(2,1)}, u32[]{:S(2)}, u32[]{:S(2)}) %collective-permute-start.8) | collective-permute-done | bytes 196640 | tf_op jit(solution)/shard_map/ppermute | solution.py:617
  63.8 12.2 %collective-permute-done.5.refs_4_ = bf16[2,1,96,768]{3,2,1,0:T(8,128)(2,1)S(1)} collective-permute-done((bf16[2,1,96,768]{3,2,1,0:T(8,128)(2,1)S(1)}, bf16[2,1,96,768]{3,2,1,0:T(8,128)(2,1)S(1)}, u32[]{:S(2)}, u32[]{:S(2)}) %collective-permute-start.5) | collective-permute-done | bytes 294944 | tf_op jit(solution)/shard_map/ppermute | solution.py:621
  76.0 11.0 %collective-permute-done.6.refs_5_ = bf16[2,1,96,768]{3,2,1,0:T(8,128)(2,1)S(1)} collective-permute-done((bf16[2,1,96,768]{3,2,1,0:T(8,128)(2,1)}, bf16[2,1,96,768]{3,2,1,0:T(8,128)(2,1)S(1)}, u32[]{:S(2)}, u32[]{:S(2)}) %collective-permute-start.6) | collective-permute-done | bytes 294944 | tf_op jit(solution)/shard_map/ppermute | solution.py:621
  94.7 2.0 pad_maximum_fusion.mem_ref
  98.3 3.9 shard_map.351
  112.7 3.0 fusion.8.q_ref.k_ref.v_ref
  115.8 2.0 collective-permute-done.15.refs_2_
  117.8 16.4 %collective-permute-done.16.refs_3_ = bf16[2,1,4,16,1536]{4,3,2,1,0:T(8,128)(2,1)} collective-permute-done((bf16[2,1,4,16,1536]{4,3,2,1,0:T(8,128)(2,1)S(1)}, bf16[2,1,4,16,1536]{4,3,2,1,0:T(8,128)(2,1)}, u32[]{:S(2)}, u32[]{:S(2)}) %collective-permute-start.16) | collective-permute-done | bytes 393248 | tf_op jit(solution)/shard_map/ppermute | solution.py:621
  134.2 4.1 collective-permute-done.18.refs_5_
  138.8 2.6 collective-permute-start.20
  145.0 8.0 %shard_map.352 = (bf16[192,1024]{1,0:T(8,128)(2,1)}, f32[3,1,1024]{2,1,0:T(1,128)}) custom-call(bf16[576,1024]{1,0:T(8,128)(2,1)} %fusion.8.q_ref.k_ref.v_ref, bf16[576,1024]{1,0:T(8,128)(2,1)} %fusion.8.q_ref.k_ref.v_ref, bf16[576,1024]{1,0:T(8,128)(2,1)} %fusion.8.q_ref.k_ref.v_ref, s32[1,1024]{1,0:T(1,128)} %bitcast.190, s32[1024,1]{1,0:T(8,128)} %copy.66.segc_ref, ...), custom_call_target="tpu_custom_call" | custom-call | flops 805306368 | bytes 4194304 | tf_op jit(solution)/shard_map/pallas_call | solution.py:164
  153.1 4.4 collective-permute-done.19.refs_6_
  158.7 4.5 shard_map.353
  165.5 2.7 broadcast_select_fusion.1
  172.8 2.0 copy-done.1
  174.8 8.2 %shard_map.354.refs_4_.key_map.value_map = bf16[4,384,1536]{2,1,0:T(8,128)(2,1)} custom-call(bf16[384,256]{1,0:T(8,128)(2,1)} %get-tuple-element.510.own_map, bf16[384,256]{1,0:T(8,128)(2,1)} %get-tuple-element.509.other_map, bf16[16,4,16,1536]{3,2,1,0:T(8,128)(2,1)} %bitcast.162, bf16[16,4,16,1536]{3,2,1,0:T(8,128)(2,1)} %collective-permute-done.22.other_ref), custom_call_target="tpu_custom_call" | custom-call | flops 2415919104 | bytes 12582912 | tf_op jit(solution)/shard_map/pallas_call | solution.py:427
  182.9 2.8 convolution_convert_fusion.3.q_ref
  187.1 2.3 convolution_convert_fusion.k_ref.v_ref
  189.4 12.4 %shard_map.355 = (bf16[192,1024]{1,0:T(8,128)(2,1)}, f32[3,1,1024]{2,1,0:T(1,128)}) custom-call(bf16[192,1024]{1,0:T(8,128)(2,1)} %convolution_convert_fusion.3.q_ref, bf16[384,1024]{1,0:T(8,128)(2,1)} %convolution_convert_fusion.k_ref.v_ref, bf16[384,1024]{1,0:T(8,128)(2,1)} %convolution_convert_fusion.k_ref.v_ref, f32[1024,1]{1,0:T(8,128)} %convert_element_type.672.keep_ref), custom_call_target="tpu_custom_call" | custom-call | flops 805306368 | bytes 4194304 | tf_op jit(solution)/shard_map/pallas_call | solution.py:164
  205.0 5.2 multiply_reduce_fusion
  210.3 2.6 copy-done
  212.8 2.3 multiply_convert_fusion.refs_1_
  215.1 57.4 %shard_map.356 = (f32[1536,1024]{1,0:T(8,128)}, f32[1536,1024]{1,0:T(8,128)}, bf16[16,3,96,1408]{3,2,1,0:T(8,128)(2,1)}) custom-call(s32[16]{0:T(128)} %stack.102.owners_ref.refs_0_, bf16[1536,1024]{1,0:T(8,128)(2,1)} %multiply_convert_fusion.refs_1_, bf16[1536,1024]{1,0:T(8,128)(2,1)} %shard_map.349.refs_2_.refs_3_, bf16[16,3,96,1408]{3,2,1,0:T(8,128)(2,1)} %bitcast.194), custom_call_target="tpu_custom_call" | custom-call | flops 39862665216 | bytes 33554432 | tf_op jit(solution)/shard_map/pallas_call | solution.py:345
  272.6 9.7 %all-gather.5.cloned.1.call-done = bf16[48,96,384]{2,1,0:T(8,128)(2,1)} async-done(((bf16[3,96,384]{2,1,0:T(8,128)(2,1)}), bf16[48,96,384]{2,1,0:T(8,128)(2,1)}) %all-gather.5.cloned.1.call-update) | async-done | bytes 3538960 | tf_op jit(solution)/shard_map/all_gather | solution.py:804
  282.3 22.3 %shard_map.357 = (bf16[1536,1024]{1,0:T(8,128)(2,1)}, bf16[1536,1024]{1,0:T(8,128)(2,1)}, bf16[2,3,96,384]{3,2,1,0:T(8,128)(2,1)}, bf16[2,3,96,384]{3,2,1,0:T(8,...) custom-call(s32[16]{0:T(128)} %stack.102.owners_ref.refs_0_, ...), custom_call_target="tpu_custom_call" | custom-call | flops 10871635968 | bytes 33554432 | tf_op jit(solution)/shard_map/pallas_call | solution.py:345
  304.8 5.9 %collective-permute-done.24.refs_5_ = bf16[1536,1024]{1,0:T(8,128)(2,1)S(1)} collective-permute-done((bf16[1536,1024]{1,0:T(8,128)(2,1)}, bf16[1536,1024]{1,0:T(8,128)(2,1)S(1)}, u32[]{:S(2)}, u32[]{:S(2)}) %collective-permute-start.24) | collective-permute-done | bytes 3145760 | tf_op jit(solution)/shard_map/ppermute | solution.py:734
  313.8 10.9 %shard_map.358 = (bf16[1536,1024]{1,0:T(8,128)(2,1)}, f32[1536,1]{1,0:T(8,128)}) custom-call(f32[1536,1024]{1,0:T(8,128)} %copy-done, f32[1,1024]{1,0:T(1,128)} %bitcast.184, f32[1536,1]{1,0:T(8,128)} %copy.67.refs_2_, bf16[1536,1024]{1,0:T(8,128)(2,1)} %shard_map.349.refs_2_.refs_3_, bf16[1536,1024]{1,0:T(8,128)(2,1)} %get-tuple-element.317.refs_4_, ...), custom_call_target="tpu_custom_call" | custom-call | flops 18874368 | bytes 31457280 | tf_op jit(solution)/shard_map/pallas_call | solution.py:604
  324.8 3.5 collective-permute-done.25
  332.8 3.7 convolution_convert_fusion.2.do_ref
  336.5 14.8 %shard_map.359.own_ref = bf16[3,192,1024]{2,1,0:T(8,128)(2,1)} custom-call(bf16[192,1024]{1,0:T(8,128)(2,1)} %convolution_convert_fusion.3.q_ref, bf16[384,1024]{1,0:T(8,128)(2,1)} %convolution_convert_fusion.k_ref.v_ref, bf16[384,1024]{1,0:T(8,128)(2,1)} %convolution_convert_fusion.k_ref.v_ref, bf16[192,1024]{1,0:T(8,128)(2,1)} %convolution_convert_fusion.2.do_ref, ...), custom_call_target="tpu_custom_call" | custom-call | flops 2013265920 | bytes 4194304 | tf_op jit(solution)/shard_map/pallas_call | solution.py:164
  359.5 10.6 %shard_map.360 = (bf16[1536,1024]{1,0:T(8,128)(2,1)}, f32[1536,1]{1,0:T(8,128)}) custom-call(f32[1536,1024]{1,0:T(8,128)} %copy-done.1, f32[1,1024]{1,0:T(1,128)} %bitcast.183, f32[1536,1]{1,0:T(8,128)} %copy.68.refs_2_, bf16[1536,1024]{1,0:T(8,128)(2,1)} %get-tuple-element.325.refs_3_.g_ref, bf16[4,384,1536]{2,1,0:T(8,128)(2,1)} %shard_map.354.refs_4_.key_map.value_map, ...), custom_call_target="tpu_custom_call" | custom-call | flops 1226833920 | bytes 31457280 | tf_op jit(solution)/shard_map/pallas_call | solution.py:604
  371.5 2.5 collective-permute-start.32
  375.7 3.8 convolution_convert_fusion.1.do_ref
  379.5 11.4 %shard_map.361 = (bf16[2,1,4,16,1536]{4,3,2,1,0:T(8,128)(2,1)}, bf16[2,1,4,16,1536]{4,3,2,1,0:T(8,128)(2,1)}, bf16[2,1,4,16,1536]{4,3,2,1,0:T(8,128)(2,1)}, bf16...) custom-call(s32[16]{0:T(128)} %stack.102.owners_ref.refs_0_, ...), custom_call_target="tpu_custom_call" | custom-call | flops 3221225472 | bytes 16777216 | tf_op jit(solution)/shard_map/pallas_call | solution.py:458
  390.9 2.4 collective-permute-done.33
  397.5 13.7 %shard_map.362 = (bf16[3,192,1024]{2,1,0:T(8,128)(2,1)}, f32[3,3,512]{2,1,0:T(4,128)}) custom-call(bf16[576,1024]{1,0:T(8,128)(2,1)} %fusion.8.q_ref.k_ref.v_ref, bf16[576,1024]{1,0:T(8,128)(2,1)} %fusion.8.q_ref.k_ref.v_ref, bf16[576,1024]{1,0:T(8,128)(2,1)} %fusion.8.q_ref.k_ref.v_ref, bf16[192,1024]{1,0:T(8,128)(2,1)} %convolution_convert_fusion.1.do_ref, ...), custom_call_target="tpu_custom_call" | custom-call | flops 2013265920 | bytes 4194304 | tf_op jit(solution)/shard_map/pallas_call | solution.py:164
  411.2 9.4 %collective-permute-done.37 = bf16[2,1,4,16,1536]{4,3,2,1,0:T(8,128)(2,1)S(1)} collective-permute-done((bf16[2,1,4,16,1536]{4,3,2,1,0:T(8,128)(2,1)}, bf16[2,1,4,16,1536]{4,3,2,1,0:T(8,128)(2,1)S(1)}, u32[]{:S(2)}, u32[]{:S(2)}) %collective-permute-start.37) | collective-permute-done | bytes 393248 | tf_op jit(solution)/shard_map/ppermute | solution.py:621
  425.7 8.3 %shard_map.363 = (bf16[2,1,96,768]{3,2,1,0:T(8,128)(2,1)}, bf16[2,1,96,768]{3,2,1,0:T(8,128)(2,1)}, bf16[2,1,96,768]{3,2,1,0:T(8,128)(2,1)}, bf16[2,1,96,768]{3,...) custom-call(s32[16]{0:T(128)} %stack.102.owners_ref.refs_0_, ...), custom_call_target="tpu_custom_call" | custom-call | flops 2415919104 | bytes 12582912 | tf_op jit(solution)/shard_map/pallas_call | solution.py:489
  438.2 1.9 fusion.38
  442.0 2.0 collective-permute-start.44
  445.7 13.7 %shard_map.364 = (f32[1472,1024]{1,0:T(8,128)}, f32[1536,1]{1,0:T(8,128)}) custom-call(bf16[1536,1024]{1,0:T(8,128)(2,1)} %shard_map.348.refs_0_, f32[1,1024]{1,0:T(1,128)} %bitcast.185, f32[1536,1]{1,0:T(8,128)} %copy.70.refs_2_, bf16[1536,1024]{1,0:T(8,128)(2,1)} %get-tuple-element.347.g_ref.refs_3_, bf16[1536,768]{1,0:T(8,128)(2,1)} %copy-done.5, ...), custom_call_target="tpu_custom_call" | custom-call | flops 3642753024 | bytes 31457280 | tf_op jit(solution)/shard_map/pallas_call | solution.py:604
  463.4 2.3 multiply_reduce_fusion.3
  465.6 2.4 collective-permute-start.47
  470.7 3.3 collective-permute-done.47
  476.1 5.3 shard_map.365
  481.4 5.8 %collective-permute-done.48 = bf16[1,4,16,1536]{3,2,1,0:T(8,128)(2,1)} collective-permute-done((bf16[1,4,16,1536]{3,2,1,0:T(8,128)(2,1)}, bf16[1,4,16,1536]{3,2,1,0:T(8,128)(2,1)}, u32[]{:S(2)}, u32[]{:S(2)}) %collective-permute-start.48) | collective-permute-done | bytes 196640 | tf_op jit(solution)/shard_map/ppermute | solution.py:617
  489.0 1.9 collective-permute-start.54
  493.4 7.4 %shard_map.366 = bf16[1472,1024]{1,0:T(8,128)(2,1)} custom-call(f32[1536,1024]{1,0:T(8,128)} %copy-done, bf16[1536,1024]{1,0:T(8,128)(2,1)} %get-tuple-element.426.own_ref, bf16[1536,1024]{1,0:T(8,128)(2,1)} %collective-permute-done.46.other_ref), custom_call_target="tpu_custom_call" | custom-call | flops 6291456 | bytes 15728640 | tf_op jit(solution)/shard_map/pallas_call | solution.py:536
  501.3 8.6 %collective-permute-done.53 = bf16[1,96,768]{2,1,0:T(8,128)(2,1)S(1)} collective-permute-done((bf16[1,96,768]{2,1,0:T(8,128)(2,1)S(1)}, bf16[1,96,768]{2,1,0:T(8,128)(2,1)S(1)}, u32[]{:S(2)}, u32[]{:S(2)}) %collective-permute-start.53) | collective-permute-done | bytes 147488 | tf_op jit(solution)/shard_map/ppermute | solution.py:617
  511.0 9.1 %reduce-scatter.2.cloned.1.call-done = bf16[1,3,96,1408]{3,2,1,0:T(8,128)(2,1)} async-done(((bf16[16,3,96,1408]{3,2,1,0:T(8,128)(2,1)}), bf16[1,3,96,1408]{3,2,1,0:T(8,128)(2,1)}) %reduce-scatter.2.cloned.1.call-update) | async-done | bytes 811024 | tf_op jit(solution)/shard_map/reduce_scatter | solution.py:688
  520.2 2.2 multiply_reduce_fusion.2
  531.5 2.5 collective-permute-done.58
  535.7 2.6 collective-permute-start.60
  546.7 2.5 multiply_subtract_fusion.2
  549.3 2.7 multiply_subtract_fusion.1
  552.6 5.4 multiply_subtract_fusion
  (373 shorter events, 124.3 us)
Async XLA Ops:
  7.2 207.9 %all-gather.7.cloned.1.call-start = ((), (), s32[]{:S(2)}) async-start(), calls=%async_computation.3 | async-start | bytes 13787136 | tf_op jit(solution)/shard_map/all_gather | solution.py:804
  11.0 271.4 %all-gather.5.cloned.1.call-start = ((), (), s32[]{:S(2)}) async-start(), calls=%async_computation.2 | async-start | bytes 3760128 | tf_op jit(solution)/shard_map/all_gather | solution.py:804
  11.7 23.5 %collective-permute-start = (bf16[1,96,768]{2,1,0:T(8,128)(2,1)S(1)}, bf16[1,96,768]{2,1,0:T(8,128)(2,1)S(1)}, u32[]{:S(2)}, u32[]{:S(2)}) collective-permute-start(bf16[1,96,768]{2,1,0:T(8,128)(2,1)S(1)} %bitcast.177), channel_id=1, source_target_pairs={{0,8},{2,10},{4,12},{6,14},{8,16},{10,18},{12,20},{14,22},{16,24},... | collective-permute-start | bytes 442376 | tf_op jit(solution)/shard_map/ppermute | solution.py:617
  14.8 20.5 %collective-permute-start.1 = (bf16[1,96,768]{2,1,0:T(8,128)(2,1)S(1)}, bf16[1,96,768]{2,1,0:T(8,128)(2,1)}, u32[]{:S(2)}, u32[]{:S(2)}) collective-permute-start(bf16[1,96,768]{2,1,0:T(8,128)(2,1)S(1)} %bitcast.178), channel_id=1, source_target_pairs={{0,16},{2,18},{4,20},{6,22},{8,24},{10,26},{12,28},{14,30},{16,0},... | collective-permute-start | bytes 442376 | tf_op jit(solution)/shard_map/ppermute | solution.py:617
  17.3 17.9 %collective-permute-start.2 = (bf16[1,96,768]{2,1,0:T(8,128)(2,1)S(1)}, bf16[1,96,768]{2,1,0:T(8,128)(2,1)}, u32[]{:S(2)}, u32[]{:S(2)}) collective-permute-start(bf16[1,96,768]{2,1,0:T(8,128)(2,1)S(1)} %bitcast.179), channel_id=1, source_target_pairs={{0,24},{2,26},{4,28},{6,30},{8,0},{10,2},{12,4},{14,6},{16,8},{18,... | collective-permute-start | bytes 442376 | tf_op jit(solution)/shard_map/ppermute | solution.py:617
  21.1 72.0 %collective-permute-start.10 = (bf16[1536,512]{1,0:T(8,128)(2,1)}, bf16[1536,512]{1,0:T(8,128)(2,1)}, u32[]{:S(2)}, u32[]{:S(2)}) collective-permute-start(bf16[1536,512]{1,0:T(8,128)(2,1)} %shard_map.350), channel_id=1, source_target_pairs={{0,1},{1,0},{2,3},{3,2},{4,5},{5,4},{6,7},{7,6},{8,9},{9,8},{10,11... | collective-permute-start | bytes 4718600 | tf_op jit(solution)/shard_map/ppermute | solution.py:734
  21.1 22.5 %collective-permute-start.11 = (s32[512]{0:T(512)S(1)}, s32[512]{0:T(512)S(1)}, u32[]{:S(2)}, u32[]{:S(2)}) collective-permute-start(s32[512]{0:T(512)S(1)} %bitcast.192), channel_id=1, source_target_pairs={{0,1},{1,0},{2,3},{3,2},{4,5},{5,4},{6,7},{7,6},{8,9},{9,8},{10,11... | collective-permute-start | bytes 6152 | tf_op jit(solution)/shard_map/ppermute | solution.py:734
  37.7 14.1 %collective-permute-start.7 = (bf16[1,4,16,1536]{3,2,1,0:T(8,128)(2,1)}, bf16[1,4,16,1536]{3,2,1,0:T(8,128)(2,1)}, u32[]{:S(2)}, u32[]{:S(2)}) collective-permute-start(bf16[1,4,16,1536]{3,2,1,0:T(8,128)(2,1)} %get-tuple-element.263), channel_id=1, source_target_pairs={{0,8},{2,10},{4,12},{6,14},{8,16},{10,18},{12,20},{14,22},{16,24},... | collective-permute-start | bytes 589832 | tf_op jit(solution)/shard_map/ppermute | solution.py:617
  40.6 19.8 %collective-permute-start.8 = (bf16[1,4,16,1536]{3,2,1,0:T(8,128)(2,1)}, bf16[1,4,16,1536]{3,2,1,0:T(8,128)(2,1)}, u32[]{:S(2)}, u32[]{:S(2)}) collective-permute-start(bf16[1,4,16,1536]{3,2,1,0:T(8,128)(2,1)} %get-tuple-element.263), channel_id=1, source_target_pairs={{0,16},{2,18},{4,20},{6,22},{8,24},{10,26},{12,28},{14,30},{16,0},... | collective-permute-start | bytes 589832 | tf_op jit(solution)/shard_map/ppermute | solution.py:617
  43.5 18.4 %collective-permute-start.9 = (bf16[1,4,16,1536]{3,2,1,0:T(8,128)(2,1)}, bf16[1,4,16,1536]{3,2,1,0:T(8,128)(2,1)}, u32[]{:S(2)}, u32[]{:S(2)}) collective-permute-start(bf16[1,4,16,1536]{3,2,1,0:T(8,128)(2,1)} %get-tuple-element.263), channel_id=1, source_target_pairs={{0,24},{2,26},{4,28},{6,30},{8,0},{10,2},{12,4},{14,6},{16,8},{18,... | collective-permute-start | bytes 589832 | tf_op jit(solution)/shard_map/ppermute | solution.py:617
  46.3 17.5 %collective-permute-start.3 = (bf16[2,1,96,768]{3,2,1,0:T(8,128)(2,1)S(1)}, bf16[2,1,96,768]{3,2,1,0:T(8,128)(2,1)S(1)}, u32[]{:S(2)}, u32[]{:S(2)}) collective-permute-start(bf16[2,1,96,768]{3,2,1,0:T(8,128)(2,1)S(1)} %get-tuple-element.259.refs_0_), channel_id=1, source_target_pairs={{0,2},{2,0},{4,6},{6,4},{8,10},{10,8},{12,14},{14,12},{16,18},{18,... | collective-permute-start | bytes 884744 | tf_op jit(solution)/shard_map/ppermute | solution.py:621
  51.8 12.0 %collective-permute-start.4 = (bf16[2,1,96,768]{3,2,1,0:T(8,128)(2,1)}, bf16[2,1,96,768]{3,2,1,0:T(8,128)(2,1)S(1)}, u32[]{:S(2)}, u32[]{:S(2)}) collective-permute-start(bf16[2,1,96,768]{3,2,1,0:T(8,128)(2,1)} %get-tuple-element.260.refs_1_), channel_id=1, source_target_pairs={{0,2},{2,0},{4,6},{6,4},{8,10},{10,8},{12,14},{14,12},{16,18},{18,... | collective-permute-start | bytes 884744 | tf_op jit(solution)/shard_map/ppermute | solution.py:621
  60.4 15.5 %collective-permute-start.5 = (bf16[2,1,96,768]{3,2,1,0:T(8,128)(2,1)S(1)}, bf16[2,1,96,768]{3,2,1,0:T(8,128)(2,1)S(1)}, u32[]{:S(2)}, u32[]{:S(2)}) collective-permute-start(bf16[2,1,96,768]{3,2,1,0:T(8,128)(2,1)S(1)} %get-tuple-element.259.refs_0_), channel_id=1, source_target_pairs={{0,4},{2,6},{4,0},{6,2},{8,12},{10,14},{12,8},{14,10},{16,20},{18,... | collective-permute-start | bytes 884744 | tf_op jit(solution)/shard_map/ppermute | solution.py:621
  61.9 25.0 %collective-permute-start.6 = (bf16[2,1,96,768]{3,2,1,0:T(8,128)(2,1)}, bf16[2,1,96,768]{3,2,1,0:T(8,128)(2,1)S(1)}, u32[]{:S(2)}, u32[]{:S(2)}) collective-permute-start(bf16[2,1,96,768]{3,2,1,0:T(8,128)(2,1)} %get-tuple-element.260.refs_1_), channel_id=1, source_target_pairs={{0,4},{2,6},{4,0},{6,2},{8,12},{10,14},{12,8},{14,10},{16,20},{18,... | collective-permute-start | bytes 884744 | tf_op jit(solution)/shard_map/ppermute | solution.py:621
  90.0 6.8 %collective-permute-start.12 = (bf16[2,1,96,768]{3,2,1,0:T(8,128)(2,1)S(1)}, bf16[2,1,96,768]{3,2,1,0:T(8,128)(2,1)S(1)}, u32[]{:S(2)}, u32[]{:S(2)}) collective-permute-start(bf16[2,1,96,768]{3,2,1,0:T(8,128)(2,1)S(1)} %collective-permute-done.5.refs_4_), channel_id=1, source_target_pairs={{0,2},{2,0},{4,6},{6,4},{8,10},{10,8},{12,14},{14,12},{16,18},{18,... | collective-permute-start | bytes 884744 | tf_op jit(solution)/shard_map/ppermute | solution.py:621
  91.5 6.8 %collective-permute-start.13 = (bf16[2,1,96,768]{3,2,1,0:T(8,128)(2,1)S(1)}, bf16[2,1,96,768]{3,2,1,0:T(8,128)(2,1)}, u32[]{:S(2)}, u32[]{:S(2)}) collective-permute-start(bf16[2,1,96,768]{3,2,1,0:T(8,128)(2,1)S(1)} %collective-permute-done.4.refs_3_), channel_id=1, source_target_pairs={{0,4},{2,6},{4,0},{6,2},{8,12},{10,14},{12,8},{14,10},{16,20},{18,... | collective-permute-start | bytes 884744 | tf_op jit(solution)/shard_map/ppermute | solution.py:621
  102.3 63.2 %collective-permute-start.14 = (bf16[1536,768]{1,0:T(8,128)(2,1)}, bf16[1536,768]{1,0:T(8,128)(2,1)}, u32[]{:S(2)}, u32[]{:S(2)}) collective-permute-start(bf16[1536,768]{1,0:T(8,128)(2,1)} %bitcast.163), channel_id=1, source_target_pairs={{0,1},{1,0},{2,3},{3,2},{4,5},{5,4},{6,7},{7,6},{8,9},{9,8},{10,11... | collective-permute-start | bytes 7077896 | tf_op jit(solution)/shard_map/ppermute | solution.py:734
  102.3 15.4 %collective-permute-start.15 = (bf16[2,1,4,16,1536]{4,3,2,1,0:T(8,128)(2,1)}, bf16[2,1,4,16,1536]{4,3,2,1,0:T(8,128)(2,1)}, u32[]{:S(2)}, u32[]{:S(2)}) collective-permute-start(bf16[2,1,4,16,1536]{4,3,2,1,0:T(8,128)(2,1)} %pad_maximum_fusion.4.refs_0_), channel_id=1, source_target_pairs={{0,2},{2,0},{4,6},{6,4},{8,10},{10,8},{12,14},{14,12},{16,18},{18,... | collective-permute-start | bytes 1179656 | tf_op jit(solution)/shard_map/ppermute | solution.py:621
  103.5 30.6 %collective-permute-start.16 = (bf16[2,1,4,16,1536]{4,3,2,1,0:T(8,128)(2,1)S(1)}, bf16[2,1,4,16,1536]{4,3,2,1,0:T(8,128)(2,1)}, u32[]{:S(2)}, u32[]{:S(2)}) collective-permute-start(bf16[2,1,4,16,1536]{4,3,2,1,0:T(8,128)(2,1)S(1)} %pad_maximum_fusion.5.refs_1_), channel_id=1, source_target_pairs={{0,2},{2,0},{4,6},{6,4},{8,10},{10,8},{12,14},{14,12},{16,18},{18,... | collective-permute-start | bytes 1179656 | tf_op jit(solution)/shard_map/ppermute | solution.py:621
  104.4 29.7 %collective-permute-start.17 = (bf16[2,1,4,16,1536]{4,3,2,1,0:T(8,128)(2,1)}, bf16[2,1,4,16,1536]{4,3,2,1,0:T(8,128)(2,1)}, u32[]{:S(2)}, u32[]{:S(2)}) collective-permute-start(bf16[2,1,4,16,1536]{4,3,2,1,0:T(8,128)(2,1)} %pad_maximum_fusion.4.refs_0_), channel_id=1, source_target_pairs={{0,4},{2,6},{4,0},{6,2},{8,12},{10,14},{12,8},{14,10},{16,20},{18,... | collective-permute-start | bytes 1179656 | tf_op jit(solution)/shard_map/ppermute | solution.py:621
  106.2 32.1 %collective-permute-start.18 = (bf16[2,1,4,16,1536]{4,3,2,1,0:T(8,128)(2,1)S(1)}, bf16[2,1,4,16,1536]{4,3,2,1,0:T(8,128)(2,1)}, u32[]{:S(2)}, u32[]{:S(2)}) collective-permute-start(bf16[2,1,4,16,1536]{4,3,2,1,0:T(8,128)(2,1)S(1)} %pad_maximum_fusion.5.refs_1_), channel_id=1, source_target_pairs={{0,4},{2,6},{4,0},{6,2},{8,12},{10,14},{12,8},{14,10},{16,20},{18,... | collective-permute-start | bytes 1179656 | tf_op jit(solution)/shard_map/ppermute | solution.py:621
  138.3 19.2 %collective-permute-start.19 = (bf16[2,1,4,16,1536]{4,3,2,1,0:T(8,128)(2,1)}, bf16[2,1,4,16,1536]{4,3,2,1,0:T(8,128)(2,1)S(1)}, u32[]{:S(2)}, u32[]{:S(2)}) collective-permute-start(bf16[2,1,4,16,1536]{4,3,2,1,0:T(8,128)(2,1)} %collective-permute-done.17.refs_4_), channel_id=1, source_target_pairs={{0,2},{2,0},{4,6},{6,4},{8,10},{10,8},{12,14},{14,12},{16,18},{18,... | collective-permute-start | bytes 1179656 | tf_op jit(solution)/shard_map/ppermute | solution.py:621
  138.8 19.9 %collective-permute-start.20 = (bf16[2,1,4,16,1536]{4,3,2,1,0:T(8,128)(2,1)}, bf16[2,1,4,16,1536]{4,3,2,1,0:T(8,128)(2,1)}, u32[]{:S(2)}, u32[]{:S(2)}) collective-permute-start(bf16[2,1,4,16,1536]{4,3,2,1,0:T(8,128)(2,1)} %collective-permute-done.16.refs_3_), channel_id=1, source_target_pairs={{0,4},{2,6},{4,0},{6,2},{8,12},{10,14},{12,8},{14,10},{16,20},{18,... | collective-permute-start | bytes 1179656 | tf_op jit(solution)/shard_map/ppermute | solution.py:621
  143.1 377.1 %reduce-scatter.2.cloned.1.call-start = ((), (), s32[]{:S(2)}) async-start(), calls=%async_computation.1 | async-start | bytes 13787136 | tf_op jit(solution)/shard_map/reduce_scatter | solution.py:688
  163.2 11.5 %collective-permute-start.22 = (bf16[16,4,16,1536]{3,2,1,0:T(8,128)(2,1)}, bf16[16,4,16,1536]{3,2,1,0:T(8,128)(2,1)}, u32[]{:S(2)}, u32[]{:S(2)}) collective-permute-start(bf16[16,4,16,1536]{3,2,1,0:T(8,128)(2,1)} %bitcast.161), channel_id=1, source_target_pairs={{0,1},{1,0},{2,3},{3,2},{4,5},{5,4},{6,7},{7,6},{8,9},{9,8},{10,11... | collective-permute-start | bytes 9437192 | tf_op jit(solution)/shard_map/ppermute | solution.py:734
  165.0 4.5 collective-permute-start.21
  201.8 2.0 collective-permute-start.23
  304.7 5.9 %collective-permute-start.24 = (bf16[1536,1024]{1,0:T(8,128)(2,1)}, bf16[1536,1024]{1,0:T(8,128)(2,1)S(1)}, u32[]{:S(2)}, u32[]{:S(2)}) collective-permute-start(bf16[1536,1024]{1,0:T(8,128)(2,1)} %get-tuple-element.317.refs_4_), channel_id=1, source_target_pairs={{0,1},{1,0},{2,3},{3,2},{4,5},{5,4},{6,7},{7,6},{8,9},{9,8},{10,11... | collective-permute-start | bytes 9437192 | tf_op jit(solution)/shard_map/ppermute | solution.py:734
  310.6 17.6 %collective-permute-start.25 = (bf16[2,3,96,384]{3,2,1,0:T(8,128)(2,1)}, bf16[2,3,96,384]{3,2,1,0:T(8,128)(2,1)}, u32[]{:S(2)}, u32[]{:S(2)}) collective-permute-start(bf16[2,3,96,384]{3,2,1,0:T(8,128)(2,1)} %get-tuple-element.320), channel_id=1, source_target_pairs={{0,2},{2,0},{4,6},{6,4},{8,10},{10,8},{12,14},{14,12},{16,18},{18,... | collective-permute-start | bytes 1327112 | tf_op jit(solution)/shard_map/ppermute | solution.py:621
  312.1 16.8 %collective-permute-start.26 = (bf16[2,3,96,384]{3,2,1,0:T(8,128)(2,1)}, bf16[2,3,96,384]{3,2,1,0:T(8,128)(2,1)}, u32[]{:S(2)}, u32[]{:S(2)}) collective-permute-start(bf16[2,3,96,384]{3,2,1,0:T(8,128)(2,1)} %get-tuple-element.321), channel_id=1, source_target_pairs={{0,4},{2,6},{4,0},{6,2},{8,12},{10,14},{12,8},{14,10},{16,20},{18,... | collective-permute-start | bytes 1327112 | tf_op jit(solution)/shard_map/ppermute | solution.py:621
  328.9 24.3 %collective-permute-start.27 = (bf16[2,3,96,384]{3,2,1,0:T(8,128)(2,1)}, bf16[2,3,96,384]{3,2,1,0:T(8,128)(2,1)S(1)}, u32[]{:S(2)}, u32[]{:S(2)}) collective-permute-start(bf16[2,3,96,384]{3,2,1,0:T(8,128)(2,1)} %get-tuple-element.327), channel_id=1, source_target_pairs={{0,2},{2,0},{4,6},{6,4},{8,10},{10,8},{12,14},{14,12},{16,18},{18,... | collective-permute-start | bytes 1327112 | tf_op jit(solution)/shard_map/ppermute | solution.py:621
  330.0 23.2 %collective-permute-start.28 = (bf16[2,3,96,384]{3,2,1,0:T(8,128)(2,1)}, bf16[2,3,96,384]{3,2,1,0:T(8,128)(2,1)S(1)}, u32[]{:S(2)}, u32[]{:S(2)}) collective-permute-start(bf16[2,3,96,384]{3,2,1,0:T(8,128)(2,1)} %get-tuple-element.328), channel_id=1, source_target_pairs={{0,4},{2,6},{4,0},{6,2},{8,12},{10,14},{12,8},{14,10},{16,20},{18,... | collective-permute-start | bytes 1327112 | tf_op jit(solution)/shard_map/ppermute | solution.py:621
  353.2 4.0 collective-permute-start.29
  355.2 15.1 %collective-permute-start.30 = (bf16[2,3,96,384]{3,2,1,0:T(8,128)(2,1)}, bf16[2,3,96,384]{3,2,1,0:T(8,128)(2,1)S(1)}, u32[]{:S(2)}, u32[]{:S(2)}) collective-permute-start(bf16[2,3,96,384]{3,2,1,0:T(8,128)(2,1)} %add_convert_fusion.1), channel_id=1, source_target_pairs={{0,2},{2,0},{4,6},{6,4},{8,10},{10,8},{12,14},{14,12},{16,18},{18,... | collective-permute-start | bytes 1327112 | tf_op jit(solution)/shard_map/ppermute | solution.py:621
  356.2 14.1 %collective-permute-start.31 = (bf16[2,3,96,384]{3,2,1,0:T(8,128)(2,1)}, bf16[2,3,96,384]{3,2,1,0:T(8,128)(2,1)}, u32[]{:S(2)}, u32[]{:S(2)}) collective-permute-start(bf16[2,3,96,384]{3,2,1,0:T(8,128)(2,1)} %add_convert_fusion), channel_id=1, source_target_pairs={{0,4},{2,6},{4,0},{6,2},{8,12},{10,14},{12,8},{14,10},{16,20},{18,... | collective-permute-start | bytes 1327112 | tf_op jit(solution)/shard_map/ppermute | solution.py:621
  371.5 19.4 %collective-permute-start.32 = (bf16[3,96,384]{2,1,0:T(8,128)(2,1)S(1)}, bf16[3,96,384]{2,1,0:T(8,128)(2,1)S(1)}, u32[]{:S(2)}, u32[]{:S(2)}) collective-permute-start(bf16[3,96,384]{2,1,0:T(8,128)(2,1)S(1)} %fusion.31), channel_id=1, source_target_pairs={{0,24},{2,26},{4,28},{6,30},{8,0},{10,2},{12,4},{14,6},{16,8},{18,... | collective-permute-start | bytes 663560 | tf_op jit(solution)/shard_map/ppermute | solution.py:617
  374.1 19.2 %collective-permute-start.33 = (bf16[3,96,384]{2,1,0:T(8,128)(2,1)S(1)}, bf16[3,96,384]{2,1,0:T(8,128)(2,1)S(1)}, u32[]{:S(2)}, u32[]{:S(2)}) collective-permute-start(bf16[3,96,384]{2,1,0:T(8,128)(2,1)S(1)} %get-tuple-element.349), channel_id=1, source_target_pairs={{0,16},{2,18},{4,20},{6,22},{8,24},{10,26},{12,28},{14,30},{16,0},... | collective-permute-start | bytes 663560 | tf_op jit(solution)/shard_map/ppermute | solution.py:617
  374.6 18.7 %collective-permute-start.34 = (bf16[3,96,384]{2,1,0:T(8,128)(2,1)S(1)}, bf16[3,96,384]{2,1,0:T(8,128)(2,1)S(1)}, u32[]{:S(2)}, u32[]{:S(2)}) collective-permute-start(bf16[3,96,384]{2,1,0:T(8,128)(2,1)S(1)} %get-tuple-element.350), channel_id=1, source_target_pairs={{0,8},{2,10},{4,12},{6,14},{8,16},{10,18},{12,20},{14,22},{16,24},... | collective-permute-start | bytes 663560 | tf_op jit(solution)/shard_map/ppermute | solution.py:617
  393.3 17.8 %collective-permute-start.35 = (bf16[2,1,4,16,1536]{4,3,2,1,0:T(8,128)(2,1)}, bf16[2,1,4,16,1536]{4,3,2,1,0:T(8,128)(2,1)S(1)}, u32[]{:S(2)}, u32[]{:S(2)}) collective-permute-start(bf16[2,1,4,16,1536]{4,3,2,1,0:T(8,128)(2,1)} %get-tuple-element.361), channel_id=1, source_target_pairs={{0,2},{2,0},{4,6},{6,4},{8,10},{10,8},{12,14},{14,12},{16,18},{18,... | collective-permute-start | bytes 1179656 | tf_op jit(solution)/shard_map/ppermute | solution.py:621
  394.9 16.2 %collective-permute-start.36 = (bf16[2,1,4,16,1536]{4,3,2,1,0:T(8,128)(2,1)}, bf16[2,1,4,16,1536]{4,3,2,1,0:T(8,128)(2,1)S(1)}, u32[]{:S(2)}, u32[]{:S(2)}) collective-permute-start(bf16[2,1,4,16,1536]{4,3,2,1,0:T(8,128)(2,1)} %get-tuple-element.362), channel_id=1, source_target_pairs={{0,4},{2,6},{4,0},{6,2},{8,12},{10,14},{12,8},{14,10},{16,20},{18,... | collective-permute-start | bytes 1179656 | tf_op jit(solution)/shard_map/ppermute | solution.py:621
  395.4 25.2 %collective-permute-start.37 = (bf16[2,1,4,16,1536]{4,3,2,1,0:T(8,128)(2,1)}, bf16[2,1,4,16,1536]{4,3,2,1,0:T(8,128)(2,1)S(1)}, u32[]{:S(2)}, u32[]{:S(2)}) collective-permute-start(bf16[2,1,4,16,1536]{4,3,2,1,0:T(8,128)(2,1)} %get-tuple-element.363), channel_id=1, source_target_pairs={{0,2},{2,0},{4,6},{6,4},{8,10},{10,8},{12,14},{14,12},{16,18},{18,... | collective-permute-start | bytes 1179656 | tf_op jit(solution)/shard_map/ppermute | solution.py:621
  396.8 24.0 %collective-permute-start.38 = (bf16[2,1,4,16,1536]{4,3,2,1,0:T(8,128)(2,1)}, bf16[2,1,4,16,1536]{4,3,2,1,0:T(8,128)(2,1)S(1)}, u32[]{:S(2)}, u32[]{:S(2)}) collective-permute-start(bf16[2,1,4,16,1536]{4,3,2,1,0:T(8,128)(2,1)} %get-tuple-element.364), channel_id=1, source_target_pairs={{0,4},{2,6},{4,0},{6,2},{8,12},{10,14},{12,8},{14,10},{16,20},{18,... | collective-permute-start | bytes 1179656 | tf_op jit(solution)/shard_map/ppermute | solution.py:621
  422.5 13.8 %collective-permute-start.39 = (bf16[3,192,1024]{2,1,0:T(8,128)(2,1)S(1)}, bf16[3,192,1024]{2,1,0:T(8,128)(2,1)S(1)}, u32[]{:S(2)}, u32[]{:S(2)}) collective-permute-start(bf16[3,192,1024]{2,1,0:T(8,128)(2,1)S(1)} %copy-done.25), channel_id=1, source_target_pairs={{0,1},{1,0},{2,3},{3,2},{4,5},{5,4},{6,7},{7,6},{8,9},{9,8},{10,11... | collective-permute-start | bytes 3538952 | tf_op jit(solution)/shard_map/ppermute | solution.py:734
  422.5 11.8 %collective-permute-start.40 = (bf16[2,1,4,16,1536]{4,3,2,1,0:T(8,128)(2,1)}, bf16[2,1,4,16,1536]{4,3,2,1,0:T(8,128)(2,1)}, u32[]{:S(2)}, u32[]{:S(2)}) collective-permute-start(bf16[2,1,4,16,1536]{4,3,2,1,0:T(8,128)(2,1)} %add_convert_fusion.3), channel_id=1, source_target_pairs={{0,2},{2,0},{4,6},{6,4},{8,10},{10,8},{12,14},{14,12},{16,18},{18,... | collective-permute-start | bytes 1179656 | tf_op jit(solution)/shard_map/ppermute | solution.py:621
  423.5 12.8 %collective-permute-start.41 = (bf16[2,1,4,16,1536]{4,3,2,1,0:T(8,128)(2,1)}, bf16[2,1,4,16,1536]{4,3,2,1,0:T(8,128)(2,1)}, u32[]{:S(2)}, u32[]{:S(2)}) collective-permute-start(bf16[2,1,4,16,1536]{4,3,2,1,0:T(8,128)(2,1)} %add_convert_fusion.2), channel_id=1, source_target_pairs={{0,4},{2,6},{4,0},{6,2},{8,12},{10,14},{12,8},{14,10},{16,20},{18,... | collective-permute-start | bytes 1179656 | tf_op jit(solution)/shard_map/ppermute | solution.py:621
  440.1 19.3 %collective-permute-start.42 = (bf16[2,1,96,768]{3,2,1,0:T(8,128)(2,1)}, bf16[2,1,96,768]{3,2,1,0:T(8,128)(2,1)S(1)}, u32[]{:S(2)}, u32[]{:S(2)}) collective-permute-start(bf16[2,1,96,768]{3,2,1,0:T(8,128)(2,1)} %get-tuple-element.393), channel_id=1, source_target_pairs={{0,2},{2,0},{4,6},{6,4},{8,10},{10,8},{12,14},{14,12},{16,18},{18,... | collective-permute-start | bytes 884744 | tf_op jit(solution)/shard_map/ppermute | solution.py:621
  440.4 19.0 %collective-permute-start.43 = (bf16[2,1,96,768]{3,2,1,0:T(8,128)(2,1)}, bf16[2,1,96,768]{3,2,1,0:T(8,128)(2,1)S(1)}, u32[]{:S(2)}, u32[]{:S(2)}) collective-permute-start(bf16[2,1,96,768]{3,2,1,0:T(8,128)(2,1)} %get-tuple-element.394), channel_id=1, source_target_pairs={{0,4},{2,6},{4,0},{6,2},{8,12},{10,14},{12,8},{14,10},{16,20},{18,... | collective-permute-start | bytes 884744 | tf_op jit(solution)/shard_map/ppermute | solution.py:621
  442.0 17.5 %collective-permute-start.44 = (bf16[2,1,96,768]{3,2,1,0:T(8,128)(2,1)}, bf16[2,1,96,768]{3,2,1,0:T(8,128)(2,1)S(1)}, u32[]{:S(2)}, u32[]{:S(2)}) collective-permute-start(bf16[2,1,96,768]{3,2,1,0:T(8,128)(2,1)} %get-tuple-element.395), channel_id=1, source_target_pairs={{0,2},{2,0},{4,6},{6,4},{8,10},{10,8},{12,14},{14,12},{16,18},{18,... | collective-permute-start | bytes 884744 | tf_op jit(solution)/shard_map/ppermute | solution.py:621
  444.0 15.5 %collective-permute-start.45 = (bf16[2,1,96,768]{3,2,1,0:T(8,128)(2,1)}, bf16[2,1,96,768]{3,2,1,0:T(8,128)(2,1)S(1)}, u32[]{:S(2)}, u32[]{:S(2)}) collective-permute-start(bf16[2,1,96,768]{3,2,1,0:T(8,128)(2,1)} %get-tuple-element.396), channel_id=1, source_target_pairs={{0,4},{2,6},{4,0},{6,2},{8,12},{10,14},{12,8},{14,10},{16,20},{18,... | collective-permute-start | bytes 884744 | tf_op jit(solution)/shard_map/ppermute | solution.py:621
  462.8 24.4 %collective-permute-start.46 = (bf16[1536,1024]{1,0:T(8,128)(2,1)}, bf16[1536,1024]{1,0:T(8,128)(2,1)}, u32[]{:S(2)}, u32[]{:S(2)}) collective-permute-start(bf16[1536,1024]{1,0:T(8,128)(2,1)} %get-tuple-element.426.own_ref), channel_id=1, source_target_pairs={{0,1},{1,0},{2,3},{3,2},{4,5},{5,4},{6,7},{7,6},{8,9},{9,8},{10,11... | collective-permute-start | bytes 9437192 | tf_op jit(solution)/shard_map/ppermute | solution.py:734
  465.6 8.3 %collective-permute-start.47 = (bf16[1,4,16,1536]{3,2,1,0:T(8,128)(2,1)}, bf16[1,4,16,1536]{3,2,1,0:T(8,128)(2,1)}, u32[]{:S(2)}, u32[]{:S(2)}) collective-permute-start(bf16[1,4,16,1536]{3,2,1,0:T(8,128)(2,1)} %get-tuple-element.411), channel_id=1, source_target_pairs={{0,24},{2,26},{4,28},{6,30},{8,0},{10,2},{12,4},{14,6},{16,8},{18,... | collective-permute-start | bytes 589832 | tf_op jit(solution)/shard_map/ppermute | solution.py:617
  468.1 19.2 %collective-permute-start.48 = (bf16[1,4,16,1536]{3,2,1,0:T(8,128)(2,1)}, bf16[1,4,16,1536]{3,2,1,0:T(8,128)(2,1)}, u32[]{:S(2)}, u32[]{:S(2)}) collective-permute-start(bf16[1,4,16,1536]{3,2,1,0:T(8,128)(2,1)} %get-tuple-element.412), channel_id=1, source_target_pairs={{0,16},{2,18},{4,20},{6,22},{8,24},{10,26},{12,28},{14,30},{16,0},... | collective-permute-start | bytes 589832 | tf_op jit(solution)/shard_map/ppermute | solution.py:617
  468.3 18.9 %collective-permute-start.50 = (bf16[2,1,96,768]{3,2,1,0:T(8,128)(2,1)}, bf16[2,1,96,768]{3,2,1,0:T(8,128)(2,1)S(1)}, u32[]{:S(2)}, u32[]{:S(2)}) collective-permute-start(bf16[2,1,96,768]{3,2,1,0:T(8,128)(2,1)} %add_convert_fusion.5), channel_id=1, source_target_pairs={{0,2},{2,0},{4,6},{6,4},{8,10},{10,8},{12,14},{14,12},{16,18},{18,... | collective-permute-start | bytes 884744 | tf_op jit(solution)/shard_map/ppermute | solution.py:621
  469.8 17.4 %collective-permute-start.51 = (bf16[2,1,96,768]{3,2,1,0:T(8,128)(2,1)S(1)}, bf16[2,1,96,768]{3,2,1,0:T(8,128)(2,1)S(1)}, u32[]{:S(2)}, u32[]{:S(2)}) collective-permute-start(bf16[2,1,96,768]{3,2,1,0:T(8,128)(2,1)S(1)} %copy-done.50), channel_id=1, source_target_pairs={{0,4},{2,6},{4,0},{6,2},{8,12},{10,14},{12,8},{14,10},{16,20},{18,... | collective-permute-start | bytes 884744 | tf_op jit(solution)/shard_map/ppermute | solution.py:621
  474.0 13.2 %collective-permute-start.49 = (bf16[1,4,16,1536]{3,2,1,0:T(8,128)(2,1)S(1)}, bf16[1,4,16,1536]{3,2,1,0:T(8,128)(2,1)S(1)}, u32[]{:S(2)}, u32[]{:S(2)}) collective-permute-start(bf16[1,4,16,1536]{3,2,1,0:T(8,128)(2,1)S(1)} %copy-done.63), channel_id=1, source_target_pairs={{0,8},{2,10},{4,12},{6,14},{8,16},{10,18},{12,20},{14,22},{16,24},... | collective-permute-start | bytes 589832 | tf_op jit(solution)/shard_map/ppermute | solution.py:617
  487.5 13.7 %collective-permute-start.52 = (bf16[1,96,768]{2,1,0:T(8,128)(2,1)S(1)}, bf16[1,96,768]{2,1,0:T(8,128)(2,1)S(1)}, u32[]{:S(2)}, u32[]{:S(2)}) collective-permute-start(bf16[1,96,768]{2,1,0:T(8,128)(2,1)S(1)} %get-tuple-element.430), channel_id=1, source_target_pairs={{0,24},{2,26},{4,28},{6,30},{8,0},{10,2},{12,4},{14,6},{16,8},{18,... | collective-permute-start | bytes 442376 | tf_op jit(solution)/shard_map/ppermute | solution.py:617
  487.9 22.0 %collective-permute-start.53 = (bf16[1,96,768]{2,1,0:T(8,128)(2,1)S(1)}, bf16[1,96,768]{2,1,0:T(8,128)(2,1)S(1)}, u32[]{:S(2)}, u32[]{:S(2)}) collective-permute-start(bf16[1,96,768]{2,1,0:T(8,128)(2,1)S(1)} %get-tuple-element.431), channel_id=1, source_target_pairs={{0,16},{2,18},{4,20},{6,22},{8,24},{10,26},{12,28},{14,30},{16,0},... | collective-permute-start | bytes 442376 | tf_op jit(solution)/shard_map/ppermute | solution.py:617
  489.0 20.9 %collective-permute-start.54 = (bf16[1,96,768]{2,1,0:T(8,128)(2,1)S(1)}, bf16[1,96,768]{2,1,0:T(8,128)(2,1)S(1)}, u32[]{:S(2)}, u32[]{:S(2)}) collective-permute-start(bf16[1,96,768]{2,1,0:T(8,128)(2,1)S(1)} %get-tuple-element.432), channel_id=1, source_target_pairs={{0,8},{2,10},{4,12},{6,14},{8,16},{10,18},{12,20},{14,22},{16,24},... | collective-permute-start | bytes 442376 | tf_op jit(solution)/shard_map/ppermute | solution.py:617
  526.3 3.8 collective-permute-start.56
  527.7 3.8 collective-permute-start.57
  529.3 4.7 collective-permute-start.58
  534.0 6.8 %collective-permute-start.59 = (f32[44,128]{1,0:T(8,128)S(1)}, f32[44,128]{1,0:T(8,128)S(1)}, u32[]{:S(2)}, u32[]{:S(2)}) collective-permute-start(f32[44,128]{1,0:T(8,128)S(1)} %add_add_fusion.1), channel_id=1, source_target_pairs={{0,16},{2,18},{4,20},{6,22},{8,24},{10,26},{12,28},{14,30},{16,0},... | collective-permute-start | bytes 67592 | tf_op jit(solution)/shard_map/ppermute | solution.py:617
  535.7 5.6 collective-permute-start.60
  538.4 3.8 collective-permute-start.61
  (83 other events, 974.6 us)
Sparse Core Ops, SparseCore 0:
  11.4 191.6 all-gather.6
  206.5 75.7 all-gather.4
  288.1 232.0 reduce-scatter.1
